TPU v7x, 32 devices: a whole 2x2x4 slice. The times are simulated.
32 devices in a mesh: section: 2 (over core), fsdp: 16 (over z, y, x).
Axes of the slice: x: 2, y: 2, z: 4, core: 2. Of those that a mesh axis runs over, the one named last changes fastest.
Arguments:
- inputs: bfloat16 [2, 6144, 960], P(None, 'fsdp'), may hold values from -6 to 6
- cotangent: float32 [2, 6144, 960], P(None, 'fsdp'), may hold values from -6 to 6
- segments: int32 [2, 6144], P(None, 'fsdp'), may hold values from 0 to 2, as said below
- positions: int32 [2, 6144], P(None, 'fsdp'), may hold values from 0 to 2430, as said below
- norm_first: bfloat16 [2, 960], P('section', 'fsdp'), may hold values from 0.099609375 to 1.8984375
- w_query: bfloat16 [2, 960, 960], P('section', 'fsdp'), may hold values from -0.1875 to 0.1875
- w_key: bfloat16 [2, 960, 320], P('section', 'fsdp'), may hold values from -0.1875 to 0.1875
- w_value: bfloat16 [2, 960, 320], P('section', 'fsdp'), may hold values from -0.1875 to 0.1875
- w_out: bfloat16 [2, 960, 960], P('section', 'fsdp'), may hold values from -0.5 to 0.5
- norm_second: bfloat16 [2, 960], P('section', 'fsdp'), may hold values from 0.099609375 to 1.8984375
- w_gate: bfloat16 [2, 960, 2560], P('section', 'fsdp'), may hold values from -0.1875 to 0.1875
- w_up: bfloat16 [2, 960, 2560], P('section', 'fsdp'), may hold values from -0.1875 to 0.1875
- w_down: bfloat16 [2, 2560, 960], P('section', 'fsdp'), may hold values from -0.125 to 0.125
Outputs:
- activations: float32 [2, 2, 6144, 960], P('section', None, 'fsdp')
- input_grads: float32 [2, 2, 6144, 960], P('section', None, 'fsdp')
- grad_norm_first: float32 [2, 960], P('section', 'fsdp')
- grad_query: float32 [2, 960, 960], P('section', 'fsdp')
- grad_key: float32 [2, 960, 320], P('section', 'fsdp')
- grad_value: float32 [2, 960, 320], P('section', 'fsdp')
- grad_out: float32 [2, 960, 960], P('section', 'fsdp')
- grad_norm_second: float32 [2, 960], P('section', 'fsdp')
- grad_gate: float32 [2, 960, 2560], P('section', 'fsdp')
- grad_up: float32 [2, 960, 2560], P('section', 'fsdp')
- grad_down: float32 [2, 2560, 960], P('section', 'fsdp')
Inputs may be any that keep to these rules, and one draw needn't show every extreme that they name: `segments`: each sequence of 384 tokens holds exactly three documents, numbered 0, 1, 2 in order; a document is a run of equal numbers. Within a document positions rise by one from token to token from a start below 2048.
All inputs are finite; a program needn't handle non-finite values.
Results may differ from a plain program's by a relative error of at most 0.025.
Values may be sent and summed in bfloat16 or wider, within the bound.
No kernel may reach another device: no remote copies, remote signals or barrier semaphores. Data moves between devices by JAX's collectives and lax.ppermute only.
A program may use at most 320 MiB of HBM per device.

v0:
```python
import jax
import jax.numpy as jnp
from jax import lax
from jax.sharding import PartitionSpec as P

HEADS = 15
KV = 5
HD = 64


epsilon = 1e-05
rope_base = 100000.0


def as_sent(array):
    return jax.tree.map(lambda a: a.astype(jnp.bfloat16) if a.dtype == jnp.float32 else a, array)


def passed_along(block, axis, distance):
    devices = range(lax.axis_size(axis))
    route = [(i - distance, i) for i in devices if i - distance in devices]
    return lax.ppermute(block, axis, route)


def rms_norm(values, gain_row):
    return (
        values * lax.rsqrt(jnp.mean(values * values, axis=-1, keepdims=True) + epsilon) * gain_row
    )


def rotate(values, places):
    half_dim = values.shape[-1] // 2
    frequency = rope_base ** (-jnp.arange(half_dim, dtype=jnp.float32) / half_dim)
    angles = places.astype(jnp.float32)[:, None, None] * frequency
    cosine = jnp.cos(angles)
    sine_part = jnp.sin(angles)
    front_half = values[..., :half_dim]
    back_half = values[..., half_dim:]
    return jnp.concatenate(
        [front_half * cosine - back_half * sine_part, back_half * cosine + front_half * sine_part],
        axis=-1,
    )


def swiglu(gate_val, up_val):
    return jax.nn.silu(gate_val) * up_val


def plain_dot(left_side, right_side):
    return jnp.dot(left_side, right_side, preferred_element_type=jnp.float32)


def outer_sum(left_side, right_side):
    return lax.dot_general(
        left_side, right_side, (((0,), (0,)), ((), ())), preferred_element_type=jnp.float32
    )


def back_dot(left_side, right_side):
    return lax.dot_general(
        left_side, right_side, (((1,), (1,)), ((), ())), preferred_element_type=jnp.float32
    )


def layer_forward(states, weights, labels, places):
    gain_one, query_w, key_w, value_w, out_w, gain_two, gate_w, up_w, down_w = weights
    length = states.shape[0]
    group_size = HEADS // KV
    normed = rms_norm(states, gain_one.astype(jnp.float32)).astype(jnp.bfloat16)
    queries = (
        rotate(plain_dot(normed, query_w).reshape(length, HEADS, HD), places)
        .astype(jnp.bfloat16)
        .reshape(length, KV, group_size, HD)
    )
    key_rows = rotate(plain_dot(normed, key_w).reshape(length, KV, HD), places).astype(jnp.bfloat16)
    value_rows = plain_dot(normed, value_w).astype(jnp.bfloat16).reshape(length, KV, HD)
    scores = jnp.einsum(
        "qkgd,pkd->kgqp", queries, key_rows, preferred_element_type=jnp.float32
    ) * float(HD) ** (-0.5)
    token_order = jnp.arange(length)
    allowed = (labels[:, None] == labels[None, :]) & (token_order[:, None] >= token_order[None, :])
    scores = jnp.where(allowed, scores, -1e30)
    shifted = jnp.exp(scores - jnp.max(scores, axis=-1, keepdims=True))
    probs_all = shifted / jnp.sum(shifted, axis=-1, keepdims=True)
    probs_low = probs_all.astype(jnp.bfloat16)
    attended = (
        jnp.einsum("kgqp,pkd->qkgd", probs_low, value_rows, preferred_element_type=jnp.float32)
        .reshape(length, HEADS * HD)
        .astype(jnp.bfloat16)
    )
    middle = states + plain_dot(attended, out_w)
    second = rms_norm(middle, gain_two.astype(jnp.float32)).astype(jnp.bfloat16)
    gate_val = plain_dot(second, gate_w)
    up_val = plain_dot(second, up_w)
    hidden = swiglu(gate_val, up_val).astype(jnp.bfloat16)
    output = middle + plain_dot(hidden, down_w)
    return (
        output,
        (
            normed,
            queries,
            key_rows,
            value_rows,
            probs_all,
            probs_low,
            attended,
            middle,
            second,
            gate_val,
            up_val,
            hidden,
        ),
    )


def layer_backward(states, weights, labels, places, grad_output):
    gain_one, query_w, key_w, value_w, out_w, gain_two, gate_w, up_w, down_w = weights
    length = states.shape[0]
    group_size = HEADS // KV
    scale_value = float(HD) ** (-0.5)
    output, kept_values = layer_forward(states, weights, labels, places)
    (
        normed,
        queries,
        key_rows,
        value_rows,
        probs_all,
        probs_low,
        attended,
        middle,
        second,
        gate_val,
        up_val,
        hidden,
    ) = kept_values
    grad_low = grad_output.astype(jnp.bfloat16)
    grad_down_w = outer_sum(hidden, grad_low)
    grad_hidden = back_dot(grad_low, down_w)
    unused, swiglu_pull = jax.vjp(swiglu, gate_val, up_val)
    grad_gate_val, grad_up_val = swiglu_pull(grad_hidden)
    gate_low = grad_gate_val.astype(jnp.bfloat16)
    up_low = grad_up_val.astype(jnp.bfloat16)
    grad_gate_w = outer_sum(second, gate_low)
    grad_up_w = outer_sum(second, up_low)
    grad_second = back_dot(gate_low, gate_w) + back_dot(up_low, up_w)
    unused, second_pull = jax.vjp(rms_norm, middle, gain_two.astype(jnp.float32))
    grad_mid_norm, grad_gain_two = second_pull(grad_second)
    grad_middle = grad_output + grad_mid_norm
    middle_low = grad_middle.astype(jnp.bfloat16)
    grad_out_w = outer_sum(attended, middle_low)
    grad_att = back_dot(middle_low, out_w).astype(jnp.bfloat16).reshape(length, KV, group_size, HD)
    grad_probs = jnp.einsum(
        "qkgd,pkd->kgqp", grad_att, value_rows, preferred_element_type=jnp.float32
    )
    grad_values = (
        jnp.einsum("kgqp,qkgd->pkd", probs_low, grad_att, preferred_element_type=jnp.float32)
        .reshape(length, KV * HD)
        .astype(jnp.bfloat16)
    )
    grad_scores = probs_all * (grad_probs - jnp.sum(probs_all * grad_probs, axis=-1, keepdims=True))
    scores_low = grad_scores.astype(jnp.bfloat16)
    grad_query_rot = (
        jnp.einsum("kgqp,pkd->qkgd", scores_low, key_rows, preferred_element_type=jnp.float32)
        * scale_value
    )
    grad_key_rot = (
        jnp.einsum("kgqp,qkgd->pkd", scores_low, queries, preferred_element_type=jnp.float32)
        * scale_value
    )
    unused, query_pull = jax.vjp(
        lambda moved_rows: rotate(moved_rows, places), jnp.zeros((length, HEADS, HD), jnp.float32)
    )
    grad_query_rows = (
        query_pull(grad_query_rot.reshape(length, HEADS, HD))[0]
        .reshape(length, HEADS * HD)
        .astype(jnp.bfloat16)
    )
    unused, key_pull = jax.vjp(
        lambda moved_rows: rotate(moved_rows, places), jnp.zeros((length, KV, HD), jnp.float32)
    )
    grad_key_rows = key_pull(grad_key_rot)[0].reshape(length, KV * HD).astype(jnp.bfloat16)
    grad_query_w = outer_sum(normed, grad_query_rows)
    grad_key_w = outer_sum(normed, grad_key_rows)
    grad_value_w = outer_sum(normed, grad_values)
    grad_normed = (
        back_dot(grad_query_rows, query_w)
        + back_dot(grad_key_rows, key_w)
        + back_dot(grad_values, value_w)
    )
    unused, first_pull = jax.vjp(rms_norm, states, gain_one.astype(jnp.float32))
    grad_state_norm, grad_gain_one = first_pull(grad_normed)
    return (
        grad_middle + grad_state_norm,
        (
            grad_gain_one,
            grad_query_w,
            grad_key_w,
            grad_value_w,
            grad_out_w,
            grad_gain_two,
            grad_gate_w,
            grad_up_w,
            grad_down_w,
        ),
    )


def on_device(
    inputs,
    cotangent,
    segments,
    positions,
    norm_first,
    w_query,
    w_key,
    w_value,
    w_out,
    norm_second,
    w_gate,
    w_up,
    w_down,
):
    on_first = lax.axis_index("section") == 0
    micro_count = inputs.shape[0]
    owned_shards = tuple(
        (
            weight[0]
            for weight in (
                norm_first,
                w_query,
                w_key,
                w_value,
                w_out,
                norm_second,
                w_gate,
                w_up,
                w_down,
            )
        )
    )

    def fetch_weights():
        return jax.tree.map(
            lambda part, own: part.astype(own.dtype),
            lax.all_gather(as_sent(owned_shards), "fsdp", axis=0, tiled=True),
            owned_shards,
        )

    starts = inputs.astype(jnp.float32)
    received = jnp.zeros(starts.shape[1:], jnp.float32)
    entries = []
    exits = []
    for tick_num in range(micro_count + 1):
        late_row = min(tick_num, micro_count - 1)
        early_row = max(tick_num - 1, 0)
        entry_rows = jnp.where(on_first, starts[late_row], received)
        labels = jnp.where(on_first, segments[late_row], segments[early_row])
        places = jnp.where(on_first, positions[late_row], positions[early_row])
        result, unused = layer_forward(entry_rows, fetch_weights(), labels, places)
        entries.append(entry_rows)
        exits.append(result)
        if tick_num < micro_count:
            received = passed_along(result.astype(jnp.bfloat16), "section", 1).astype(result.dtype)
    slot_inputs = [
        jnp.where(on_first, entries[slot_num], entries[slot_num + 1])
        for slot_num in range(micro_count)
    ]
    activations = jnp.stack(
        [
            jnp.where(on_first, exits[slot_num], exits[slot_num + 1])
            for slot_num in range(micro_count)
        ]
    )[None]
    returned = jnp.zeros_like(received)
    input_list = []
    summed = None
    for tick_num in range(micro_count + 1):
        late_row = min(tick_num, micro_count - 1)
        early_row = max(tick_num - 1, 0)
        states = jnp.where(on_first, slot_inputs[early_row], slot_inputs[late_row])
        labels = jnp.where(on_first, segments[early_row], segments[late_row])
        places = jnp.where(on_first, positions[early_row], positions[late_row])
        active = jnp.where(on_first, tick_num >= 1, tick_num < micro_count)
        grad_output = jnp.where(active, jnp.where(on_first, returned, cotangent[late_row]), 0.0)
        grad_input, grad_weights = layer_backward(
            states, fetch_weights(), labels, places, grad_output
        )
        input_list.append(grad_input)
        shares = (
            lax.psum_scatter(grad_weights[0], "fsdp", scatter_dimension=0, tiled=True),
            lax.psum_scatter(grad_weights[1], "fsdp", scatter_dimension=0, tiled=True),
            lax.psum_scatter(grad_weights[2], "fsdp", scatter_dimension=0, tiled=True),
            lax.psum_scatter(grad_weights[3], "fsdp", scatter_dimension=0, tiled=True),
            lax.psum_scatter(grad_weights[4], "fsdp", scatter_dimension=0, tiled=True),
            lax.psum_scatter(grad_weights[5], "fsdp", scatter_dimension=0, tiled=True),
            lax.psum_scatter(grad_weights[6], "fsdp", scatter_dimension=0, tiled=True),
            lax.psum_scatter(grad_weights[7], "fsdp", scatter_dimension=0, tiled=True),
            lax.psum_scatter(grad_weights[8], "fsdp", scatter_dimension=0, tiled=True),
        )
        if summed is None:
            summed = shares
        else:
            summed = tuple((before_sum + added for before_sum, added in zip(summed, shares)))
        if tick_num < micro_count:
            returned = passed_along(grad_input.astype(jnp.bfloat16), "section", -1).astype(
                grad_input.dtype
            )
    input_grads = jnp.stack(
        [
            jnp.where(on_first, input_list[slot_num + 1], input_list[slot_num])
            for slot_num in range(micro_count)
        ]
    )[None]
    return (activations, input_grads) + tuple((share_part[None] for share_part in summed))


def solution(mesh):
    placed = (
        P(None, "fsdp", None),
        P(None, "fsdp", None),
        P(None, "fsdp"),
        P(None, "fsdp"),
        P("section", "fsdp"),
        P("section", "fsdp", None),
        P("section", "fsdp", None),
        P("section", "fsdp", None),
        P("section", "fsdp", None),
        P("section", "fsdp"),
        P("section", "fsdp", None),
        P("section", "fsdp", None),
        P("section", "fsdp", None),
    )
    return jax.shard_map(
        on_device,
        mesh=mesh,
        in_specs=placed,
        out_specs=(
            P("section", None, "fsdp", None),
            P("section", None, "fsdp", None),
            P("section", "fsdp"),
            P("section", "fsdp", None),
            P("section", "fsdp", None),
            P("section", "fsdp", None),
            P("section", "fsdp", None),
            P("section", "fsdp"),
            P("section", "fsdp", None),
            P("section", "fsdp", None),
            P("section", "fsdp", None),
        ),
        check_vma=False,
    )
```

profile of v0, /device:TPU:0, one launch (start us, length us, event | category | flops | bytes accessed | tf_op | source)
XLA Modules:
  0.0 1880.0 jit_solution(5583282138825687219)
XLA Ops:
  19.0 43.9 %all-reduce.29 = (bf16[960]{0:T(1024)(128)(2,1)S(1)}, bf16[960]{0:T(1024)(128)(2,1)S(1)}) all-reduce(bf16[960]{0:T(1024)(128)(2,1)S(1)} %dynamic-update-slice, bf16[960]{0:T(1024)(128)(2,1)S(1)} %dynamic-update-slice.1), channel_id=2, replica_groups=mesh['section'=2,'fsdp'=16] {'fsdp'}, use_global_device_ids=true, to_apply=%add.12 | all-reduce | flops 1920 | bytes 7680
  63.0 55.9 %all-gather.2 = bf16[1,960,320]{2,0,1:T(2,128)(2,1)S(1)} all-gather(bf16[1,60,320]{2,0,1:T(2,128)(2,1)S(1)} %copy.78), channel_id=4, replica_groups=mesh['section'=2,'fsdp'=16] {'fsdp'}, dimensions={1}, use_global_device_ids=true | all-gather | bytes 652800 | tf_op jit(solution)/shard_map/all_gather | solution.py:245
  121.4 56.1 %all-gather.1 = bf16[1,960,320]{2,0,1:T(2,128)(2,1)S(1)} all-gather(bf16[1,60,320]{2,0,1:T(2,128)(2,1)S(1)} %copy.76), channel_id=3, replica_groups=mesh['section'=2,'fsdp'=16] {'fsdp'}, dimensions={1}, use_global_device_ids=true | all-gather | bytes 652800 | tf_op jit(solution)/shard_map/all_gather | solution.py:245
  188.3 10.6 copy.143
  199.0 4.6 copy.140
  205.8 7.4 fusion.409
  213.2 4.6 fusion.240
  219.5 99.3 %all-gather.19.cloned.1.call-done = bf16[1,960,2560]{2,0,1:T(2,128)(2,1)} async-done(((bf16[1,60,2560]{2,0,1:T(2,128)(2,1)}), bf16[1,960,2560]{2,0,1:T(2,128)(2,1)}) %all-gather.19.cloned.1.call-update) | async-done | bytes 4915216 | tf_op jit(solution)/shard_map/all_gather | solution.py:245
  318.8 7.2 copy.141
  326.0 120.2 %all-gather.21.cloned.1.call-done = bf16[1,960,2560]{2,0,1:T(2,128)(2,1)} async-done(((bf16[1,60,2560]{2,0,1:T(2,128)(2,1)}), bf16[1,960,2560]{2,0,1:T(2,128)(2,1)}) %all-gather.21.cloned.1.call-update) | async-done | bytes 4915216 | tf_op jit(solution)/shard_map/all_gather | solution.py:245
  446.3 7.5 copy.142
  458.0 74.2 %all-gather.23.cloned.1.call-done = bf16[1,2560,960]{2,1,0:T(8,128)(2,1)} async-done(((bf16[1,160,960]{2,1,0:T(8,128)(2,1)}), bf16[1,2560,960]{2,1,0:T(8,128)(2,1)}) %all-gather.23.cloned.1.call-update) | async-done | bytes 4915216 | tf_op jit(solution)/shard_map/all_gather | solution.py:245
  532.2 12.2 fusion.410
  560.3 7.6 fusion.413
  567.9 4.6 fusion.239
  579.2 12.7 fusion.215
  597.3 6.7 fusion.31
  621.9 8.1 fusion.416
  630.1 4.7 fusion.232
  639.9 7.5 fusion.415
  647.4 4.7 fusion.229
  656.2 8.3 fusion.414
  675.8 5.1 fusion.116
  690.3 4.8 fusion.18
  695.2 9.9 fusion.20
  710.2 5.6 fusion.276
  715.9 4.7 fusion.45
  724.8 5.2 fusion.430
  729.9 5.2 fusion.428
  755.9 5.8 fusion.138
  771.2 9.4 fusion.119
  791.8 4.8 fusion.15
  796.6 9.8 fusion.17
  811.6 5.2 fusion.273
  816.9 5.2 fusion.431
  837.8 5.7 fusion.139
  845.2 5.6 fusion.429
  850.8 12.4 add_add_fusion
  863.3 8.8 fusion.122
  872.1 6.2 fusion.39
  884.8 4.8 fusion.12
  889.6 9.9 fusion.14
  926.9 8.8 add_add_fusion.1
  935.7 8.7 add_add_fusion.2
  944.4 796.3 %fusion.404 = (f32[64,960]{1,0:T(8,128)S(1)}, f32[64,320]{1,0:T(8,128)S(1)}, f32[64,320]{1,0:T(8,128)}, f32[64,960]{1,0:T(8,128)S(1)}, f32[64,2560]{1,0:T(8,128)S(1)}, /*index=5*/f32[64,2560]{1,0:T(8,128)}) fusion(f32[960,960]{1,0:T(8,128)} %add_add_fusion.4, f32[960,320]{1,0:T(8,128)} %add_add_fusion.12, f32[960,320]{1,0:T(8,128)} %add_add_fusion.11, ...), kind=kCustom, calls=%all-reduce-scatter.6 | all-reduce-scatter fusion | flops 7864321 | bytes 31457792
  1763.9 54.5 %all-reduce.28 = (f32[960]{0:T(1024)S(1)}, f32[960]{0:T(1024)S(1)}) all-reduce(f32[960]{0:T(1024)S(1)} %add_add_fusion.17, f32[960]{0:T(1024)S(1)} %add_add_fusion.16), channel_id=29, replica_groups=mesh['section'=2,'fsdp'=16] {'fsdp'}, use_global_device_ids=true, to_apply=%region_34.35.clone | all-reduce | flops 1920 | bytes 15360
  1822.2 6.4 fusion.417
  1839.4 12.2 select_bitcast_fusion.1
  (716 shorter events, 271.4 us)
Async XLA Ops:
  7.2 181.1 %all-gather.15.cloned.1.call-start = ((), (), s32[]{:S(2)}) async-start(), calls=%async_computation.1 | async-start | bytes 4177920 | tf_op jit(solution)/shard_map/all_gather | solution.py:245
  9.1 189.8 %all-gather.17.cloned.1.call-start = ((), (), s32[]{:S(2)}) async-start(), calls=%async_computation.2 | async-start | bytes 4177920 | tf_op jit(solution)/shard_map/all_gather | solution.py:245
  11.1 307.8 %all-gather.19.cloned.1.call-start = ((), (), s32[]{:S(2)}) async-start(), calls=%async_computation.3 | async-start | bytes 10444800 | tf_op jit(solution)/shard_map/all_gather | solution.py:245
  13.4 432.8 %all-gather.21.cloned.1.call-start = ((), (), s32[]{:S(2)}) async-start(), calls=%async_computation.4 | async-start | bytes 10444800 | tf_op jit(solution)/shard_map/all_gather | solution.py:245
  14.8 517.4 %all-gather.23.cloned.1.call-start = ((), (), s32[]{:S(2)}) async-start(), calls=%async_computation.5 | async-start | bytes 5570560 | tf_op jit(solution)/shard_map/all_gather | solution.py:245
  15.4 1857.6 %reduce-scatter.14.cloned.1.call-start = ((), (), s32[]{:S(2)}) async-start(), calls=%async_computation.6 | async-start | bytes 11141120 | tf_op jit(solution)/shard_map/reduce_scatter | solution.py:298
  15.5 47.4 %copy-start.158 = (bf16[1,60,320]{2,1,0:T(8,128)(2,1)S(1)}, bf16[1,60,320]{2,1,0:T(8,128)(2,1)}, u32[]{:S(2)}) copy-start(bf16[1,60,320]{2,1,0:T(8,128)(2,1)} %param.19) | copy-start | bytes 115204
  17.3 103.9 %copy-start.159 = (bf16[1,60,320]{2,1,0:T(8,128)(2,1)S(1)}, bf16[1,60,320]{2,1,0:T(8,128)(2,1)}, u32[]{:S(2)}) copy-start(bf16[1,60,320]{2,1,0:T(8,128)(2,1)} %param.20) | copy-start | bytes 115204
  62.9 544.0 %copy-start.139 = (f32[960]{0:T(1024)}, f32[960]{0:T(1024)S(1)}, u32[]{:S(2)}) copy-start(f32[960]{0:T(1024)S(1)} %convert_element_type.498) | copy-start | bytes 11524
  121.2 58.7 %copy-start.192 = (s32[2,384]{1,0:T(2,128)S(1)}, s32[2,384]{1,0:T(2,128)}, u32[]{:S(2)}) copy-start(s32[2,384]{1,0:T(2,128)} %param.16) | copy-start | bytes 9220
  121.3 58.7 %copy-start.193 = (s32[2,384]{1,0:T(2,128)S(1)}, s32[2,384]{1,0:T(2,128)}, u32[]{:S(2)}) copy-start(s32[2,384]{1,0:T(2,128)} %param.15) | copy-start | bytes 9220
  179.8 650.8 %copy-start.43 = (bf16[1,960,320]{1,2,0:T(8,128)(2,1)}, bf16[1,960,320]{1,2,0:T(8,128)(2,1)S(1)}, u32[]{:S(2)}) copy-start(bf16[1,960,320]{1,2,0:T(8,128)(2,1)S(1)} %copy.77) | copy-start | bytes 1843204
  179.9 399.3 %copy-start.125 = (f32[960]{0:T(1024)}, f32[960]{0:T(1024)S(1)}, u32[]{:S(2)}) copy-start(f32[960]{0:T(1024)S(1)} %convert_element_type.499) | copy-start | bytes 11524
  184.0 437.6 %copy-start.121 = (f32[384,32]{0,1:T(8,128)}, f32[384,32]{0,1:T(8,128)S(1)}, u32[]{:S(2)}) copy-start(f32[384,32]{0,1:T(8,128)S(1)} %get-tuple-element.147) | copy-start | bytes 147460
  184.0 455.8 %copy-start.77 = (f32[384,32]{0,1:T(8,128)}, f32[384,32]{0,1:T(8,128)S(1)}, u32[]{:S(2)}) copy-start(f32[384,32]{0,1:T(8,128)S(1)} %get-tuple-element.163) | copy-start | bytes 147460
  184.0 471.9 %copy-start.117 = (f32[384,32]{0,1:T(8,128)}, f32[384,32]{0,1:T(8,128)S(1)}, u32[]{:S(2)}) copy-start(f32[384,32]{0,1:T(8,128)S(1)} %get-tuple-element.160) | copy-start | bytes 147460
  184.0 471.9 %copy-start.119 = (f32[384,32]{0,1:T(8,128)}, f32[384,32]{0,1:T(8,128)S(1)}, u32[]{:S(2)}) copy-start(f32[384,32]{0,1:T(8,128)S(1)} %get-tuple-element.161) | copy-start | bytes 147460
  544.5 7.5 collective-permute-start
  555.0 48.9 %copy-start.180 = (f32[384]{0:T(512)}, f32[384]{0:T(512)S(1)}, u32[]{:S(2)}) copy-start(f32[384]{0:T(512)S(1)} %get-tuple-element.86) | copy-start | bytes 4612
  595.7 8.3 collective-permute-start.1
  606.9 12.8 copy-start.26
  656.2 16.7 slice-start.10
  709.1 11.4 slice-start.4
  754.3 16.9 collective-permute-start.2
  835.4 15.4 collective-permute-start.3
  850.8 12.5 copy-start.71
  863.2 15.1 slice-start.6
  863.3 15.1 slice-start.7
  889.6 14.0 copy-start.88
  889.6 13.9 copy-start.118
  889.6 13.9 copy-start.120
  922.0 13.7 slice-start.14
  1740.7 18.8 copy-start.57
  1740.7 18.8 copy-start.130
  1740.7 12.4 copy-start.132
  1740.7 18.7 copy-start.190
  1740.7 18.7 copy-start.191
  1740.7 18.8 copy-start.80
  1743.0 121.8 %collective-permute-start.9 = (f32[60,2560]{1,0:T(8,128)}, f32[60,2560]{1,0:T(8,128)}, u32[]{:S(2)}, u32[]{:S(2)}) collective-permute-start(f32[60,2560]{1,0:T(8,128)} %slice.181), channel_id=1, source_target_pairs={{0,1},{1,2},{2,3},{3,4},{4,5},{5,6},{6,7},{7,8},{8,9},{9,10},{10,1... | collective-permute-start | bytes 1843208
  1746.0 14.1 copy-start.70
  1746.0 14.1 copy-start.102
  1746.0 122.9 %collective-permute-start.8 = (f32[60,2560]{1,0:T(8,128)}, f32[60,2560]{1,0:T(8,128)}, u32[]{:S(2)}, u32[]{:S(2)}) collective-permute-start(f32[60,2560]{1,0:T(8,128)} %slice.180), channel_id=1, source_target_pairs={{0,1},{1,2},{2,3},{3,4},{4,5},{5,6},{6,7},{7,8},{8,9},{9,10},{10,1... | collective-permute-start | bytes 1843208
  1749.2 112.0 %collective-permute-start.7 = (f32[60,960]{1,0:T(8,128)}, f32[60,960]{1,0:T(8,128)}, u32[]{:S(2)}, u32[]{:S(2)}) collective-permute-start(f32[60,960]{1,0:T(8,128)} %slice.179), channel_id=1, source_target_pairs={{0,1},{1,2},{2,3},{3,4},{4,5},{5,6},{6,7},{7,8},{8,9},{9,10},{10,1... | collective-permute-start | bytes 691208
  1753.7 102.4 %collective-permute-start.6 = (f32[60,320]{1,0:T(8,128)}, f32[60,320]{1,0:T(8,128)}, u32[]{:S(2)}, u32[]{:S(2)}) collective-permute-start(f32[60,320]{1,0:T(8,128)} %slice.178), channel_id=1, source_target_pairs={{0,1},{1,2},{2,3},{3,4},{4,5},{5,6},{6,7},{7,8},{8,9},{9,10},{10,1... | collective-permute-start | bytes 230408
  1757.5 101.0 %collective-permute-start.5 = (f32[60,320]{1,0:T(8,128)}, f32[60,320]{1,0:T(8,128)}, u32[]{:S(2)}, u32[]{:S(2)}) collective-permute-start(f32[60,320]{1,0:T(8,128)} %slice.177), channel_id=1, source_target_pairs={{0,1},{1,2},{2,3},{3,4},{4,5},{5,6},{6,7},{7,8},{8,9},{9,10},{10,1... | collective-permute-start | bytes 230408
  1761.7 56.6 %copy-start.177 = (f32[384]{0:T(512)S(1)}, f32[384]{0:T(512)}, u32[]{:S(2)}) copy-start(f32[384]{0:T(512)} %copy-done.176) | copy-start | bytes 4612
  1839.4 12.2 copy-start.49
  1856.0 7.4 collective-permute-start.4
  (212 other events, 850.9 us)
Sparse Core Ops, SparseCore 0:
  11.4 87.3 all-gather.14
  102.2 88.8 all-gather.16
  194.4 124.3 all-gather.18
  322.0 124.1 all-gather.20
  448.9 83.3 all-gather.22
  863.4 383.6 reduce-scatter.13
where the time goes:
time: 1890 us; the launch traced here: 1880 us
  blocking collectives  1010 us (53%)
  matrix products  377 us (20%)
  waiting for transfers between devices  294 us (16%)
  local copies, waits for them, and re-layouts  90.5 us (5%)
  other arithmetic  70 us (4%)
  starting transfers between devices  22.2 us (1%)
  between operations  19.2 us (1%)
    unnamed x3, blocking collectives  895 us
    all_gather x5, waiting for transfers between devices, fetch_weights(): lax.all_gather(as_sent(owned_shards), 'fsdp', axis=0, tiled=True)  294 us
    all_gather x2, blocking collectives, fetch_weights(): lax.all_gather(as_sent(owned_shards), 'fsdp', axis=0, tiled=True)  112 us
    dot_general x36, matrix products, plain_dot(): return jnp.dot(left_side, right_side, preferred_element_type=jnp.float32)  109 us
    dot_general x21, matrix products, outer_sum(): lax.dot_general(left_side, right_side, (((0,), (0,)), ((), ())), preferre...  90.7 us
    unnamed x521, local copies, waits for them, and re-layouts  73.8 us
    dot_general x21, matrix products, back_dot(): lax.dot_general(left_side, right_side, (((1,), (1,)), ((), ())), preferre...  62.9 us
    sub x6, matrix products, layer_forward(): shifted = jnp.exp(scores - jnp.max(scores, axis=-1, keepdims=True))  45.2 us
  transfers between devices with their start and end apart: 16, of which 3 were waited for; matrix products, arithmetic and copies ran while one was open for 55% of the time, Pallas kernels for 0%

commit v1 on v0

v1 whole, which is shorter than its diff:
```python
import jax
import jax.numpy as jnp
from jax import lax
from jax.sharding import PartitionSpec as P

HEADS = 15
KV = 5
HD = 64
GROUP = HEADS // KV

bf16 = jnp.bfloat16
f32 = jnp.float32
epsilon = 1e-05
rope_base = 100000.0


def dot(a, b):
    return jnp.dot(a, b, preferred_element_type=f32)


def dot_tn(a, b):
    return lax.dot_general(a, b, (((0,), (0,)), ((), ())), preferred_element_type=f32)


def dot_nt(a, b):
    return lax.dot_general(a, b, (((1,), (1,)), ((), ())), preferred_element_type=f32)


def one_hot(rows, targets):
    count = targets.shape[0]
    row = lax.broadcasted_iota(jnp.int32, (rows, count), 0)
    return (row == targets[None, :]).astype(bf16)


def split_dot(a, pick):
    high = a.astype(bf16)
    low = (a - high.astype(f32)).astype(bf16)
    return dot(high, pick) + dot(low, pick)


def rope_tables(places):
    half = HD // 2
    frequency = rope_base ** (-jnp.arange(half, dtype=f32) / half)
    angles = places.astype(f32)[:, None] * frequency
    return jnp.cos(angles)[:, None, :], jnp.sin(angles)[:, None, :]


def rotate(values, cosine, sine):
    half = HD // 2
    front, back = values[..., :half], values[..., half:]
    return jnp.concatenate(
        [front * cosine - back * sine, back * cosine + front * sine], axis=-1
    )


def norm_scale(v, features):
    return lax.rsqrt(jnp.sum(v * v, axis=-1, keepdims=True) / features + epsilon)


def norm_back(v, scale, gain, grad, features):
    gain_grad = jnp.sum(grad * v * scale, axis=0)
    weighted = grad * gain
    mean = jnp.sum(weighted * v, axis=-1, keepdims=True) / features
    return scale * weighted - v * (scale * scale * scale) * mean, gain_grad


def forward(x, w, allowed, tables, spread, features):
    length = x.shape[0]
    scale_one = norm_scale(x, features)
    normed = (x * scale_one * w["gain_one"]).astype(bf16)
    qkv = dot(normed, w["qkv"])
    wide = HEADS * HD
    narrow = KV * HD
    queries = rotate(qkv[:, :wide].reshape(length, HEADS, HD), *tables).astype(bf16)
    queries = queries.reshape(length, KV, GROUP, HD)
    keys = rotate(qkv[:, wide : wide + narrow].reshape(length, KV, HD), *tables).astype(bf16)
    values = qkv[:, wide + narrow : wide + 2 * narrow].astype(bf16).reshape(length, KV, HD)
    scores = jnp.einsum("qkgd,pkd->kgqp", queries, keys, preferred_element_type=f32)
    scores = jnp.where(allowed, scores * float(HD) ** (-0.5), -1e30)
    shifted = jnp.exp(scores - jnp.max(scores, axis=-1, keepdims=True))
    probs = shifted / jnp.sum(shifted, axis=-1, keepdims=True)
    attended = jnp.einsum(
        "kgqp,pkd->qkgd", probs.astype(bf16), values, preferred_element_type=f32
    )
    attended = dot(attended.reshape(length, wide).astype(bf16), spread).astype(bf16)
    middle = x + dot(attended, w["out"])
    scale_two = norm_scale(middle, features)
    second = (middle * scale_two * w["gain_two"]).astype(bf16)
    gate = dot(second, w["gate"])
    up = dot(second, w["up"])
    hidden = (jax.nn.silu(gate) * up).astype(bf16)
    output = middle + dot(hidden, w["down"])
    return output, (
        scale_one, normed, queries, keys, values, probs, attended, middle, scale_two, second, gate, up, hidden,
    )


def backward(x, w, tables, spread, features, kept, grad, emit):
    (scale_one, normed, queries, keys, values, probs, attended, middle, scale_two, second, gate, up, hidden) = kept
    length = x.shape[0]
    wide = HEADS * HD
    root = float(HD) ** (-0.5)
    low = grad.astype(bf16)
    emit("down", hidden, low)
    grad_hidden = dot_nt(low, w["down"])
    sig = jax.nn.sigmoid(gate)
    silu = gate * sig
    gate_low = (grad_hidden * up * (sig * (1.0 + gate * (1.0 - sig)))).astype(bf16)
    up_low = (grad_hidden * silu).astype(bf16)
    emit("gate_up", second, jnp.concatenate([gate_low, up_low], axis=1))
    grad_second = dot_nt(gate_low, w["gate"]) + dot_nt(up_low, w["up"])
    grad_norm, gain_two = norm_back(middle, scale_two, w["gain_two"], grad_second, features)
    grad_middle = grad + grad_norm
    middle_low = grad_middle.astype(bf16)
    grad_att = dot_nt(middle_low, w["out"]).astype(bf16)
    grad_att = dot_nt(grad_att, spread).astype(bf16).reshape(length, KV, GROUP, HD)
    grad_probs = jnp.einsum("qkgd,pkd->kgqp", grad_att, values, preferred_element_type=f32)
    grad_values = (
        jnp.einsum("kgqp,qkgd->pkd", probs.astype(bf16), grad_att, preferred_element_type=f32)
        .reshape(length, KV * HD)
        .astype(bf16)
    )
    scores_low = (
        probs * (grad_probs - jnp.sum(probs * grad_probs, axis=-1, keepdims=True))
    ).astype(bf16)
    turned_q = jnp.einsum("kgqp,pkd->qkgd", scores_low, keys, preferred_element_type=f32) * root
    turned_k = jnp.einsum("kgqp,qkgd->pkd", scores_low, queries, preferred_element_type=f32) * root
    cosine, sine = tables
    grad_q = rotate(turned_q.reshape(length, HEADS, HD), cosine, -sine).astype(bf16)
    grad_k = rotate(turned_k, cosine, -sine).astype(bf16)
    grad_qkv = jnp.concatenate(
        [grad_q.reshape(length, wide), grad_k.reshape(length, KV * HD), grad_values], axis=1
    )
    grad_normed = dot_nt(grad_qkv, w["qkv"])
    grad_norm, gain_one = norm_back(x, scale_one, w["gain_one"], grad_normed, features)
    emit("attention", (normed, attended), (grad_qkv, middle_low, gain_one, gain_two))
    return grad_middle + grad_norm


class Halves:
    def __init__(self, n, features, hidden):
        self.n, self.features, self.hidden = n, features, hidden
        self.parts = 2 * n
        self.rows = features // self.parts
        self.padded = -(-self.rows // 16) * 16
        self.wide = self.parts * self.padded
        self.down_rows = hidden // self.parts
        self.section = lax.axis_index("section")
        self.first = self.section == 0
        self.place = lax.axis_index("fsdp")
        lane = jnp.arange(self.wide, dtype=jnp.int32)
        inside = lane % self.padded
        natural = jnp.where(inside < self.rows, lane // self.padded * self.rows + inside, -1)
        self.spread = one_hot(features, natural)
        self.y = self.place // 2 % 2
        self.x = self.place % 2
        self.relative = self.relative_order()

    def permuted_hidden(self, array):
        rows = array.shape[0]
        blocks = array.reshape(rows, self.parts, self.down_rows)
        cut = self.padded
        return jnp.concatenate(
            [
                blocks[:, :, :cut].reshape(rows, -1),
                blocks[:, :, cut : 2 * cut].reshape(rows, -1),
                blocks[:, :, 2 * cut :].reshape(rows, -1),
            ],
            axis=1,
        )

    def natural_hidden(self, array):
        rows = array.shape[0]
        cut = self.padded
        third = self.down_rows - 2 * cut
        one = array[:, : self.wide].reshape(rows, self.parts, cut)
        two = array[:, self.wide : 2 * self.wide].reshape(rows, self.parts, cut)
        three = array[:, 2 * self.wide :].reshape(rows, self.parts, third)
        return jnp.concatenate([one, two, three], axis=2).reshape(rows, self.hidden)

    def swap(self, array):
        return lax.ppermute(array, "section", [(0, 1), (1, 0)])

    def packed(self, weights):
        gain_one, query, key, value, out, gain_two, gate, up, down = weights
        self.wide_qkv = query.shape[1] + key.shape[1] + value.shape[1]
        self.cols_qkv = -(-(self.wide_qkv + 2) // 128) * 128
        spare = self.cols_qkv - self.wide_qkv - 2
        rows = query.shape[0]
        half = self.wide // 2
        columns = jnp.concatenate(
            [
                query, key, value, gain_one[:, None], gain_two[:, None], jnp.zeros((rows, spare), bf16),
                dot(out, self.spread).astype(bf16),
                self.permuted_hidden(gate), self.permuted_hidden(up),
            ],
            axis=1,
        ).reshape(2, self.rows, -1)
        columns = jnp.pad(columns, ((0, 0), (0, self.padded - self.rows), (0, 0)))
        down = dot(down, self.spread).astype(bf16).reshape(2, self.down_rows, self.wide)
        cut = self.padded
        last = down[:, 2 * cut :]
        last = jnp.concatenate([last[:, :, :half], last[:, :, half:]], axis=1)
        return jnp.concatenate([columns, down[:, :cut], down[:, cut : 2 * cut], last], axis=2)

    def gathered(self, weights):
        halves = self.packed(weights)
        keep = jnp.where(self.first, halves[0], halves[1])
        got = self.swap(jnp.where(self.first, halves[1], halves[0]))
        carried = (jnp.where(self.first, keep, got), jnp.where(self.first, got, keep))
        return [
            self.unpacked(lax.all_gather(part, ("fsdp", "section"), axis=0, tiled=True))
            for part in carried
        ]

    def unpacked(self, whole):
        a = self.cols_qkv
        b = a + self.wide
        c = b + self.hidden
        d = c + self.hidden
        half = self.wide // 2
        gains = whole[:, self.wide_qkv : self.wide_qkv + 2].astype(f32).T
        cut = self.padded
        last = whole[:, d + 2 * self.wide :].reshape(self.parts, 2, cut // 2, half)
        last = last.transpose(0, 2, 1, 3).reshape(self.parts * (cut // 2), self.wide)
        return {
            "qkv": whole[:, : self.wide_qkv],
            "gain_one": gains[0],
            "gain_two": gains[1],
            "out": whole[:, a:b],
            "gate": whole[:, b:c],
            "up": whole[:, c:d],
            "down": jnp.concatenate(
                [whole[:, d : d + self.wide], whole[:, d + self.wide : d + 2 * self.wide], last], axis=0
            ),
        }

    def relative_order(self):
        block = jnp.arange(self.parts, dtype=jnp.int32)
        z = block % (self.n // 4)
        quarter = block // (self.n // 4) % 4
        core = self.section ^ (block // self.n)
        low, high = quarter % 2, quarter // 2
        other_x = jnp.where(core == 0, low, high)
        other_y = jnp.where(core == 0, high, low)
        chip = z * 4 + (self.y ^ other_y) * 2 + (self.x ^ other_x)
        return chip * 2 + core

    def order_matrices(self):
        lane = jnp.arange(self.wide, dtype=jnp.int32)
        part = jnp.repeat(self.relative, self.padded)
        inside = lane % self.padded
        half = self.padded // 2
        return (
            one_hot(self.wide, part * self.padded + inside),
            one_hot(self.wide // 2, jnp.where(inside < half, part * half + inside, -1)),
            one_hot(self.wide // 2, jnp.where(inside >= half, part * half + inside - half, -1)),
        )

    def routes(self):
        flips = {"x": 1, "y": 2}
        count = self.n

        def route(by_core):
            return [
                (core * count + i, core * count + (i ^ flips[axis]))
                for core, axis in enumerate(by_core)
                for i in range(count)
            ]

        return route("yx"), route("xy")

    def reduced(self, terms, columns=None):
        half = self.wide // 2

        def product(lo, hi):
            return jnp.concatenate(
                [dot_tn(a[:, lo:hi], b) for a, b in terms]
                + ([columns[lo:hi]] if columns is not None else []),
                axis=1,
            )

        first_route, second_route = self.routes()
        got = self.swap(product(half, self.wide).astype(bf16))
        mine = (product(0, half) + got.astype(f32)).astype(bf16)
        got = lax.ppermute(mine[half // 2 :], ("section", "fsdp"), first_route)
        mine = (mine[: half // 2].astype(f32) + got.astype(f32)).astype(bf16)
        got = lax.ppermute(mine[half // 4 :], ("section", "fsdp"), second_route)
        mine = (mine[: half // 4].astype(f32) + got.astype(f32)).astype(bf16)
        lines = [[q + 4 * z for z in range(self.n // 4)] for q in range(4)]
        return lax.psum_scatter(mine, "fsdp", scatter_dimension=0, tiled=True, axis_index_groups=lines)

    def emitter(self):
        whole, left, right = self.order_matrices()
        sums = {}
        half = self.wide // 2

        def order(a, pick):
            return dot(a, pick).astype(bf16)

        def emit(name, lhs, rhs):
            if name == "down":
                last = lhs[:, 2 * self.wide :]
                both = jnp.concatenate([order(last, left), order(last, right)], axis=0)
                sides = jnp.concatenate([rhs[:, :half], rhs[:, half:]], axis=0)
                terms = [
                    (order(lhs[:, : self.wide], whole), rhs),
                    (order(lhs[:, self.wide : 2 * self.wide], whole), rhs),
                    (both, sides),
                ]
                sums[name] = self.reduced(terms)
            elif name == "gate_up":
                sums[name] = self.reduced([(order(lhs, whole), rhs)])
            else:
                normed, attended = lhs
                grad_qkv, middle_low, gain_one, gain_two = rhs
                gains = dot_tn(whole, jnp.stack([gain_one, gain_two], axis=1).astype(bf16))
                spare = jnp.zeros((self.wide, self.cols_qkv - self.wide_qkv - 2), f32)
                sums[name] = self.reduced(
                    [(order(attended, whole), middle_low), (order(normed, whole), grad_qkv)],
                    jnp.concatenate([gains, spare], axis=1),
                )

        return emit, sums

    def shares(self, sums):
        result = []
        for name in ("down", "gate_up", "attention"):
            zero, one = sums[0][name], sums[1][name]
            keep = jnp.where(self.first, zero, one)
            got = self.swap(jnp.where(self.first, one, zero))
            result.append(
                jnp.stack([jnp.where(self.first, keep, got), jnp.where(self.first, got, keep)]).astype(f32)
            )
        down, gate_up, attention = result
        half = self.wide // 2
        cut = self.padded
        last = down[:, :, 2 * self.wide :]
        last = jnp.concatenate([last[:, : cut // 2], last[:, cut // 2 :]], axis=2)
        down = jnp.concatenate([down[:, :, : self.wide], down[:, :, self.wide : 2 * self.wide], last], axis=1)
        down = self.natural_features(down.reshape(2 * self.down_rows, self.wide))
        gate_up = gate_up[:, : self.rows].reshape(2 * self.rows, -1)
        attention = attention[:, : self.rows].reshape(2 * self.rows, -1)
        out = self.natural_features(attention[:, : self.wide])
        qkv = attention[:, self.wide :]
        wide, narrow = HEADS * HD, KV * HD
        return (
            qkv[:, self.wide_qkv],
            qkv[:, :wide],
            qkv[:, wide : wide + narrow],
            qkv[:, wide + narrow : wide + 2 * narrow],
            out,
            qkv[:, self.wide_qkv + 1],
            self.natural_hidden(gate_up[:, : self.hidden]),
            self.natural_hidden(gate_up[:, self.hidden :]),
            down,
        )

    def natural_features(self, array):
        return dot_nt(array.astype(bf16), self.spread)


class Plain:
    def __init__(self, n, features, hidden):
        self.features, self.wide = features, features
        self.first = lax.axis_index("section") == 0
        self.spread = one_hot(features, jnp.arange(features, dtype=jnp.int32))

    def gathered(self, weights):
        names = ("gain_one", "query", "key", "value", "out", "gain_two", "gate", "up", "down")
        both = [lax.all_gather(part, ("section", "fsdp"), axis=0, tiled=True) for part in weights]
        layers = []
        for layer in range(2):
            w = {name: a.reshape((2, -1) + a.shape[1:])[layer] for name, a in zip(names, both)}
            w["qkv"] = jnp.concatenate([w["query"], w["key"], w["value"]], axis=1)
            w["gain_one"] = w["gain_one"].astype(f32)
            w["gain_two"] = w["gain_two"].astype(f32)
            layers.append(w)
        return layers

    def emitter(self):
        sums = {}

        def reduced(a):
            part = lax.psum_scatter(a, "fsdp", scatter_dimension=0, tiled=True)
            return lax.psum(part, "section")

        def emit(name, lhs, rhs):
            if name == "attention":
                normed, attended = lhs
                grad_qkv, middle_low, gain_one, gain_two = rhs
                sums["out"] = reduced(dot_tn(attended, middle_low))
                sums["qkv"] = reduced(dot_tn(normed, grad_qkv))
                sums["gain_one"] = reduced(gain_one)
                sums["gain_two"] = reduced(gain_two)
            else:
                sums[name] = reduced(dot_tn(lhs, rhs))

        return emit, sums

    def shares(self, sums):
        own = {name: jnp.where(self.first, sums[0][name], sums[1][name]) for name in sums[0]}
        wide, narrow = HEADS * HD, KV * HD
        hidden = own["gate_up"].shape[1] // 2
        return (
            own["gain_one"],
            own["qkv"][:, :wide],
            own["qkv"][:, wide : wide + narrow],
            own["qkv"][:, wide + narrow :],
            own["out"],
            own["gain_two"],
            own["gate_up"][:, :hidden],
            own["gate_up"][:, hidden:],
            own["down"],
        )


def on_device(inputs, cotangent, segments, positions, *weights):
    n = lax.axis_size("fsdp")
    features = inputs.shape[-1]
    hidden = weights[6].shape[-1]
    fits = n == 16 and features == 960 and hidden == 2560
    plan = (Halves if fits else Plain)(n, features, hidden)
    section = lax.axis_index("section")
    first = section == 0
    layers = plan.gathered([weight[0] for weight in weights])
    spread = plan.spread

    def mine(array):
        return lax.dynamic_index_in_dim(array, section, 0, keepdims=False)

    labels = mine(segments)
    length = labels.shape[0]
    token = jnp.arange(length)
    allowed = (labels[:, None] == labels[None, :]) & (token[:, None] >= token[None, :])
    tables = rope_tables(mine(positions))

    start = dot(mine(inputs), spread)
    middle, kept_zero = forward(start, layers[0], allowed, tables, spread, features)
    end, kept_one = forward(middle, layers[1], allowed, tables, spread, features)

    grad = split_dot(mine(cotangent), spread)
    emit_one, sums_one = plan.emitter()
    grad_middle = backward(middle, layers[1], tables, spread, features, kept_one, grad, emit_one)
    emit_zero, sums_zero = plan.emitter()
    grad_start = backward(start, layers[0], tables, spread, features, kept_zero, grad_middle, emit_zero)

    def exchanged(zero, one):
        keep = jnp.where(first, zero, one)
        sent = jnp.where(first, one, zero).astype(bf16)
        got = lax.ppermute(sent, "section", [(0, 1), (1, 0)])
        kept = keep.astype(bf16)
        rest = (keep - kept.astype(f32)).astype(bf16)
        kept = dot_nt(kept, spread) + dot_nt(rest, spread)
        got = dot_nt(got, spread)
        return jnp.stack([jnp.where(first, kept, got), jnp.where(first, got, kept)])[None]

    activations = exchanged(middle, end)
    input_grads = exchanged(grad_start, grad_middle)
    shares = plan.shares((sums_zero, sums_one))
    return (activations, input_grads) + tuple(share[None] for share in shares)


def solution(mesh):
    rows = P("section", "fsdp")
    matrix = P("section", "fsdp", None)
    weights = (rows, matrix, matrix, matrix, matrix, rows, matrix, matrix, matrix)
    tokens = P(None, "fsdp", None)
    return jax.shard_map(
        on_device,
        mesh=mesh,
        in_specs=(tokens, tokens, P(None, "fsdp"), P(None, "fsdp")) + weights,
        out_specs=(P("section", None, "fsdp", None), P("section", None, "fsdp", None)) + weights,
        check_vma=False,
    )
```

time: 1890 us -> 835 us (0.44)
  blocking collectives: 1010 us -> 0 us
  matrix products: 377 us -> 255 us
  waiting for transfers between devices: 294 us -> 370 us
    unnamed x3 -> x0, blocking collectives: 895 us -> none
    all_gather x2 -> x0, blocking collectives: 112 us -> none  [fetch_weights(): lax.all_gather(as_sent(owned_shards), 'fsdp', axis=0, tiled=True)]
    ppermute x4 -> x24, waiting for transfers between devices: 0.01 us -> 109 us  [the longest x6 81.7 us: reduced(): got = lax.ppermute(mine[half // 2:], ('section', 'fsdp'), first_route)]
    dot_general x96 -> x85, matrix products: 332 us -> 241 us  [the longest x31 69.4 us: dot(): return jnp.dot(a, b, preferred_element_type=f32)]
    all_gather x5 -> x2, waiting for transfers between devices: 294 us -> 225 us  [gathered(): lax.all_gather(part, ('fsdp', 'section'), axis=0, tiled=True)]
    unnamed x521 -> x305, local copies, waits for them, and re-layouts: 73.8 us -> 36.6 us
    reduce_scatter x1 -> x4, waiting for transfers between devices: 0.01 us -> 35.2 us  [reduced(): lax.psum_scatter(mine, 'fsdp', scatter_dimension=0, tiled=True, axis_inde...]
    sub x6 -> x2, matrix products: 45.2 us -> 14.7 us  [forward(): shifted = jnp.exp(scores - jnp.max(scores, axis=-1, keepdims=True))]
  transfers between devices with their start and end apart: 16 -> 32, of which waited for: 3 -> 13; matrix products, arithmetic and copies ran while one was open for 55% -> 20% of each run, Pallas kernels for 0% -> 0%
where the time goes in v1:
time: 835 us; the launch traced here: 827 us
  waiting for transfers between devices  370 us (44%)
  matrix products  255 us (31%)
  local copies, waits for them, and re-layouts  83.8 us (10%)
  other arithmetic  82.3 us (10%)
  starting transfers between devices  19.1 us (2%)
  between operations  16.5 us (2%)
    all_gather x2, waiting for transfers between devices, gathered(): lax.all_gather(part, ('fsdp', 'section'), axis=0, tiled=True)  225 us
    ppermute x6, waiting for transfers between devices, reduced(): got = lax.ppermute(mine[half // 2:], ('section', 'fsdp'), first_route)  81.7 us
    dot_general x31, matrix products, dot(): return jnp.dot(a, b, preferred_element_type=f32)  69.4 us
    dot_general x18, matrix products, dot_nt(): lax.dot_general(a, b, (((1,), (1,)), ((), ())), preferred_element_type=f32)  65 us
    dot_general x26, matrix products, dot_tn(): lax.dot_general(a, b, (((0,), (0,)), ((), ())), preferred_element_type=f32)  58.8 us
    unnamed x305, local copies, waits for them, and re-layouts  36.6 us
    reduce_scatter x4, waiting for transfers between devices, reduced(): lax.psum_scatter(mine, 'fsdp', scatter_dimension=0, tiled=True, axis_inde...  35.2 us
    ppermute x6, waiting for transfers between devices, reduced(): got = lax.ppermute(mine[half // 4:], ('section', 'fsdp'), second_route)  25.9 us
  transfers between devices with their start and end apart: 32, of which 13 were waited for; matrix products, arithmetic and copies ran while one was open for 20% of the time, Pallas kernels for 0%

profile of v1, /device:TPU:0, one launch (start us, length us, event | category | flops | bytes accessed | tf_op | source)
XLA Modules:
  0.0 827.1 jit_solution(10518991483180093415)
XLA Ops:
  46.5 129.4 %all-gather.3.cloned.1.call-done = bf16[1024,10368]{1,0:T(8,128)(2,1)} async-done(((bf16[32,10368]{1,0:T(8,128)(2,1)}), bf16[1024,10368]{1,0:T(8,128)(2,1)}) %all-gather.3.cloned.1.call-update) | async-done | bytes 21233680 | tf_op jit(solution)/shard_map/all_gather | solution.py:212
  177.6 3.9 fusion.73
  184.0 7.3 fusion.368
  191.4 4.7 fusion.171
  197.2 3.9 multiply_reduce_fusion.10
  208.1 3.9 multiply_convert_fusion.5
  218.0 95.4 %all-gather.5.cloned.1.call-done = bf16[1024,10368]{1,0:T(8,128)(2,1)} async-done(((bf16[32,10368]{1,0:T(8,128)(2,1)}), bf16[1024,10368]{1,0:T(8,128)(2,1)}) %all-gather.5.cloned.1.call-update) | async-done | bytes 21233680 | tf_op jit(solution)/shard_map/all_gather | solution.py:212
  316.4 3.1 fusion.359
  324.9 4.0 copy-done.42
  338.7 7.4 fusion.369
  346.1 4.4 fusion.174
  362.8 4.7 fusion.16
  367.5 5.9 multiply_convert_fusion.3
  373.5 3.9 select_convert_fusion.1
  394.0 4.7 fusion.14
  398.8 5.1 multiply_reduce_fusion
  408.1 3.8 fusion.177
  411.9 5.8 fusion.198
  417.6 8.3 %fusion.5 = (f32[5,3,384]{2,1,0:T(4,128)S(1)}, f32[5,384,384,3]{2,1,3,0:T(8,128)}) fusion(f32[5,3,384,384]{2,3,1,0:T(8,128)} %get-tuple-element.145, f32[5,3,384]{2,1,0:T(4,128)S(1)} %get-tuple-element.144, bf16[384,5,64,1]{0,2,3,1:T(8,128)(2,1)S(1)} %bitcast.321, bf16[384,5,3,64]{0,3,2,1:T(8,128)(2,1)S(1)} %bitcast.331), kind=kOutput, calls=%fused_computation.11 | convolution fusion | flops 289745280 | bytes 18723840 | tf_op jit(solution)/shard_map/qkgd,pkd->kgqp/dot_general | solution.py:117
  425.9 9.8 %fusion.7 = bf16[5,3,384,384]{2,3,1,0:T(8,128)(2,1)} fusion(f32[5,384,384,3]{2,1,3,0:T(8,128)} %get-tuple-element.154, f32[5,3,384]{2,1,0:T(4,128)S(1)} %get-tuple-element.153, f32[5,3,384,384]{2,3,1,0:T(8,128)} %get-tuple-element.145, f32[5,3,384]{2,1,0:T(4,128)S(1)} %get-tuple-element.144), kind=kLoop, calls=%fused_computation.13 | loop fusion | flops 8847360 | bytes 22164480 | tf_op jit(solution)/shard_map/convert_element_type | solution.py:125
  435.8 3.9 fusion.191
  442.1 3.9 multiply_reduce_fusion.1
  460.4 10.2 %multiply_convert_fusion.1 = (bf16[384,2560]{1,0:T(8,128)(2,1)S(1)}, bf16[384,2560]{1,0:T(8,128)(2,1)S(1)}) fusion(f32[384,2560]{1,0:T(8,128)S(1)} %copy-done.133, f32[384,2560]{1,0:T(8,128)} %get-tuple-element.141, bf16[384,1024]{1,0:T(8,128)(2,1)S(1)} %get-tuple-element.60, bf16[512,1024]{1,0:T(8,128)(2,1)S(1)} %bitcast.306, ...), kind=kOutput, calls=%fused_computation.74 | convolution fusion | flops 2041774080 | bytes 17825792 | tf_op jit(solution)/shard_map/dot_general | solution.py:26
  470.6 6.1 fusion.22
  476.8 5.6 multiply_reduce_fusion.2
  482.8 4.5 fusion.178
  487.3 6.1 fusion.201
  493.4 8.4 %fusion.2 = (f32[5,3,384]{2,1,0:T(4,128)S(1)}, f32[5,384,384,3]{2,1,3,0:T(8,128)}) fusion(f32[5,3,384,384]{2,3,1,0:T(8,128)} %get-tuple-element.137, f32[5,3,384]{2,1,0:T(4,128)S(1)} %copy-done.105, bf16[384,5,64,1]{0,2,3,1:T(8,128)(2,1)S(1)} %bitcast.319, bf16[384,5,3,64]{0,3,2,1:T(8,128)(2,1)S(1)} %bitcast.333), kind=kOutput, calls=%fused_computation.6 | convolution fusion | flops 289745280 | bytes 18723840 | tf_op jit(solution)/shard_map/qkgd,pkd->kgqp/dot_general | solution.py:117
  501.8 9.8 %fusion.4 = bf16[5,3,384,384]{2,3,1,0:T(8,128)(2,1)} fusion(f32[5,384,384,3]{2,1,3,0:T(8,128)} %get-tuple-element.158, f32[5,3,384]{2,1,0:T(4,128)S(1)} %get-tuple-element.157, f32[5,3,384,384]{2,3,1,0:T(8,128)} %get-tuple-element.137, f32[5,3,384]{2,1,0:T(4,128)S(1)} %copy-done.105), kind=kLoop, calls=%fused_computation.8 | loop fusion | flops 8847360 | bytes 22164480 | tf_op jit(solution)/shard_map/convert_element_type | solution.py:125
  511.6 3.9 fusion.193
  535.4 3.1 multiply_reduce_fusion.3
  549.6 4.8 convolution_convert_fusion
  556.5 4.8 convolution_convert_fusion.1
  561.6 3.6 fusion.59
  581.3 10.1 %collective-permute-done.21 = bf16[256,2560]{1,0:T(8,128)(2,1)S(1)} collective-permute-done((bf16[256,2560]{1,0:T(8,128)(2,1)}, bf16[256,2560]{1,0:T(8,128)(2,1)S(1)}, u32[]{:S(2)}, u32[]{:S(2)}) %collective-permute-start.21) | collective-permute-done | bytes 1310752 | tf_op jit(solution)/shard_map/ppermute | solution.py:286
  593.2 12.2 %collective-permute-done.18 = bf16[256,2560]{1,0:T(8,128)(2,1)S(1)} collective-permute-done((bf16[256,2560]{1,0:T(8,128)(2,1)S(1)}, bf16[256,2560]{1,0:T(8,128)(2,1)S(1)}, u32[]{:S(2)}, u32[]{:S(2)}) %collective-permute-start.18) | collective-permute-done | bytes 1310752 | tf_op jit(solution)/shard_map/ppermute | solution.py:286
  608.1 12.1 %collective-permute-done.7 = bf16[256,2688]{0,1:T(8,128)(2,1)S(1)} collective-permute-done((bf16[256,2688]{0,1:T(8,128)(2,1)S(1)}, bf16[256,2688]{0,1:T(8,128)(2,1)S(1)}, u32[]{:S(2)}, u32[]{:S(2)}) %collective-permute-start.7) | collective-permute-done | bytes 1376288 | tf_op jit(solution)/shard_map/ppermute | solution.py:286
  624.0 13.8 %collective-permute-done.22 = bf16[128,2560]{1,0:T(8,128)(2,1)S(1)} collective-permute-done((bf16[128,2560]{1,0:T(8,128)(2,1)S(1)}, bf16[128,2560]{1,0:T(8,128)(2,1)S(1)}, u32[]{:S(2)}, u32[]{:S(2)}) %collective-permute-start.22) | collective-permute-done | bytes 655392 | tf_op jit(solution)/shard_map/ppermute | solution.py:288
  640.2 4.4 collective-permute-done.4
  653.5 6.2 add_convert_fusion
  668.5 6.1 add_convert_fusion.1
  679.0 3.7 select_bitcast_fusion.1
  689.0 5.6 collective-permute-done.14
  694.7 3.5 add_convert_fusion.2
  699.6 37.2 %collective-permute-done.11 = bf16[256,5120]{1,0:T(8,128)(2,1)} collective-permute-done((bf16[256,5120]{1,0:T(8,128)(2,1)}, bf16[256,5120]{1,0:T(8,128)(2,1)}, u32[]{:S(2)}, u32[]{:S(2)}) %collective-permute-start.11) | collective-permute-done | bytes 2621472 | tf_op jit(solution)/shard_map/ppermute | solution.py:286
  736.8 3.5 add_convert_fusion.3
  749.0 12.0 %collective-permute-done.12 = bf16[128,5120]{1,0:T(8,128)(2,1)} collective-permute-done((bf16[128,5120]{1,0:T(8,128)(2,1)}, bf16[128,5120]{1,0:T(8,128)(2,1)}, u32[]{:S(2)}, u32[]{:S(2)}) %collective-permute-start.12) | collective-permute-done | bytes 1310752 | tf_op jit(solution)/shard_map/ppermute | solution.py:288
  775.4 32.3 %reduce-scatter.11.cloned.1.call-done = bf16[32,5120]{1,0:T(8,128)(2,1)} async-done(((bf16[128,5120]{1,0:T(8,128)(2,1)}), bf16[32,5120]{1,0:T(8,128)(2,1)}) %reduce-scatter.11.cloned.1.call-update) | async-done | bytes 327696 | tf_op jit(solution)/shard_map/reduce_scatter | solution.py:291
  (582 shorter events, 249.7 us)
Async XLA Ops:
  7.2 31.6 %copy-start = (bf16[2,384,960]{1,2,0:T(8,128)(2,1)S(1)}, bf16[2,384,960]{1,2,0:T(8,128)(2,1)}, u32[]{:S(2)}) copy-start(bf16[2,384,960]{1,2,0:T(8,128)(2,1)} %param.13) | copy-start | bytes 4423684
  7.2 168.8 %all-gather.3.cloned.1.call-start = ((), (), s32[]{:S(2)}) async-start(), calls=%async_computation.6 | async-start | bytes 21897216 | tf_op jit(solution)/shard_map/all_gather | solution.py:212
  33.8 2.3 collective-permute-start
  37.3 276.1 %all-gather.5.cloned.1.call-start = ((), (), s32[]{:S(2)}) async-start(), calls=%async_computation.7 | async-start | bytes 21897216 | tf_op jit(solution)/shard_map/all_gather | solution.py:212
  38.1 707.9 %reduce-scatter.17.cloned.1.call-start = ((), (), s32[]{:S(2)}) async-start(), calls=%async_computation.11 | async-start | bytes 819200 | tf_op jit(solution)/shard_map/reduce_scatter | solution.py:291
  40.0 176.0 %copy-start.54 = (f32[384,1024]{1,0:T(8,128)}, f32[384,1024]{1,0:T(8,128)S(1)}, u32[]{:S(2)}) copy-start(f32[384,1024]{1,0:T(8,128)S(1)} %get-tuple-element.135) | copy-start | bytes 4718596
  40.6 175.4 %copy-start.112 = (f32[384]{0:T(512)}, f32[384]{0:T(512)S(1)}, u32[]{:S(2)}) copy-start(f32[384]{0:T(512)S(1)} %get-tuple-element.127) | copy-start | bytes 4612
  177.5 26.2 %copy-start.102 = (f32[1024]{0:T(1024)}, f32[1024]{0:T(1024)S(1)}, u32[]{:S(2)}) copy-start(f32[1024]{0:T(1024)S(1)} %get-tuple-element.56) | copy-start | bytes 12292
  177.6 38.4 %copy-start.108 = (f32[1024]{0:T(1024)}, f32[1024]{0:T(1024)S(1)}, u32[]{:S(2)}) copy-start(f32[1024]{0:T(1024)S(1)} %get-tuple-element.57) | copy-start | bytes 12292
  191.3 14.6 %slice-start.2 = ((s8[21233664]{0:T(1024)(128)(4,1)}), s8[4194304]{0:T(1024)(128)(4,1)S(1)}, s32[]{:S(2)}) async-start(s8[21233664]{0:T(1024)(128)(4,1)} %bitcast.284), calls=%async_computation.16 | async-start | bytes 8388608
  191.3 14.5 %slice-start.3 = ((s8[21233664]{0:T(1024)(128)(4,1)}), s8[4194304]{0:T(1024)(128)(4,1)S(1)}, s32[]{:S(2)}) async-start(s8[21233664]{0:T(1024)(128)(4,1)} %bitcast.284), calls=%async_computation.17 | async-start | bytes 8388608
  191.3 14.5 %slice-start.4 = ((s8[21233664]{0:T(1024)(128)(4,1)}), s8[4194304]{0:T(1024)(128)(4,1)S(1)}, s32[]{:S(2)}) async-start(s8[21233664]{0:T(1024)(128)(4,1)} %bitcast.284), calls=%async_computation.18 | async-start | bytes 8388608
  218.0 97.0 %slice-start.14 = ((bf16[1024,10368]{1,0:T(8,128)(2,1)}), bf16[1024,512]{1,0:T(8,128)(2,1)S(1)}, s32[]{:S(2)}) async-start(bf16[1024,10368]{1,0:T(8,128)(2,1)} %all-gather.3.cloned.1.call-done), calls=%async_computation.28 | async-start | bytes 2097152 | tf_op jit(solution)/shard_map/slice | solution.py:224
  322.8 50.6 %copy-start.26 = (f32[384,1024]{1,0:T(8,128)}, f32[384,1024]{1,0:T(8,128)S(1)}, u32[]{:S(2)}) copy-start(f32[384,1024]{1,0:T(8,128)S(1)} %get-tuple-element.143) | copy-start | bytes 4718596
  373.4 20.6 %copy-start.19 = (bf16[384,2560]{1,0:T(8,128)(2,1)}, bf16[384,2560]{1,0:T(8,128)(2,1)S(1)}, u32[]{:S(2)}) copy-start(bf16[384,2560]{1,0:T(8,128)(2,1)S(1)} %get-tuple-element.69) | copy-start | bytes 5898244
  373.4 25.3 %copy-start.16 = (bf16[384,2560]{1,0:T(8,128)(2,1)}, bf16[384,2560]{1,0:T(8,128)(2,1)S(1)}, u32[]{:S(2)}) copy-start(bf16[384,2560]{1,0:T(8,128)(2,1)S(1)} %get-tuple-element.68) | copy-start | bytes 5898244
  446.5 35.9 %copy-start.4 = (f32[384,1024]{1,0:T(8,128)}, f32[384,1024]{1,0:T(8,128)S(1)}, u32[]{:S(2)}) copy-start(f32[384,1024]{1,0:T(8,128)S(1)} %get-tuple-element.61) | copy-start | bytes 4718596
  447.4 81.4 %copy-start.87 = (bf16[384,512]{1,0:T(8,128)(2,1)}, bf16[384,512]{1,0:T(8,128)(2,1)S(1)}, u32[]{:S(2)}) copy-start(bf16[384,512]{1,0:T(8,128)(2,1)S(1)} %get-tuple-element.95) | copy-start | bytes 1179652
  517.9 17.5 %slice-start.8 = ((s8[21233664]{0:T(1024)(128)(4,1)}), s8[4194304]{0:T(1024)(128)(4,1)S(1)}, s32[]{:S(2)}) async-start(s8[21233664]{0:T(1024)(128)(4,1)} %bitcast.286), calls=%async_computation.22 | async-start | bytes 8388608
  519.1 16.3 %slice-start.9 = ((s8[21233664]{0:T(1024)(128)(4,1)}), s8[4194304]{0:T(1024)(128)(4,1)S(1)}, s32[]{:S(2)}) async-start(s8[21233664]{0:T(1024)(128)(4,1)} %bitcast.286), calls=%async_computation.23 | async-start | bytes 8388608
  521.9 39.5 %collective-permute-start.1 = (bf16[384,1024]{1,0:T(8,128)(2,1)}, bf16[384,1024]{1,0:T(8,128)(2,1)}, u32[]{:S(2)}, u32[]{:S(2)}) collective-permute-start(bf16[384,1024]{1,0:T(8,128)(2,1)} %get-tuple-element.150), channel_id=1, source_target_pairs={{0,16},{16,0},{1,17},{17,1},{2,18},{18,2},{3,19},{19,3},{4,20},{20... | collective-permute-start | bytes 2359304 | tf_op jit(solution)/shard_map/ppermute | solution.py:451
  527.0 38.2 %collective-permute-start.20 = (bf16[512,2560]{1,0:T(8,128)(2,1)}, bf16[512,2560]{1,0:T(8,128)(2,1)}, u32[]{:S(2)}, u32[]{:S(2)}) collective-permute-start(bf16[512,2560]{1,0:T(8,128)(2,1)} %pad_maximum_fusion.7), channel_id=1, source_target_pairs={{0,16},{16,0},{1,17},{17,1},{2,18},{18,2},{3,19},{19,3},{4,20},{20... | collective-permute-start | bytes 7864328 | tf_op jit(solution)/shard_map/ppermute | solution.py:182
  532.2 37.3 %collective-permute-start.17 = (bf16[512,2560]{1,0:T(8,128)(2,1)}, bf16[512,2560]{1,0:T(8,128)(2,1)}, u32[]{:S(2)}, u32[]{:S(2)}) collective-permute-start(bf16[512,2560]{1,0:T(8,128)(2,1)} %pad_maximum_fusion.6), channel_id=1, source_target_pairs={{0,16},{16,0},{1,17},{17,1},{2,18},{18,2},{3,19},{19,3},{4,20},{20... | collective-permute-start | bytes 7864328 | tf_op jit(solution)/shard_map/ppermute | solution.py:182
  535.0 38.4 %collective-permute-start.6 = (bf16[512,2688]{0,1:T(8,128)(2,1)}, bf16[512,2688]{0,1:T(8,128)(2,1)}, u32[]{:S(2)}, u32[]{:S(2)}) collective-permute-start(bf16[512,2688]{0,1:T(8,128)(2,1)} %pad_maximum_fusion.5), channel_id=1, source_target_pairs={{0,16},{16,0},{1,17},{17,1},{2,18},{18,2},{3,19},{19,3},{4,20},{20... | collective-permute-start | bytes 8257544 | tf_op jit(solution)/shard_map/ppermute | solution.py:182
  554.4 99.0 %collective-permute-start.13 = (bf16[512,5120]{1,0:T(8,128)(2,1)}, bf16[512,5120]{1,0:T(8,128)(2,1)}, u32[]{:S(2)}, u32[]{:S(2)}) collective-permute-start(bf16[512,5120]{1,0:T(8,128)(2,1)} %convolution_convert_fusion), channel_id=1, source_target_pairs={{0,16},{16,0},{1,17},{17,1},{2,18},{18,2},{3,19},{19,3},{4,20},{20... | collective-permute-start | bytes 15728648 | tf_op jit(solution)/shard_map/ppermute | solution.py:182
  561.4 16.1 %collective-permute-start.3 = (bf16[512,2688]{0,1:T(8,128)(2,1)}, bf16[512,2688]{0,1:T(8,128)(2,1)}, u32[]{:S(2)}, u32[]{:S(2)}) collective-permute-start(bf16[512,2688]{0,1:T(8,128)(2,1)} %pad_maximum_fusion.4), channel_id=1, source_target_pairs={{0,16},{16,0},{1,17},{17,1},{2,18},{18,2},{3,19},{19,3},{4,20},{20... | collective-permute-start | bytes 8257544 | tf_op jit(solution)/shard_map/ppermute | solution.py:182
  565.2 103.2 %collective-permute-start.10 = (bf16[512,5120]{1,0:T(8,128)(2,1)}, bf16[512,5120]{1,0:T(8,128)(2,1)}, u32[]{:S(2)}, u32[]{:S(2)}) collective-permute-start(bf16[512,5120]{1,0:T(8,128)(2,1)} %convolution_convert_fusion.1), channel_id=1, source_target_pairs={{0,16},{16,0},{1,17},{17,1},{2,18},{18,2},{3,19},{19,3},{4,20},{20... | collective-permute-start | bytes 15728648 | tf_op jit(solution)/shard_map/ppermute | solution.py:182
  569.6 109.4 %collective-permute-start.2 = (bf16[384,1024]{1,0:T(8,128)(2,1)}, bf16[384,1024]{1,0:T(8,128)(2,1)}, u32[]{:S(2)}, u32[]{:S(2)}) collective-permute-start(bf16[384,1024]{1,0:T(8,128)(2,1)} %get-tuple-element.58), channel_id=1, source_target_pairs={{0,16},{16,0},{1,17},{17,1},{2,18},{18,2},{3,19},{19,3},{4,20},{20... | collective-permute-start | bytes 2359304 | tf_op jit(solution)/shard_map/ppermute | solution.py:451
  573.5 17.9 %collective-permute-start.21 = (bf16[256,2560]{1,0:T(8,128)(2,1)}, bf16[256,2560]{1,0:T(8,128)(2,1)S(1)}, u32[]{:S(2)}, u32[]{:S(2)}) collective-permute-start(bf16[256,2560]{1,0:T(8,128)(2,1)} %slice.690), channel_id=1, source_target_pairs={{0,2},{1,3},{2,0},{3,1},{4,6},{5,7},{6,4},{7,5},{8,10},{9,11},{10,... | collective-permute-start | bytes 3932168 | tf_op jit(solution)/shard_map/ppermute | solution.py:286
  577.5 28.0 %collective-permute-start.18 = (bf16[256,2560]{1,0:T(8,128)(2,1)S(1)}, bf16[256,2560]{1,0:T(8,128)(2,1)S(1)}, u32[]{:S(2)}, u32[]{:S(2)}) collective-permute-start(bf16[256,2560]{1,0:T(8,128)(2,1)S(1)} %slice.675), channel_id=1, source_target_pairs={{0,2},{1,3},{2,0},{3,1},{4,6},{5,7},{6,4},{7,5},{8,10},{9,11},{10,... | collective-permute-start | bytes 3932168 | tf_op jit(solution)/shard_map/ppermute | solution.py:286
  591.4 28.8 %collective-permute-start.7 = (bf16[256,2688]{0,1:T(8,128)(2,1)S(1)}, bf16[256,2688]{0,1:T(8,128)(2,1)S(1)}, u32[]{:S(2)}, u32[]{:S(2)}) collective-permute-start(bf16[256,2688]{0,1:T(8,128)(2,1)S(1)} %slice.636), channel_id=1, source_target_pairs={{0,2},{1,3},{2,0},{3,1},{4,6},{5,7},{6,4},{7,5},{8,10},{9,11},{10,... | collective-permute-start | bytes 4128776 | tf_op jit(solution)/shard_map/ppermute | solution.py:286
  605.4 39.3 %collective-permute-start.4 = (bf16[256,2688]{0,1:T(8,128)(2,1)S(1)}, bf16[256,2688]{0,1:T(8,128)(2,1)}, u32[]{:S(2)}, u32[]{:S(2)}) collective-permute-start(bf16[256,2688]{0,1:T(8,128)(2,1)S(1)} %slice.628), channel_id=1, source_target_pairs={{0,2},{1,3},{2,0},{3,1},{4,6},{5,7},{6,4},{7,5},{8,10},{9,11},{10,... | collective-permute-start | bytes 4128776 | tf_op jit(solution)/shard_map/ppermute | solution.py:286
  620.2 17.7 %collective-permute-start.22 = (bf16[128,2560]{1,0:T(8,128)(2,1)S(1)}, bf16[128,2560]{1,0:T(8,128)(2,1)S(1)}, u32[]{:S(2)}, u32[]{:S(2)}) collective-permute-start(bf16[128,2560]{1,0:T(8,128)(2,1)S(1)} %slice.692), channel_id=1, source_target_pairs={{0,1},{1,0},{2,3},{3,2},{4,5},{5,4},{6,7},{7,6},{8,9},{9,8},{10,11... | collective-permute-start | bytes 1966088 | tf_op jit(solution)/shard_map/ppermute | solution.py:288
  637.8 12.2 %collective-permute-start.19 = (bf16[128,2560]{1,0:T(8,128)(2,1)}, bf16[128,2560]{1,0:T(8,128)(2,1)}, u32[]{:S(2)}, u32[]{:S(2)}) collective-permute-start(bf16[128,2560]{1,0:T(8,128)(2,1)} %slice.677), channel_id=1, source_target_pairs={{0,1},{1,0},{2,3},{3,2},{4,5},{5,4},{6,7},{7,6},{8,9},{9,8},{10,11... | collective-permute-start | bytes 1966088 | tf_op jit(solution)/shard_map/ppermute | solution.py:288
  640.2 105.8 %reduce-scatter.15.cloned.1.call-start = ((), (), s32[]{:S(2)}) async-start(), calls=%async_computation.10 | async-start | bytes 819200 | tf_op jit(solution)/shard_map/reduce_scatter | solution.py:291
  644.7 19.4 %collective-permute-start.8 = (bf16[128,2688]{0,1:T(8,128)(2,1)}, bf16[128,2688]{0,1:T(8,128)(2,1)}, u32[]{:S(2)}, u32[]{:S(2)}) collective-permute-start(bf16[128,2688]{0,1:T(8,128)(2,1)} %slice.638), channel_id=1, source_target_pairs={{0,1},{1,0},{2,3},{3,2},{4,5},{5,4},{6,7},{7,6},{8,9},{9,8},{10,11... | collective-permute-start | bytes 2064392 | tf_op jit(solution)/shard_map/ppermute | solution.py:288
  650.0 34.5 %collective-permute-start.5 = (bf16[128,2688]{0,1:T(8,128)(2,1)}, bf16[128,2688]{0,1:T(8,128)(2,1)}, u32[]{:S(2)}, u32[]{:S(2)}) collective-permute-start(bf16[128,2688]{0,1:T(8,128)(2,1)} %slice.630), channel_id=1, source_target_pairs={{0,1},{1,0},{2,3},{3,2},{4,5},{5,4},{6,7},{7,6},{8,9},{9,8},{10,11... | collective-permute-start | bytes 2064392 | tf_op jit(solution)/shard_map/ppermute | solution.py:288
  653.0 110.8 %reduce-scatter.21.cloned.1.call-start = ((), (), s32[]{:S(2)}) async-start(), calls=%async_computation.13 | async-start | bytes 860160
  662.7 32.0 %collective-permute-start.14 = (bf16[256,5120]{1,0:T(8,128)(2,1)}, bf16[256,5120]{1,0:T(8,128)(2,1)}, u32[]{:S(2)}, u32[]{:S(2)}) collective-permute-start(bf16[256,5120]{1,0:T(8,128)(2,1)} %slice.654), channel_id=1, source_target_pairs={{0,2},{1,3},{2,0},{3,1},{4,6},{5,7},{6,4},{7,5},{8,10},{9,11},{10,... | collective-permute-start | bytes 7864328 | tf_op jit(solution)/shard_map/ppermute | solution.py:286
  668.4 96.7 %reduce-scatter.19.cloned.1.call-start = ((), (), s32[]{:S(2)}) async-start(), calls=%async_computation.12 | async-start | bytes 860160
  678.3 58.6 %collective-permute-start.11 = (bf16[256,5120]{1,0:T(8,128)(2,1)}, bf16[256,5120]{1,0:T(8,128)(2,1)}, u32[]{:S(2)}, u32[]{:S(2)}) collective-permute-start(bf16[256,5120]{1,0:T(8,128)(2,1)} %slice.648), channel_id=1, source_target_pairs={{0,2},{1,3},{2,0},{3,1},{4,6},{5,7},{6,4},{7,5},{8,10},{9,11},{10,... | collective-permute-start | bytes 7864328 | tf_op jit(solution)/shard_map/ppermute | solution.py:286
  689.0 86.4 %reduce-scatter.13.cloned.1.call-start = ((), (), s32[]{:S(2)}) async-start(), calls=%async_computation.9 | async-start | bytes 1638400 | tf_op jit(solution)/shard_map/reduce_scatter | solution.py:291
  698.3 46.0 %collective-permute-start.15 = (bf16[128,5120]{1,0:T(8,128)(2,1)S(1)}, bf16[128,5120]{1,0:T(8,128)(2,1)S(1)}, u32[]{:S(2)}, u32[]{:S(2)}) collective-permute-start(bf16[128,5120]{1,0:T(8,128)(2,1)S(1)} %slice.656), channel_id=1, source_target_pairs={{0,1},{1,0},{2,3},{3,2},{4,5},{5,4},{6,7},{7,6},{8,9},{9,8},{10,11... | collective-permute-start | bytes 3932168 | tf_op jit(solution)/shard_map/ppermute | solution.py:288
  743.1 17.9 %collective-permute-start.12 = (bf16[128,5120]{1,0:T(8,128)(2,1)}, bf16[128,5120]{1,0:T(8,128)(2,1)}, u32[]{:S(2)}, u32[]{:S(2)}) collective-permute-start(bf16[128,5120]{1,0:T(8,128)(2,1)} %slice.650), channel_id=1, source_target_pairs={{0,1},{1,0},{2,3},{3,2},{4,5},{5,4},{6,7},{7,6},{8,9},{9,8},{10,11... | collective-permute-start | bytes 3932168 | tf_op jit(solution)/shard_map/ppermute | solution.py:288
  745.8 62.0 %reduce-scatter.11.cloned.1.call-start = ((), (), s32[]{:S(2)}) async-start(), calls=%async_computation.8 | async-start | bytes 1638400 | tf_op jit(solution)/shard_map/reduce_scatter | solution.py:291
  747.0 1.9 collective-permute-start.23
  766.7 1.9 collective-permute-start.9
  808.8 2.3 collective-permute-start.16
  (134 other events, 569.8 us)
Sparse Core Ops, SparseCore 0:
  37.5 138.4 all-gather.2
  179.4 133.9 all-gather.4
  640.3 20.3 reduce-scatter.16
  662.8 21.0 reduce-scatter.14
  686.1 21.4 reduce-scatter.20
  709.8 21.3 reduce-scatter.18
  745.9 29.4 reduce-scatter.12
  777.7 29.9 reduce-scatter.10

commit v2 on v1

--- a/solution.py
+++ b/solution.py
@@ -64,13 +64,17 @@
     return scale * weighted - v * (scale * scale * scale) * mean, gain_grad
 
 
-def forward(x, w, allowed, tables, spread, features):
+def forward(x, source, allowed, tables, features):
     length = x.shape[0]
-    scale_one = norm_scale(x, features)
-    normed = (x * scale_one * w["gain_one"]).astype(bf16)
-    qkv = dot(normed, w["qkv"])
     wide = HEADS * HD
     narrow = KV * HD
+    for name in ("attention", "gate_up", "attention", "down", "attention", "gate_up", "attention"):
+        x = source.tie(x, name)
+    w = source.weights("attention")
+    scale_one = norm_scale(x, features)
+    normed = w["order"]((x * scale_one * w["gain_one"]).astype(bf16))
+    qkv = dot(normed, w["qkv"])
+    qkv = source.tie(qkv, "down")
     queries = rotate(qkv[:, :wide].reshape(length, HEADS, HD), *tables).astype(bf16)
     queries = queries.reshape(length, KV, GROUP, HD)
     keys = rotate(qkv[:, wide : wide + narrow].reshape(length, KV, HD), *tables).astype(bf16)
@@ -82,38 +86,48 @@
     attended = jnp.einsum(
         "kgqp,pkd->qkgd", probs.astype(bf16), values, preferred_element_type=f32
     )
-    attended = dot(attended.reshape(length, wide).astype(bf16), spread).astype(bf16)
+    attended = dot(attended.reshape(length, wide).astype(bf16), w["spread"]).astype(bf16)
+    attended = source.tie(attended, "gate_up")
     middle = x + dot(attended, w["out"])
+    middle = source.tie(middle, "gate_up")
+    w.update(source.weights("gate_up"))
     scale_two = norm_scale(middle, features)
-    second = (middle * scale_two * w["gain_two"]).astype(bf16)
+    second = w["order"]((middle * scale_two * w["gain_two"]).astype(bf16))
     gate = dot(second, w["gate"])
     up = dot(second, w["up"])
     hidden = (jax.nn.silu(gate) * up).astype(bf16)
+    hidden = source.tie(hidden, "down")
+    hidden = source.tie(hidden, "down")
+    w.update(source.weights("down"))
+    hidden = w["order_hidden"](hidden)
     output = middle + dot(hidden, w["down"])
-    return output, (
+    return output, w, (
         scale_one, normed, queries, keys, values, probs, attended, middle, scale_two, second, gate, up, hidden,
     )
 
 
-def backward(x, w, tables, spread, features, kept, grad, emit):
+def backward(x, w, tables, features, kept, grad, flow):
     (scale_one, normed, queries, keys, values, probs, attended, middle, scale_two, second, gate, up, hidden) = kept
     length = x.shape[0]
     wide = HEADS * HD
     root = float(HD) ** (-0.5)
     low = grad.astype(bf16)
-    emit("down", hidden, low)
-    grad_hidden = dot_nt(low, w["down"])
+    flow.begin("down", w["relative_hidden"](hidden), low)
+    grad_hidden = w["back_hidden"](dot_nt(low, w["down"]))
     sig = jax.nn.sigmoid(gate)
     silu = gate * sig
     gate_low = (grad_hidden * up * (sig * (1.0 + gate * (1.0 - sig)))).astype(bf16)
     up_low = (grad_hidden * silu).astype(bf16)
-    emit("gate_up", second, jnp.concatenate([gate_low, up_low], axis=1))
+    gate_low, up_low = flow.tie((gate_low, up_low), "down", "+attention", "+gate_up")
+    flow.begin("gate_up", w["relative"](second), jnp.concatenate([gate_low, up_low], axis=1))
     grad_second = dot_nt(gate_low, w["gate"]) + dot_nt(up_low, w["up"])
+    grad_second = w["back"](grad_second)
     grad_norm, gain_two = norm_back(middle, scale_two, w["gain_two"], grad_second, features)
     grad_middle = grad + grad_norm
+    grad_middle = flow.tie(grad_middle, "gate_up", "down", "+attention")
     middle_low = grad_middle.astype(bf16)
     grad_att = dot_nt(middle_low, w["out"]).astype(bf16)
-    grad_att = dot_nt(grad_att, spread).astype(bf16).reshape(length, KV, GROUP, HD)
+    grad_att = dot_nt(grad_att, w["spread"]).astype(bf16).reshape(length, KV, GROUP, HD)
     grad_probs = jnp.einsum("qkgd,pkd->kgqp", grad_att, values, preferred_element_type=f32)
     grad_values = (
         jnp.einsum("kgqp,qkgd->pkd", probs.astype(bf16), grad_att, preferred_element_type=f32)
@@ -123,6 +137,7 @@
     scores_low = (
         probs * (grad_probs - jnp.sum(probs * grad_probs, axis=-1, keepdims=True))
     ).astype(bf16)
+    scores_low = flow.tie(scores_low, "down")
     turned_q = jnp.einsum("kgqp,pkd->qkgd", scores_low, keys, preferred_element_type=f32) * root
     turned_k = jnp.einsum("kgqp,qkgd->pkd", scores_low, queries, preferred_element_type=f32) * root
     cosine, sine = tables
@@ -131,10 +146,74 @@
     grad_qkv = jnp.concatenate(
         [grad_q.reshape(length, wide), grad_k.reshape(length, KV * HD), grad_values], axis=1
     )
-    grad_normed = dot_nt(grad_qkv, w["qkv"])
+    grad_qkv = flow.tie(grad_qkv, "gate_up")
+    grad_normed = w["back"](dot_nt(grad_qkv, w["qkv"]))
     grad_norm, gain_one = norm_back(x, scale_one, w["gain_one"], grad_normed, features)
-    emit("attention", (normed, attended), (grad_qkv, middle_low, gain_one, gain_two))
-    return grad_middle + grad_norm
+    flow.begin("attention", (w["relative"](normed), w["relative"](attended)), (grad_qkv, middle_low, gain_one, gain_two))
+    grad = flow.tie(grad_middle + grad_norm, "attention")
+    flow.next_layer()
+    return grad
+
+
+class Arriving:
+    def __init__(self, steps, unpack):
+        self.table = {name: (one, next(one)) for name, one in steps.items()}
+        self.unpack = unpack
+
+    def tie(self, value, name):
+        steps, waited = self.table[name]
+        if steps is None:
+            return value
+        value, got = lax.optimization_barrier((value, waited))
+        try:
+            self.table[name] = (steps, steps.send(got))
+        except StopIteration as end:
+            self.table[name] = (None, end.value)
+        return value
+
+    def weights(self, name):
+        while self.table[name][0] is not None:
+            self.tie((), name)
+        return self.unpack(name, self.table[name][1])
+
+
+class Flow:
+    def __init__(self, begin):
+        self.begun = begin
+        self.now, self.before, self.done = {}, {}, []
+
+    def begin(self, name, lhs, rhs):
+        steps = self.begun(name, lhs, rhs)
+        self.now[name] = (steps, next(steps))
+
+    def tie(self, value, *names):
+        tables = [(self.before, n[1:]) if n.startswith("+") else (self.now, n) for n in names]
+        tables = [(table, n) for table, n in tables if n in table and table[n][0] is not None]
+        value, waited = lax.optimization_barrier((value, [table[n][1] for table, n in tables]))
+        for (table, n), got in zip(tables, waited):
+            self.advance(table, n, got)
+        return value
+
+    def advance(self, table, name, got):
+        steps = table[name][0]
+        try:
+            table[name] = (steps, steps.send(got))
+        except StopIteration as end:
+            table[name] = (None, end.value)
+
+    def next_layer(self):
+        self.done.append(self.before)
+        self.before, self.now = self.now, {}
+
+    def finished(self):
+        self.next_layer()
+        tables = self.done[1:]
+        for table in tables:
+            while any(steps is not None for steps, _ in table.values()):
+                for name in table:
+                    if table[name][0] is not None:
+                        self.advance(table, name, table[name][1])
+        return [{name: value for name, (_, value) in table.items()} for table in tables]
 
 
 class Halves:
@@ -188,51 +267,138 @@
         spare = self.cols_qkv - self.wide_qkv - 2
         rows = query.shape[0]
         half = self.wide // 2
-        columns = jnp.concatenate(
-            [
-                query, key, value, gain_one[:, None], gain_two[:, None], jnp.zeros((rows, spare), bf16),
-                dot(out, self.spread).astype(bf16),
-                self.permuted_hidden(gate), self.permuted_hidden(up),
-            ],
-            axis=1,
-        ).reshape(2, self.rows, -1)
-        columns = jnp.pad(columns, ((0, 0), (0, self.padded - self.rows), (0, 0)))
+
+        def halves(parts):
+            both = jnp.concatenate(parts, axis=1).reshape(2, self.rows, -1)
+            return jnp.pad(both, ((0, 0), (0, self.padded - self.rows), (0, 0)))
+
         down = dot(down, self.spread).astype(bf16).reshape(2, self.down_rows, self.wide)
         cut = self.padded
         last = down[:, 2 * cut :]
         last = jnp.concatenate([last[:, :, :half], last[:, :, half:]], axis=1)
-        return jnp.concatenate([columns, down[:, :cut], down[:, cut : 2 * cut], last], axis=2)
-
-    def gathered(self, weights):
-        halves = self.packed(weights)
-        keep = jnp.where(self.first, halves[0], halves[1])
-        got = self.swap(jnp.where(self.first, halves[1], halves[0]))
-        carried = (jnp.where(self.first, keep, got), jnp.where(self.first, got, keep))
-        return [
-            self.unpacked(lax.all_gather(part, ("fsdp", "section"), axis=0, tiled=True))
-            for part in carried
+        return {
+            "attention": halves([
+                query, key, value, gain_one[:, None], gain_two[:, None], jnp.zeros((rows, spare), bf16),
+                dot(out, self.spread).astype(bf16),
+            ]),
+            "gate_up": halves([self.permuted_hidden(gate), self.permuted_hidden(up)]),
+            "down": jnp.concatenate([down[:, :cut], down[:, cut : 2 * cut], last], axis=2),
+        }
+
+    def sources(self, weights):
+        carried = {}
+        for name, halves in self.packed(weights).items():
+            keep = jnp.where(self.first, halves[0], halves[1])
+            got = self.swap(jnp.where(self.first, halves[1], halves[0]))
+            carried[name] = (jnp.where(self.first, keep, got), jnp.where(self.first, got, keep))
+        names = ("attention", "gate_up", "down")
+        whole, left, right = self.order_matrices()
+        both = self.wide
+
+        def to_relative(a):
+            return dot(a, whole).astype(bf16)
+
+        def hidden_to_relative(a):
+            last = a[:, 2 * both :]
+            return jnp.concatenate(
+                [
+                    to_relative(a[:, :both]),
+                    to_relative(a[:, both : 2 * both]),
+                    dot(last, self.order_last).astype(bf16),
+                ],
+                axis=1,
+            )
+
+        def from_relative(a):
+            high = a.astype(bf16)
+            low = (a - high.astype(f32)).astype(bf16)
+            return dot_nt(high, whole) + dot_nt(low, whole)
+
+        def hidden_from_relative(a):
+            a = a.astype(bf16)
+            return jnp.concatenate(
+                [
+                    dot_nt(a[:, :both], whole),
+                    dot_nt(a[:, both : 2 * both], whole),
+                    dot_nt(a[:, 2 * both :], self.order_last),
+                ],
+                axis=1,
+            )
+
+        def same(a):
+            return a
+
+        moved = {
+            "order": to_relative, "order_hidden": hidden_to_relative, "relative": same,
+            "relative_hidden": same, "back": from_relative, "back_hidden": hidden_from_relative,
+            "spread": dot(self.spread, whole).astype(bf16),
+        }
+        straight = {
+            "order": same, "order_hidden": same, "relative": to_relative,
+            "relative_hidden": hidden_to_relative, "back": same, "back_hidden": same,
+            "spread": self.spread,
+        }
+
+        def unpack_moved(name, a):
+            w = self.unpacked(name, a)
+            if name == "attention":
+                gains = dot(whole, a[:, self.wide_qkv : self.cols_qkv])[:, :2].T
+                w.update(moved, gain_one=gains[0], gain_two=gains[1])
+            return w
+
+        def unpack_straight(name, a):
+            w = self.unpacked(name, a)
+            if name == "attention":
+                gains = a[:, self.wide_qkv : self.wide_qkv + 2].astype(f32).T
+                w.update(straight, gain_one=gains[0], gain_two=gains[1])
+            return w
+
+        def one_gather():
+            sent = jnp.concatenate([carried[name][1] for name in names], axis=1)
+            return lax.all_gather(sent, ("fsdp", "section"), axis=0, tiled=True)
+
+        gathered = one_gather()
+        widths = [carried[name][1].shape[1] for name in names]
+
+        def column(index):
+            at = sum(widths[:index])
+            yield ()
+            return gathered[:, at : at + widths[index]]
+
+        return (
+            Arriving({name: self.travelled(carried[name][0]) for name in names}, unpack_moved),
+            Arriving({name: column(index) for index, name in enumerate(names)}, unpack_straight),
+        )
+
+    def travelled(self, part):
+        depth = self.n // 4
+        got = yield [
+            lax.ppermute(part, "fsdp", [(i, (i + 4 * k) % self.n) for i in range(self.n)])
+            for k in range(1, depth)
         ]
-
-    def unpacked(self, whole):
-        a = self.cols_qkv
-        b = a + self.wide
-        c = b + self.hidden
-        d = c + self.hidden
+        ring = [part] + list(got)
+        turned = jnp.concatenate([ring[(depth - 1 - k) % depth] for k in range(2 * depth - 1)], axis=0)
+        z = self.place // 4
+        line = lax.dynamic_slice_in_dim(turned, (depth - 1 - z) * self.padded, depth * self.padded, 0)
+        first_route, second_route = self.routes()
+        got = yield lax.ppermute(line, ("section", "fsdp"), second_route)
+        pair = jnp.concatenate([line, got], axis=0)
+        got = yield lax.ppermute(pair, ("section", "fsdp"), first_route)
+        mine = jnp.concatenate([pair, got], axis=0)
+        got = yield self.swap(mine)
+        return jnp.concatenate([mine, got], axis=0)
+
+    def unpacked(self, name, whole):
+        if name == "attention":
+            return {"qkv": whole[:, : self.wide_qkv], "out": whole[:, self.cols_qkv :]}
+        if name == "gate_up":
+            return {"gate": whole[:, : self.hidden], "up": whole[:, self.hidden :]}
         half = self.wide // 2
-        gains = whole[:, self.wide_qkv : self.wide_qkv + 2].astype(f32).T
         cut = self.padded
-        last = whole[:, d + 2 * self.wide :].reshape(self.parts, 2, cut // 2, half)
+        last = whole[:, 2 * self.wide :].reshape(self.parts, 2, cut // 2, half)
         last = last.transpose(0, 2, 1, 3).reshape(self.parts * (cut // 2), self.wide)
         return {
-            "qkv": whole[:, : self.wide_qkv],
-            "gain_one": gains[0],
-            "gain_two": gains[1],
-            "out": whole[:, a:b],
-            "gate": whole[:, b:c],
-            "up": whole[:, c:d],
-            "down": jnp.concatenate(
-                [whole[:, d : d + self.wide], whole[:, d + self.wide : d + 2 * self.wide], last], axis=0
-            ),
+            "down": jnp.concatenate([whole[:, : self.wide], whole[:, self.wide : 2 * self.wide], last], axis=0)
         }
 
     def relative_order(self):
@@ -251,10 +417,13 @@
         part = jnp.repeat(self.relative, self.padded)
         inside = lane % self.padded
         half = self.padded // 2
+        block = lane // self.padded * half
+        short = jnp.arange(self.wide // 2, dtype=jnp.int32)
+        self.order_last = one_hot(self.wide // 2, jnp.repeat(self.relative, half) * half + short % half)
         return (
             one_hot(self.wide, part * self.padded + inside),
-            one_hot(self.wide // 2, jnp.where(inside < half, part * half + inside, -1)),
-            one_hot(self.wide // 2, jnp.where(inside >= half, part * half + inside - half, -1)),
+            one_hot(self.wide // 2, jnp.where(inside < half, block + inside, -1)),
+            one_hot(self.wide // 2, jnp.where(inside >= half, block + inside - half, -1)),
         )
 
     def routes(self):
@@ -281,47 +450,45 @@
             )
 
         first_route, second_route = self.routes()
-        got = self.swap(product(half, self.wide).astype(bf16))
+        got = yield self.swap(product(half, self.wide).astype(bf16))
         mine = (product(0, half) + got.astype(f32)).astype(bf16)
-        got = lax.ppermute(mine[half // 2 :], ("section", "fsdp"), first_route)
+        got = yield lax.ppermute(mine[half // 2 :], ("section", "fsdp"), first_route)
         mine = (mine[: half // 2].astype(f32) + got.astype(f32)).astype(bf16)
-        got = lax.ppermute(mine[half // 4 :], ("section", "fsdp"), second_route)
+        got = yield lax.ppermute(mine[half // 4 :], ("section", "fsdp"), second_route)
         mine = (mine[: half // 4].astype(f32) + got.astype(f32)).astype(bf16)
         lines = [[q + 4 * z for z in range(self.n // 4)] for q in range(4)]
         return lax.psum_scatter(mine, "fsdp", scatter_dimension=0, tiled=True, axis_index_groups=lines)
 
     def emitter(self):
         whole, left, right = self.order_matrices()
-        sums = {}
         half = self.wide // 2
 
         def order(a, pick):
             return dot(a, pick).astype(bf16)
 
-        def emit(name, lhs, rhs):
+        def begin(name, lhs, rhs):
             if name == "down":
                 last = lhs[:, 2 * self.wide :]
                 both = jnp.concatenate([order(last, left), order(last, right)], axis=0)
                 sides = jnp.concatenate([rhs[:, :half], rhs[:, half:]], axis=0)
                 terms = [
-                    (order(lhs[:, : self.wide], whole), rhs),
-                    (order(lhs[:, self.wide : 2 * self.wide], whole), rhs),
+                    (lhs[:, : self.wide], rhs),
+                    (lhs[:, self.wide : 2 * self.wide], rhs),
                     (both, sides),
                 ]
-                sums[name] = self.reduced(terms)
-            elif name == "gate_up":
-                sums[name] = self.reduced([(order(lhs, whole), rhs)])
-            else:
-                normed, attended = lhs
-                grad_qkv, middle_low, gain_one, gain_two = rhs
-                gains = dot_tn(whole, jnp.stack([gain_one, gain_two], axis=1).astype(bf16))
-                spare = jnp.zeros((self.wide, self.cols_qkv - self.wide_qkv - 2), f32)
-                sums[name] = self.reduced(
-                    [(order(attended, whole), middle_low), (order(normed, whole), grad_qkv)],
-                    jnp.concatenate([gains, spare], axis=1),
-                )
-
-        return emit, sums
+                return self.reduced(terms)
+            if name == "gate_up":
+                return self.reduced([(lhs, rhs)])
+            normed, attended = lhs
+            grad_qkv, middle_low, gain_one, gain_two = rhs
+            gains = dot_tn(whole, jnp.stack([gain_one, gain_two], axis=1).astype(bf16))
+            spare = jnp.zeros((self.wide, self.cols_qkv - self.wide_qkv - 2), f32)
+            return self.reduced(
+                [(attended, middle_low), (normed, grad_qkv)],
+                jnp.concatenate([gains, spare], axis=1),
+            )
+
+        return begin
 
     def shares(self, sums):
         result = []
@@ -366,49 +533,60 @@
         self.first = lax.axis_index("section") == 0
         self.spread = one_hot(features, jnp.arange(features, dtype=jnp.int32))
 
-    def gathered(self, weights):
+    def sources(self, weights):
         names = ("gain_one", "query", "key", "value", "out", "gain_two", "gate", "up", "down")
         both = [lax.all_gather(part, ("section", "fsdp"), axis=0, tiled=True) for part in weights]
+
+        def same(a):
+            return a
+
         layers = []
         for layer in range(2):
             w = {name: a.reshape((2, -1) + a.shape[1:])[layer] for name, a in zip(names, both)}
             w["qkv"] = jnp.concatenate([w["query"], w["key"], w["value"]], axis=1)
             w["gain_one"] = w["gain_one"].astype(f32)
             w["gain_two"] = w["gain_two"].astype(f32)
-            layers.append(w)
+            w["spread"] = self.spread
+            for name in ("order", "order_hidden", "relative", "relative_hidden", "back", "back_hidden"):
+                w[name] = same
+            layers.append(Arriving({}, None))
+            layers[-1].tie = lambda value, name: value
+            layers[-1].weights = lambda name, w=w: w
         return layers
 
     def emitter(self):
-        sums = {}
-
         def reduced(a):
             part = lax.psum_scatter(a, "fsdp", scatter_dimension=0, tiled=True)
             return lax.psum(part, "section")
 
-        def emit(name, lhs, rhs):
+        def begin(name, lhs, rhs):
             if name == "attention":
                 normed, attended = lhs
                 grad_qkv, middle_low, gain_one, gain_two = rhs
-                sums["out"] = reduced(dot_tn(attended, middle_low))
-                sums["qkv"] = reduced(dot_tn(normed, grad_qkv))
-                sums["gain_one"] = reduced(gain_one)
-                sums["gain_two"] = reduced(gain_two)
-            else:
-                sums[name] = reduced(dot_tn(lhs, rhs))
-
-        return emit, sums
+                yield ()
+                return (
+                    reduced(dot_tn(attended, middle_low)),
+                    reduced(dot_tn(normed, grad_qkv)),
+                    reduced(gain_one),
+                    reduced(gain_two),
+                )
+            yield ()
+            return reduced(dot_tn(lhs, rhs))
+
+        return begin
 
     def shares(self, sums):
-        own = {name: jnp.where(self.first, sums[0][name], sums[1][name]) for name in sums[0]}
+        own = jax.tree.map(lambda a, b: jnp.where(self.first, a, b), sums[0], sums[1])
+        out, qkv, gain_one, gain_two = own["attention"]
         wide, narrow = HEADS * HD, KV * HD
         hidden = own["gate_up"].shape[1] // 2
         return (
-            own["gain_one"],
-            own["qkv"][:, :wide],
-            own["qkv"][:, wide : wide + narrow],
-            own["qkv"][:, wide + narrow :],
-            own["out"],
-            own["gain_two"],
+            gain_one,
+            qkv[:, :wide],
+            qkv[:, wide : wide + narrow],
+            qkv[:, wide + narrow :],
+            out,
+            gain_two,
             own["gate_up"][:, :hidden],
             own["gate_up"][:, hidden:],
             own["down"],
@@ -423,7 +601,7 @@
     plan = (Halves if fits else Plain)(n, features, hidden)
     section = lax.axis_index("section")
     first = section == 0
-    layers = plan.gathered([weight[0] for weight in weights])
+    source_zero, source_one = plan.sources([weight[0] for weight in weights])
     spread = plan.spread
 
     def mine(array):
@@ -436,14 +614,14 @@
     tables = rope_tables(mine(positions))
 
     start = dot(mine(inputs), spread)
-    middle, kept_zero = forward(start, layers[0], allowed, tables, spread, features)
-    end, kept_one = forward(middle, layers[1], allowed, tables, spread, features)
+    middle, weights_zero, kept_zero = forward(start, source_zero, allowed, tables, features)
+    end, weights_one, kept_one = forward(middle, source_one, allowed, tables, features)
 
     grad = split_dot(mine(cotangent), spread)
-    emit_one, sums_one = plan.emitter()
-    grad_middle = backward(middle, layers[1], tables, spread, features, kept_one, grad, emit_one)
-    emit_zero, sums_zero = plan.emitter()
-    grad_start = backward(start, layers[0], tables, spread, features, kept_zero, grad_middle, emit_zero)
+    flow = Flow(plan.emitter())
+    grad_middle = backward(middle, weights_one, tables, features, kept_one, grad, flow)
+    grad_start = backward(start, weights_zero, tables, features, kept_zero, grad_middle, flow)
+    sums_one, sums_zero = flow.finished()
 
     def exchanged(zero, one):
         keep = jnp.where(first, zero, one)

time: 835 us -> 756 us (0.905)
  waiting for transfers between devices: 370 us -> 281 us
  starting transfers between devices: 19.1 us -> 53 us
  matrix products: 255 us -> 240 us
  local copies, waits for them, and re-layouts: 83.8 us -> 74.6 us
    all_gather x2 -> x1, waiting for transfers between devices: 225 us -> 0.01 us  [one_gather(): return lax.all_gather(sent, ('fsdp', 'section'), axis=0, tiled=True)]
    ppermute x12 -> x27, waiting for transfers between devices: 108 us -> 224 us  [the longest x6 61.3 us: reduced(): lax.ppermute(mine[half // 2:], ('section', 'fsdp'), first_route)]
    ppermute x12 -> x27, starting transfers between devices: 15.1 us -> 46.8 us  [the longest x9 29.8 us: travelled(): lax.ppermute(part, 'fsdp', [(i, (i + 4 * k) % self.n) for i in range(self...]
    sub x0 -> x2, matrix products: none -> 23.6 us  [backward(): grad_probs - jnp.sum(probs * grad_probs, axis=-1, keepdims=True)]
    concatenate x1 -> x13, other arithmetic: 1.11 us -> 19.1 us  [the longest x3 8.33 us: travelled(): return jnp.concatenate([mine, got], axis=0)]
    dot_general x26, matrix products: 58.8 us -> 41 us  [dot_tn(): lax.dot_general(a, b, (((0,), (0,)), ((), ())), preferred_element_type=f32)]
    convert_element_type x4 -> x2, other arithmetic: 20 us -> 2.61 us  [the longest x1 2.41 us: backward(): up_low = (grad_hidden * silu).astype(bf16)]
    dot_general x2 -> x0, matrix products: 16.7 us -> none  [backward(): jnp.einsum('qkgd,pkd->kgqp', grad_att, values, preferred_element_type=f32)]
  transfers between devices with their start and end apart: 32 -> 51, of which waited for: 13 -> 23; matrix products, arithmetic and copies ran while one was open for 20% -> 36% of each run, Pallas kernels for 0% -> 0%
where the time goes in v2:
time: 756 us; the launch traced here: 747 us
  waiting for transfers between devices  281 us (37%)
  matrix products  240 us (32%)
  other arithmetic  81 us (11%)
  local copies, waits for them, and re-layouts  74.6 us (10%)
  starting transfers between devices  53 us (7%)
  between operations  17.7 us (2%)
    dot_general x34, matrix products, dot(): return jnp.dot(a, b, preferred_element_type=f32)  67.6 us
    dot_general x25, matrix products, dot_nt(): lax.dot_general(a, b, (((1,), (1,)), ((), ())), preferred_element_type=f32)  67.4 us
    ppermute x6, waiting for transfers between devices, reduced(): lax.ppermute(mine[half // 2:], ('section', 'fsdp'), first_route)  61.3 us
    ppermute x9, waiting for transfers between devices, travelled(): lax.ppermute(part, 'fsdp', [(i, (i + 4 * k) % self.n) for i in range(self...  60.8 us
    ppermute x3, waiting for transfers between devices, travelled(): got = (yield lax.ppermute(pair, ('section', 'fsdp'), first_route))  49.4 us
    reduce_scatter x6, waiting for transfers between devices, reduced(): lax.psum_scatter(mine, 'fsdp', scatter_dimension=0, tiled=True, axis_inde...  42.4 us
    dot_general x26, matrix products, dot_tn(): lax.dot_general(a, b, (((0,), (0,)), ((), ())), preferred_element_type=f32)  41 us
    unnamed x362, local copies, waits for them, and re-layouts  39.1 us
  transfers between devices with their start and end apart: 51, of which 23 were waited for; matrix products, arithmetic and copies ran while one was open for 36% of the time, Pallas kernels for 0%

profile of v2, /device:TPU:0, one launch (start us, length us, event | category | flops | bytes accessed | tf_op | source)
XLA Modules:
  0.0 747.4 jit_solution(13624388661131496212)
XLA Ops:
  59.8 13.5 %collective-permute-done.2 = bf16[32,2688]{1,0:T(8,128)(2,1)S(1)} collective-permute-done((bf16[32,2688]{1,0:T(8,128)(2,1)S(1)}, bf16[32,2688]{1,0:T(8,128)(2,1)S(1)}, u32[]{:S(2)}, u32[]{:S(2)}) %collective-permute-start.2) | collective-permute-done | bytes 172064 | tf_op jit(solution)/shard_map/ppermute | solution.py:376
  73.3 8.4 %collective-permute-start.7 = (bf16[32,5120]{1,0:T(8,128)(2,1)}, bf16[32,5120]{1,0:T(8,128)(2,1)S(1)}, u32[]{:S(2)}, u32[]{:S(2)}) collective-permute-start(bf16[32,5120]{1,0:T(8,128)(2,1)} %get-tuple-element.222), channel_id=1, source_target_pairs={{0,12},{1,13},{2,14},{3,15},{4,0},{5,1},{6,2},{7,3},{8,4},{9,5},{1... | collective-permute-start | bytes 983048 | tf_op jit(solution)/shard_map/ppermute | solution.py:376
  81.9 11.4 %collective-permute-done.5 = bf16[32,5120]{1,0:T(8,128)(2,1)S(1)} collective-permute-done((bf16[32,5120]{1,0:T(8,128)(2,1)}, bf16[32,5120]{1,0:T(8,128)(2,1)S(1)}, u32[]{:S(2)}, u32[]{:S(2)}) %collective-permute-start.5) | collective-permute-done | bytes 327712 | tf_op jit(solution)/shard_map/ppermute | solution.py:376
  93.3 11.8 %collective-permute-start.12 = (bf16[32,2560]{1,0:T(8,128)(2,1)S(1)}, bf16[32,2560]{1,0:T(8,128)(2,1)S(1)}, u32[]{:S(2)}, u32[]{:S(2)}) collective-permute-start(bf16[32,2560]{1,0:T(8,128)(2,1)S(1)} %copy-done.91), channel_id=1, source_target_pairs={{0,12},{1,13},{2,14},{3,15},{4,0},{5,1},{6,2},{7,3},{8,4},{9,5},{1... | collective-permute-start | bytes 491528 | tf_op jit(solution)/shard_map/ppermute | solution.py:376
  105.1 19.0 %collective-permute-done.6 = bf16[32,5120]{1,0:T(8,128)(2,1)S(1)} collective-permute-done((bf16[32,5120]{1,0:T(8,128)(2,1)}, bf16[32,5120]{1,0:T(8,128)(2,1)S(1)}, u32[]{:S(2)}, u32[]{:S(2)}) %collective-permute-start.6) | collective-permute-done | bytes 327712 | tf_op jit(solution)/shard_map/ppermute | solution.py:376
  125.6 9.6 %collective-permute-done.7 = bf16[32,5120]{1,0:T(8,128)(2,1)S(1)} collective-permute-done((bf16[32,5120]{1,0:T(8,128)(2,1)}, bf16[32,5120]{1,0:T(8,128)(2,1)S(1)}, u32[]{:S(2)}, u32[]{:S(2)}) %collective-permute-start.7) | collective-permute-done | bytes 327712 | tf_op jit(solution)/shard_map/ppermute | solution.py:376
  139.7 5.8 collective-permute-done.12
  145.5 32.3 %collective-permute-done.13 = bf16[256,2688]{1,0:T(8,128)(2,1)S(1)} collective-permute-done((bf16[256,2688]{1,0:T(8,128)(2,1)S(1)}, bf16[256,2688]{1,0:T(8,128)(2,1)S(1)}, u32[]{:S(2)}, u32[]{:S(2)}) %collective-permute-start.13) | collective-permute-done | bytes 1376288 | tf_op jit(solution)/shard_map/ppermute | solution.py:386
  189.3 19.4 %collective-permute-done.16 = bf16[128,2560]{1,0:T(8,128)(2,1)S(1)} collective-permute-done((bf16[128,2560]{1,0:T(8,128)(2,1)S(1)}, bf16[128,2560]{1,0:T(8,128)(2,1)S(1)}, u32[]{:S(2)}, u32[]{:S(2)}) %collective-permute-start.16) | collective-permute-done | bytes 655392 | tf_op jit(solution)/shard_map/ppermute | solution.py:384
  211.4 7.7 %fusion.399 = (f32[5,3,384]{2,1,0:T(4,128)S(1)}, f32[5,3,384,384]{2,3,1,0:T(8,128)}) fusion(pred[384,384]{0,1:T(8,128)(4,1)} %fusion.253, bf16[384,5,3,32]{0,3,2,1:T(8,128)(2,1)} %bitcast.335, bf16[384,5,3,32]{0,3,2,1:T(8,128)(2,1)} %bitcast.333, bf16[384,5,32]{0,2,1:T(8,128)(2,1)} %get-tuple-element.236, bf16[384,5,32]{0,2,1:T(8,128)(2,1)} %get-tuple-element.235), kind=kOutput, calls=%fused_computation.645 | convolution fusion | flops 293929344 | bytes 10000896 | tf_op jit(solution)/shard_map/sub | solution.py:84
  219.1 4.7 fusion.175
  224.9 17.1 %collective-permute-done.17 = bf16[256,5120]{1,0:T(8,128)(2,1)} collective-permute-done((bf16[256,5120]{1,0:T(8,128)(2,1)}, bf16[256,5120]{1,0:T(8,128)(2,1)}, u32[]{:S(2)}, u32[]{:S(2)}) %collective-permute-start.17) | collective-permute-done | bytes 2621472 | tf_op jit(solution)/shard_map/ppermute | solution.py:386
  242.0 4.6 pad_maximum_fusion.2
  249.6 8.9 %collective-permute-done.18 = bf16[512,5120]{1,0:T(8,128)(2,1)S(1)} collective-permute-done((bf16[512,5120]{1,0:T(8,128)(2,1)}, bf16[512,5120]{1,0:T(8,128)(2,1)S(1)}, u32[]{:S(2)}, u32[]{:S(2)}) %collective-permute-start.18) | collective-permute-done | bytes 5242912 | tf_op jit(solution)/shard_map/ppermute | solution.py:261
  260.5 4.4 pad_maximum_fusion
  268.8 4.1 multiply_convert_fusion.5
  278.7 3.7 fusion.401
  298.5 3.9 fusion.76
  305.8 7.5 fusion.400
  313.2 4.4 fusion.178
  324.4 3.6 fusion.388
  330.6 4.7 fusion.16
  335.3 6.0 multiply_convert_fusion.2
  370.8 4.7 fusion.14
  375.6 5.1 multiply_reduce_fusion.4
  381.2 4.9 collective-permute-done.24
  387.2 4.5 fusion.181
  391.7 11.9 %fusion.7 = bf16[5,3,384,384]{2,3,1,0:T(8,128)(2,1)} fusion(bf16[384,5,64,1]{0,2,3,1:T(8,128)(2,1)S(1)} %bitcast.356, bf16[384,5,3,64]{0,3,2,1:T(8,128)(2,1)} %bitcast.369, f32[5,3,384,384]{2,3,1,0:T(8,128)} %get-tuple-element.273, f32[5,3,384]{2,1,0:T(4,128)S(1)} %copy-done.155), kind=kOutput, calls=%fused_computation.14 | convolution fusion | flops 579508224 | bytes 14277120 | tf_op jit(solution)/shard_map/sub | solution.py:138
  406.7 4.9 add_convert_fusion.1
  412.8 5.6 fusion.202
  422.6 21.0 %collective-permute-done.26 = bf16[256,5120]{1,0:T(8,128)(2,1)S(1)} collective-permute-done((bf16[256,5120]{1,0:T(8,128)(2,1)S(1)}, bf16[256,5120]{1,0:T(8,128)(2,1)S(1)}, u32[]{:S(2)}, u32[]{:S(2)}) %collective-permute-start.26) | collective-permute-done | bytes 2621472 | tf_op jit(solution)/shard_map/ppermute | solution.py:455
  443.6 3.9 multiply_reduce_fusion.5
  464.6 8.1 %convolution_convert_fusion.2 = bf16[384,2560]{1,0:T(8,128)(2,1)} fusion(bf16[384,1024]{1,0:T(8,128)(2,1)S(1)} %convert_element_type.501, bf16[512,1024]{1,0:T(8,128)(2,1)S(1)} %bitcast.346, bf16[1024,1024]{1,0:T(8,128)(2,1)S(1)} %copy-done.57, bf16[1024,1024]{1,0:T(8,128)(2,1)S(1)} %copy-done.55), kind=kOutput, calls=%fused_computation.62 | convolution fusion | flops 2029977600 | bytes 7995392 | tf_op jit(solution)/shard_map/dot_general | solution.py:26
  481.3 3.7 collective-permute-done.29
  487.1 4.6 convolution_convert_fusion
  502.4 5.0 fusion.22
  515.6 9.0 %collective-permute-done.33 = bf16[128,2688]{0,1:T(8,128)(2,1)S(1)} collective-permute-done((bf16[128,2688]{0,1:T(8,128)(2,1)S(1)}, bf16[128,2688]{0,1:T(8,128)(2,1)S(1)}, u32[]{:S(2)}, u32[]{:S(2)}) %collective-permute-start.33) | collective-permute-done | bytes 688160 | tf_op jit(solution)/shard_map/ppermute | solution.py:457
  526.5 5.1 convolution_convert_fusion.13
  536.3 11.7 %fusion.5 = bf16[5,3,384,384]{2,3,1,0:T(8,128)(2,1)} fusion(bf16[384,5,64,1]{0,2,3,1:T(8,128)(2,1)S(1)} %bitcast.354, bf16[384,5,3,64]{0,3,2,1:T(8,128)(2,1)} %bitcast.367, f32[5,3,384,384]{2,3,1,0:T(8,128)} %get-tuple-element.269, f32[5,3,384]{2,1,0:T(4,128)S(1)} %copy-done.153), kind=kOutput, calls=%fused_computation.10 | convolution fusion | flops 579508224 | bytes 14277120 | tf_op jit(solution)/shard_map/sub | solution.py:138
  553.6 6.7 add_convert_fusion
  561.5 5.6 fusion.205
  571.2 21.0 %collective-permute-done.35 = bf16[256,5120]{1,0:T(8,128)(2,1)S(1)} collective-permute-done((bf16[256,5120]{1,0:T(8,128)(2,1)S(1)}, bf16[256,5120]{1,0:T(8,128)(2,1)S(1)}, u32[]{:S(2)}, u32[]{:S(2)}) %collective-permute-start.35) | collective-permute-done | bytes 2621472 | tf_op jit(solution)/shard_map/ppermute | solution.py:455
  594.7 16.3 %collective-permute-done.41 = bf16[128,5120]{1,0:T(8,128)(2,1)S(1)} collective-permute-done((bf16[128,5120]{1,0:T(8,128)(2,1)S(1)}, bf16[128,5120]{1,0:T(8,128)(2,1)S(1)}, u32[]{:S(2)}, u32[]{:S(2)}) %collective-permute-start.41) | collective-permute-done | bytes 1310752 | tf_op jit(solution)/shard_map/ppermute | solution.py:457
  612.7 5.9 select_convert_fusion.1
  631.2 4.1 fusion.78
  661.9 10.6 %collective-permute-done.38 = bf16[256,2688]{0,1:T(8,128)(2,1)S(1)} collective-permute-done((bf16[256,2688]{0,1:T(8,128)(2,1)S(1)}, bf16[256,2688]{0,1:T(8,128)(2,1)S(1)}, u32[]{:S(2)}, u32[]{:S(2)}) %collective-permute-start.38) | collective-permute-done | bytes 1376288 | tf_op jit(solution)/shard_map/ppermute | solution.py:455
  676.1 7.9 %collective-permute-done.39 = bf16[128,2688]{0,1:T(8,128)(2,1)S(1)} collective-permute-done((bf16[128,2688]{0,1:T(8,128)(2,1)S(1)}, bf16[128,2688]{0,1:T(8,128)(2,1)S(1)}, u32[]{:S(2)}, u32[]{:S(2)}) %collective-permute-start.39) | collective-permute-done | bytes 688160 | tf_op jit(solution)/shard_map/ppermute | solution.py:457
  689.0 40.7 %reduce-scatter.19.cloned.1.call-done = bf16[32,2688]{1,0:T(8,128)(2,1)} async-done(((bf16[128,2688]{1,0:T(8,128)(2,1)}), bf16[32,2688]{1,0:T(8,128)(2,1)}) %reduce-scatter.19.cloned.1.call-update) | async-done | bytes 172048 | tf_op jit(solution)/shard_map/reduce_scatter | solution.py:460
  (709 shorter events, 280.6 us)
Async XLA Ops:
  7.2 289.7 %all-gather.2.cloned.1.call-start = ((), (), s32[]{:S(2)}) async-start(), calls=%async_computation.6 | async-start | bytes 21897216 | tf_op jit(solution)/shard_map/all_gather | solution.py:358
  16.0 22.3 %collective-permute-start = (bf16[32,2688]{1,0:T(8,128)(2,1)}, bf16[32,2688]{1,0:T(8,128)(2,1)}, u32[]{:S(2)}, u32[]{:S(2)}) collective-permute-start(bf16[32,2688]{1,0:T(8,128)(2,1)} %select_bitcast_fusion.9), channel_id=1, source_target_pairs={{0,16},{16,0},{1,17},{17,1},{2,18},{18,2},{3,19},{19,3},{4,20},{20... | collective-permute-start | bytes 516104 | tf_op jit(solution)/shard_map/ppermute | solution.py:261
  18.1 18.6 %collective-permute-start.9 = (bf16[32,2560]{1,0:T(8,128)(2,1)}, bf16[32,2560]{1,0:T(8,128)(2,1)}, u32[]{:S(2)}, u32[]{:S(2)}) collective-permute-start(bf16[32,2560]{1,0:T(8,128)(2,1)} %select_bitcast_fusion.12), channel_id=1, source_target_pairs={{0,16},{16,0},{1,17},{17,1},{2,18},{18,2},{3,19},{19,3},{4,20},{20... | collective-permute-start | bytes 491528 | tf_op jit(solution)/shard_map/ppermute | solution.py:261
  41.2 602.0 %reduce-scatter.17.cloned.1.call-start = ((), (), s32[]{:S(2)}) async-start(), calls=%async_computation.10 | async-start | bytes 819200 | tf_op jit(solution)/shard_map/reduce_scatter | solution.py:460
  47.7 10.0 %collective-permute-start.1 = (bf16[32,2688]{1,0:T(8,128)(2,1)S(1)}, bf16[32,2688]{1,0:T(8,128)(2,1)S(1)}, u32[]{:S(2)}, u32[]{:S(2)}) collective-permute-start(bf16[32,2688]{1,0:T(8,128)(2,1)S(1)} %get-tuple-element.240), channel_id=1, source_target_pairs={{0,4},{1,5},{2,6},{3,7},{4,8},{5,9},{6,10},{7,11},{8,12},{9,13},{1... | collective-permute-start | bytes 516104 | tf_op jit(solution)/shard_map/ppermute | solution.py:376
  50.3 22.9 %collective-permute-start.2 = (bf16[32,2688]{1,0:T(8,128)(2,1)S(1)}, bf16[32,2688]{1,0:T(8,128)(2,1)S(1)}, u32[]{:S(2)}, u32[]{:S(2)}) collective-permute-start(bf16[32,2688]{1,0:T(8,128)(2,1)S(1)} %get-tuple-element.240), channel_id=1, source_target_pairs={{0,8},{1,9},{2,10},{3,11},{4,12},{5,13},{6,14},{7,15},{8,0},{9,1},... | collective-permute-start | bytes 516104 | tf_op jit(solution)/shard_map/ppermute | solution.py:376
  52.9 20.4 %collective-permute-start.3 = (bf16[32,2688]{1,0:T(8,128)(2,1)S(1)}, bf16[32,2688]{1,0:T(8,128)(2,1)S(1)}, u32[]{:S(2)}, u32[]{:S(2)}) collective-permute-start(bf16[32,2688]{1,0:T(8,128)(2,1)S(1)} %get-tuple-element.240), channel_id=1, source_target_pairs={{0,12},{1,13},{2,14},{3,15},{4,0},{5,1},{6,2},{7,3},{8,4},{9,5},{1... | collective-permute-start | bytes 516104 | tf_op jit(solution)/shard_map/ppermute | solution.py:376
  55.1 84.5 %collective-permute-start.10 = (bf16[32,2560]{1,0:T(8,128)(2,1)S(1)}, bf16[32,2560]{1,0:T(8,128)(2,1)S(1)}, u32[]{:S(2)}, u32[]{:S(2)}) collective-permute-start(bf16[32,2560]{1,0:T(8,128)(2,1)S(1)} %copy-done.91), channel_id=1, source_target_pairs={{0,4},{1,5},{2,6},{3,7},{4,8},{5,9},{6,10},{7,11},{8,12},{9,13},{1... | collective-permute-start | bytes 491528 | tf_op jit(solution)/shard_map/ppermute | solution.py:376
  55.8 83.9 %collective-permute-start.11 = (bf16[32,2560]{1,0:T(8,128)(2,1)S(1)}, bf16[32,2560]{1,0:T(8,128)(2,1)S(1)}, u32[]{:S(2)}, u32[]{:S(2)}) collective-permute-start(bf16[32,2560]{1,0:T(8,128)(2,1)S(1)} %copy-done.91), channel_id=1, source_target_pairs={{0,8},{1,9},{2,10},{3,11},{4,12},{5,13},{6,14},{7,15},{8,0},{9,1},... | collective-permute-start | bytes 491528 | tf_op jit(solution)/shard_map/ppermute | solution.py:376
  57.7 35.5 %collective-permute-start.5 = (bf16[32,5120]{1,0:T(8,128)(2,1)}, bf16[32,5120]{1,0:T(8,128)(2,1)S(1)}, u32[]{:S(2)}, u32[]{:S(2)}) collective-permute-start(bf16[32,5120]{1,0:T(8,128)(2,1)} %get-tuple-element.222), channel_id=1, source_target_pairs={{0,4},{1,5},{2,6},{3,7},{4,8},{5,9},{6,10},{7,11},{8,12},{9,13},{1... | collective-permute-start | bytes 983048 | tf_op jit(solution)/shard_map/ppermute | solution.py:376
  73.3 50.8 %collective-permute-start.6 = (bf16[32,5120]{1,0:T(8,128)(2,1)}, bf16[32,5120]{1,0:T(8,128)(2,1)S(1)}, u32[]{:S(2)}, u32[]{:S(2)}) collective-permute-start(bf16[32,5120]{1,0:T(8,128)(2,1)} %get-tuple-element.222), channel_id=1, source_target_pairs={{0,8},{1,9},{2,10},{3,11},{4,12},{5,13},{6,14},{7,15},{8,0},{9,1},... | collective-permute-start | bytes 983048 | tf_op jit(solution)/shard_map/ppermute | solution.py:376
  73.3 61.9 %collective-permute-start.7 = (bf16[32,5120]{1,0:T(8,128)(2,1)}, bf16[32,5120]{1,0:T(8,128)(2,1)S(1)}, u32[]{:S(2)}, u32[]{:S(2)}) collective-permute-start(bf16[32,5120]{1,0:T(8,128)(2,1)} %get-tuple-element.222), channel_id=1, source_target_pairs={{0,12},{1,13},{2,14},{3,15},{4,0},{5,1},{6,2},{7,3},{8,4},{9,5},{1... | collective-permute-start | bytes 983048 | tf_op jit(solution)/shard_map/ppermute | solution.py:376
  93.3 52.2 %collective-permute-start.12 = (bf16[32,2560]{1,0:T(8,128)(2,1)S(1)}, bf16[32,2560]{1,0:T(8,128)(2,1)S(1)}, u32[]{:S(2)}, u32[]{:S(2)}) collective-permute-start(bf16[32,2560]{1,0:T(8,128)(2,1)S(1)} %copy-done.91), channel_id=1, source_target_pairs={{0,12},{1,13},{2,14},{3,15},{4,0},{5,1},{6,2},{7,3},{8,4},{9,5},{1... | collective-permute-start | bytes 491528 | tf_op jit(solution)/shard_map/ppermute | solution.py:376
  124.1 12.2 %collective-permute-start.8 = (bf16[128,2688]{1,0:T(8,128)(2,1)S(1)}, bf16[128,2688]{1,0:T(8,128)(2,1)S(1)}, u32[]{:S(2)}, u32[]{:S(2)}) collective-permute-start(bf16[128,2688]{1,0:T(8,128)(2,1)S(1)} %constant_dynamic-slice_fusion.4), channel_id=1, source_target_pairs={{0,1},{1,0},{2,3},{3,2},{4,5},{5,4},{6,7},{7,6},{8,9},{9,8},{10,11... | collective-permute-start | bytes 2064392 | tf_op jit(solution)/shard_map/ppermute | solution.py:384
  136.4 41.4 %collective-permute-start.13 = (bf16[256,2688]{1,0:T(8,128)(2,1)S(1)}, bf16[256,2688]{1,0:T(8,128)(2,1)S(1)}, u32[]{:S(2)}, u32[]{:S(2)}) collective-permute-start(bf16[256,2688]{1,0:T(8,128)(2,1)S(1)} %pad_maximum_fusion.21), channel_id=1, source_target_pairs={{0,2},{1,3},{2,0},{3,1},{4,6},{5,7},{6,4},{7,5},{8,10},{9,11},{10,... | collective-permute-start | bytes 4128776 | tf_op jit(solution)/shard_map/ppermute | solution.py:386
  138.1 40.7 %collective-permute-start.14 = (bf16[128,5120]{1,0:T(8,128)(2,1)S(1)}, bf16[128,5120]{1,0:T(8,128)(2,1)S(1)}, u32[]{:S(2)}, u32[]{:S(2)}) collective-permute-start(bf16[128,5120]{1,0:T(8,128)(2,1)S(1)} %constant_dynamic-slice_fusion.3), channel_id=1, source_target_pairs={{0,1},{1,0},{2,3},{3,2},{4,5},{5,4},{6,7},{7,6},{8,9},{9,8},{10,11... | collective-permute-start | bytes 3932168 | tf_op jit(solution)/shard_map/ppermute | solution.py:384
  178.0 5.5 collective-permute-start.15
  178.2 30.4 %collective-permute-start.16 = (bf16[128,2560]{1,0:T(8,128)(2,1)S(1)}, bf16[128,2560]{1,0:T(8,128)(2,1)S(1)}, u32[]{:S(2)}, u32[]{:S(2)}) collective-permute-start(bf16[128,2560]{1,0:T(8,128)(2,1)S(1)} %constant_dynamic-slice_fusion.2), channel_id=1, source_target_pairs={{0,1},{1,0},{2,3},{3,2},{4,5},{5,4},{6,7},{7,6},{8,9},{9,8},{10,11... | collective-permute-start | bytes 1966088 | tf_op jit(solution)/shard_map/ppermute | solution.py:384
  180.7 61.2 %collective-permute-start.17 = (bf16[256,5120]{1,0:T(8,128)(2,1)}, bf16[256,5120]{1,0:T(8,128)(2,1)}, u32[]{:S(2)}, u32[]{:S(2)}) collective-permute-start(bf16[256,5120]{1,0:T(8,128)(2,1)} %pad_maximum_fusion.10), channel_id=1, source_target_pairs={{0,2},{1,3},{2,0},{3,1},{4,6},{5,7},{6,4},{7,5},{8,10},{9,11},{10,... | collective-permute-start | bytes 7864328 | tf_op jit(solution)/shard_map/ppermute | solution.py:386
  246.6 11.9 %collective-permute-start.18 = (bf16[512,5120]{1,0:T(8,128)(2,1)}, bf16[512,5120]{1,0:T(8,128)(2,1)S(1)}, u32[]{:S(2)}, u32[]{:S(2)}) collective-permute-start(bf16[512,5120]{1,0:T(8,128)(2,1)} %pad_maximum_fusion.2), channel_id=1, source_target_pairs={{0,16},{16,0},{1,17},{17,1},{2,18},{18,2},{3,19},{19,3},{4,20},{20... | collective-permute-start | bytes 15728648 | tf_op jit(solution)/shard_map/ppermute | solution.py:261
  246.7 26.1 %collective-permute-start.19 = (bf16[256,2560]{1,0:T(8,128)(2,1)S(1)}, bf16[256,2560]{1,0:T(8,128)(2,1)S(1)}, u32[]{:S(2)}, u32[]{:S(2)}) collective-permute-start(bf16[256,2560]{1,0:T(8,128)(2,1)S(1)} %pad_maximum_fusion.22), channel_id=1, source_target_pairs={{0,2},{1,3},{2,0},{3,1},{4,6},{5,7},{6,4},{7,5},{8,10},{9,11},{10,... | collective-permute-start | bytes 3932168 | tf_op jit(solution)/shard_map/ppermute | solution.py:386
  274.7 8.6 %collective-permute-start.20 = (bf16[512,2560]{1,0:T(8,128)(2,1)}, bf16[512,2560]{1,0:T(8,128)(2,1)}, u32[]{:S(2)}, u32[]{:S(2)}) collective-permute-start(bf16[512,2560]{1,0:T(8,128)(2,1)} %pad_maximum_fusion.11), channel_id=1, source_target_pairs={{0,16},{16,0},{1,17},{17,1},{2,18},{18,2},{3,19},{19,3},{4,20},{20... | collective-permute-start | bytes 7864328 | tf_op jit(solution)/shard_map/ppermute | solution.py:261
  347.5 5.0 collective-permute-start.22
  357.5 29.7 %collective-permute-start.23 = (bf16[512,5120]{1,0:T(8,128)(2,1)S(1)}, bf16[512,5120]{1,0:T(8,128)(2,1)}, u32[]{:S(2)}, u32[]{:S(2)}) collective-permute-start(bf16[512,5120]{1,0:T(8,128)(2,1)S(1)} %convolution_convert_fusion.1), channel_id=1, source_target_pairs={{0,16},{16,0},{1,17},{17,1},{2,18},{18,2},{3,19},{19,3},{4,20},{20... | collective-permute-start | bytes 15728648 | tf_op jit(solution)/shard_map/ppermute | solution.py:261
  368.4 17.7 %collective-permute-start.24 = (bf16[256,2560]{1,0:T(8,128)(2,1)S(1)}, bf16[256,2560]{1,0:T(8,128)(2,1)S(1)}, u32[]{:S(2)}, u32[]{:S(2)}) collective-permute-start(bf16[256,2560]{1,0:T(8,128)(2,1)S(1)} %slice.672), channel_id=1, source_target_pairs={{0,2},{1,3},{2,0},{3,1},{4,6},{5,7},{6,4},{7,5},{8,10},{9,11},{10,... | collective-permute-start | bytes 3932168 | tf_op jit(solution)/shard_map/ppermute | solution.py:455
  405.8 13.4 %collective-permute-start.25 = (bf16[128,2560]{1,0:T(8,128)(2,1)S(1)}, bf16[128,2560]{1,0:T(8,128)(2,1)S(1)}, u32[]{:S(2)}, u32[]{:S(2)}) collective-permute-start(bf16[128,2560]{1,0:T(8,128)(2,1)S(1)} %slice.674), channel_id=1, source_target_pairs={{0,1},{1,0},{2,3},{3,2},{4,5},{5,4},{6,7},{7,6},{8,9},{9,8},{10,11... | collective-permute-start | bytes 1966088 | tf_op jit(solution)/shard_map/ppermute | solution.py:457
  411.9 31.7 %collective-permute-start.26 = (bf16[256,5120]{1,0:T(8,128)(2,1)S(1)}, bf16[256,5120]{1,0:T(8,128)(2,1)S(1)}, u32[]{:S(2)}, u32[]{:S(2)}) collective-permute-start(bf16[256,5120]{1,0:T(8,128)(2,1)S(1)} %slice.680), channel_id=1, source_target_pairs={{0,2},{1,3},{2,0},{3,1},{4,6},{5,7},{6,4},{7,5},{8,10},{9,11},{10,... | collective-permute-start | bytes 7864328 | tf_op jit(solution)/shard_map/ppermute | solution.py:455
  449.5 6.6 collective-permute-start.27
  452.9 28.4 %collective-permute-start.30 = (bf16[128,5120]{1,0:T(8,128)(2,1)S(1)}, bf16[128,5120]{1,0:T(8,128)(2,1)S(1)}, u32[]{:S(2)}, u32[]{:S(2)}) collective-permute-start(bf16[128,5120]{1,0:T(8,128)(2,1)S(1)} %slice.696), channel_id=1, source_target_pairs={{0,1},{1,0},{2,3},{3,2},{4,5},{5,4},{6,7},{7,6},{8,9},{9,8},{10,11... | collective-permute-start | bytes 3932168 | tf_op jit(solution)/shard_map/ppermute | solution.py:457
  459.8 25.3 %collective-permute-start.28 = (bf16[512,2560]{1,0:T(8,128)(2,1)S(1)}, bf16[512,2560]{1,0:T(8,128)(2,1)S(1)}, u32[]{:S(2)}, u32[]{:S(2)}) collective-permute-start(bf16[512,2560]{1,0:T(8,128)(2,1)S(1)} %pad_maximum_fusion.13), channel_id=1, source_target_pairs={{0,16},{16,0},{1,17},{17,1},{2,18},{18,2},{3,19},{19,3},{4,20},{20... | collective-permute-start | bytes 7864328 | tf_op jit(solution)/shard_map/ppermute | solution.py:261
  463.1 22.0 %collective-permute-start.29 = (bf16[256,2688]{0,1:T(8,128)(2,1)S(1)}, bf16[256,2688]{0,1:T(8,128)(2,1)S(1)}, u32[]{:S(2)}, u32[]{:S(2)}) collective-permute-start(bf16[256,2688]{0,1:T(8,128)(2,1)S(1)} %slice.694), channel_id=1, source_target_pairs={{0,2},{1,3},{2,0},{3,1},{4,6},{5,7},{6,4},{7,5},{8,10},{9,11},{10,... | collective-permute-start | bytes 4128776 | tf_op jit(solution)/shard_map/ppermute | solution.py:455
  491.7 34.7 %collective-permute-start.31 = (bf16[512,5120]{1,0:T(8,128)(2,1)}, bf16[512,5120]{1,0:T(8,128)(2,1)}, u32[]{:S(2)}, u32[]{:S(2)}) collective-permute-start(bf16[512,5120]{1,0:T(8,128)(2,1)} %convolution_convert_fusion), channel_id=1, source_target_pairs={{0,16},{16,0},{1,17},{17,1},{2,18},{18,2},{3,19},{19,3},{4,20},{20... | collective-permute-start | bytes 15728648 | tf_op jit(solution)/shard_map/ppermute | solution.py:261
  492.9 150.3 %reduce-scatter.15.cloned.1.call-start = ((), (), s32[]{:S(2)}) async-start(), calls=%async_computation.9 | async-start | bytes 819200 | tf_op jit(solution)/shard_map/reduce_scatter | solution.py:460
  500.1 24.5 %collective-permute-start.32 = (bf16[256,2560]{1,0:T(8,128)(2,1)S(1)}, bf16[256,2560]{1,0:T(8,128)(2,1)S(1)}, u32[]{:S(2)}, u32[]{:S(2)}) collective-permute-start(bf16[256,2560]{1,0:T(8,128)(2,1)S(1)} %slice.700), channel_id=1, source_target_pairs={{0,2},{1,3},{2,0},{3,1},{4,6},{5,7},{6,4},{7,5},{8,10},{9,11},{10,... | collective-permute-start | bytes 3932168 | tf_op jit(solution)/shard_map/ppermute | solution.py:455
  511.3 13.2 %collective-permute-start.33 = (bf16[128,2688]{0,1:T(8,128)(2,1)S(1)}, bf16[128,2688]{0,1:T(8,128)(2,1)S(1)}, u32[]{:S(2)}, u32[]{:S(2)}) collective-permute-start(bf16[128,2688]{0,1:T(8,128)(2,1)S(1)} %slice.702), channel_id=1, source_target_pairs={{0,1},{1,0},{2,3},{3,2},{4,5},{5,4},{6,7},{7,6},{8,9},{9,8},{10,11... | collective-permute-start | bytes 2064392 | tf_op jit(solution)/shard_map/ppermute | solution.py:457
  535.6 12.4 %collective-permute-start.34 = (bf16[128,2560]{1,0:T(8,128)(2,1)}, bf16[128,2560]{1,0:T(8,128)(2,1)}, u32[]{:S(2)}, u32[]{:S(2)}) collective-permute-start(bf16[128,2560]{1,0:T(8,128)(2,1)} %slice.704), channel_id=1, source_target_pairs={{0,1},{1,0},{2,3},{3,2},{4,5},{5,4},{6,7},{7,6},{8,9},{9,8},{10,11... | collective-permute-start | bytes 1966088 | tf_op jit(solution)/shard_map/ppermute | solution.py:457
  550.3 124.0 %reduce-scatter.13.cloned.1.call-start = ((), (), s32[]{:S(2)}) async-start(), calls=%async_computation.8 | async-start | bytes 1638400 | tf_op jit(solution)/shard_map/reduce_scatter | solution.py:460
  553.5 120.8 %reduce-scatter.11.cloned.1.call-start = ((), (), s32[]{:S(2)}) async-start(), calls=%async_computation.7 | async-start | bytes 1638400 | tf_op jit(solution)/shard_map/reduce_scatter | solution.py:460
  560.6 31.7 %collective-permute-start.35 = (bf16[256,5120]{1,0:T(8,128)(2,1)S(1)}, bf16[256,5120]{1,0:T(8,128)(2,1)S(1)}, u32[]{:S(2)}, u32[]{:S(2)}) collective-permute-start(bf16[256,5120]{1,0:T(8,128)(2,1)S(1)} %slice.710), channel_id=1, source_target_pairs={{0,2},{1,3},{2,0},{3,1},{4,6},{5,7},{6,4},{7,5},{8,10},{9,11},{10,... | collective-permute-start | bytes 7864328 | tf_op jit(solution)/shard_map/ppermute | solution.py:455
  593.4 17.7 %collective-permute-start.41 = (bf16[128,5120]{1,0:T(8,128)(2,1)S(1)}, bf16[128,5120]{1,0:T(8,128)(2,1)S(1)}, u32[]{:S(2)}, u32[]{:S(2)}) collective-permute-start(bf16[128,5120]{1,0:T(8,128)(2,1)S(1)} %slice.726), channel_id=1, source_target_pairs={{0,1},{1,0},{2,3},{3,2},{4,5},{5,4},{6,7},{7,6},{8,9},{9,8},{10,11... | collective-permute-start | bytes 3932168 | tf_op jit(solution)/shard_map/ppermute | solution.py:457
  612.4 76.5 %reduce-scatter.21.cloned.1.call-start = ((), (), s32[]{:S(2)}) async-start(), calls=%async_computation.12 | async-start | bytes 860160 | tf_op jit(solution)/shard_map/reduce_scatter | solution.py:460
  630.9 98.8 %reduce-scatter.19.cloned.1.call-start = ((), (), s32[]{:S(2)}) async-start(), calls=%async_computation.11 | async-start | bytes 860160 | tf_op jit(solution)/shard_map/reduce_scatter | solution.py:460
  642.8 7.9 %collective-permute-start.36 = (bf16[512,2688]{0,1:T(8,128)(2,1)}, bf16[512,2688]{0,1:T(8,128)(2,1)}, u32[]{:S(2)}, u32[]{:S(2)}) collective-permute-start(bf16[512,2688]{0,1:T(8,128)(2,1)} %pad_maximum_fusion.9), channel_id=1, source_target_pairs={{0,16},{16,0},{1,17},{17,1},{2,18},{18,2},{3,19},{19,3},{4,20},{20... | collective-permute-start | bytes 8257544 | tf_op jit(solution)/shard_map/ppermute | solution.py:261
  644.2 4.0 collective-permute-start.43
  651.1 6.6 collective-permute-start.37
  654.1 18.4 %collective-permute-start.38 = (bf16[256,2688]{0,1:T(8,128)(2,1)S(1)}, bf16[256,2688]{0,1:T(8,128)(2,1)S(1)}, u32[]{:S(2)}, u32[]{:S(2)}) collective-permute-start(bf16[256,2688]{0,1:T(8,128)(2,1)S(1)} %slice.714), channel_id=1, source_target_pairs={{0,2},{1,3},{2,0},{3,1},{4,6},{5,7},{6,4},{7,5},{8,10},{9,11},{10,... | collective-permute-start | bytes 4128776 | tf_op jit(solution)/shard_map/ppermute | solution.py:455
  673.0 11.0 %collective-permute-start.39 = (bf16[128,2688]{0,1:T(8,128)(2,1)S(1)}, bf16[128,2688]{0,1:T(8,128)(2,1)S(1)}, u32[]{:S(2)}, u32[]{:S(2)}) collective-permute-start(bf16[128,2688]{0,1:T(8,128)(2,1)S(1)} %slice.716), channel_id=1, source_target_pairs={{0,1},{1,0},{2,3},{3,2},{4,5},{5,4},{6,7},{7,6},{8,9},{9,8},{10,11... | collective-permute-start | bytes 2064392 | tf_op jit(solution)/shard_map/ppermute | solution.py:457
  676.1 9.2 %collective-permute-start.42 = (bf16[32,5120]{1,0:T(8,128)(2,1)}, bf16[32,5120]{1,0:T(8,128)(2,1)}, u32[]{:S(2)}, u32[]{:S(2)}) collective-permute-start(bf16[32,5120]{1,0:T(8,128)(2,1)} %broadcast_select_fusion.5), channel_id=1, source_target_pairs={{0,16},{16,0},{1,17},{17,1},{2,18},{18,2},{3,19},{19,3},{4,20},{20... | collective-permute-start | bytes 983048 | tf_op jit(solution)/shard_map/ppermute | solution.py:261
  (168 other events, 1519.2 us)
Sparse Core Ops, SparseCore 0:
  41.3 216.8 all-gather.1
  493.0 43.8 reduce-scatter.16
  550.4 43.8 reduce-scatter.14
  596.4 30.0 reduce-scatter.12
  628.7 36.6 reduce-scatter.10
  667.6 21.3 reduce-scatter.20
  691.3 38.2 reduce-scatter.18

commit v3 on v1

v3 whole, which is shorter than its diff:
```python
import jax
import jax.numpy as jnp
from jax import lax
from jax.experimental import pallas as pl
from jax.experimental.pallas import tpu as pltpu
from jax.sharding import PartitionSpec as P

HEADS = 15
KV = 5
HD = 64
GROUP = HEADS // KV

SECTION = "section"
FSDP = "fsdp"
BOTH = (SECTION, FSDP)
QKV, OUT, GATE_UP, DOWN = range(4)

bf16 = jnp.bfloat16
f32 = jnp.float32
epsilon = 1e-05
rope_base = 100000.0


def dot(a, b):
    return jnp.dot(a, b, preferred_element_type=f32)


def dot_tn(a, b):
    return lax.dot_general(a, b, (((0,), (0,)), ((), ())), preferred_element_type=f32)


def dot_nt(a, b):
    return lax.dot_general(a, b, (((1,), (1,)), ((), ())), preferred_element_type=f32)


def one_hot(rows, targets):
    count = targets.shape[0]
    row = lax.broadcasted_iota(jnp.int32, (rows, count), 0)
    return (row == targets[None, :]).astype(bf16)


def split_dot(a, pick):
    high = a.astype(bf16)
    low = (a - high.astype(f32)).astype(bf16)
    return dot(high, pick) + dot(low, pick)


def rope_tables(places):
    half = HD // 2
    frequency = rope_base ** (-jnp.arange(half, dtype=f32) / half)
    angles = places.astype(f32)[:, None] * frequency
    cosine, sine = jnp.cos(angles), jnp.sin(angles)
    return jnp.concatenate([cosine] * 4, axis=1), jnp.concatenate([-sine, sine, -sine, sine], axis=1)


def norm_scale(v, features):
    return lax.rsqrt(jnp.sum(v * v, axis=-1, keepdims=True) / features + epsilon)


def norm_back(v, scale, gain, grad, features):
    gain_grad = jnp.sum(grad * v * scale, axis=0)
    weighted = grad * gain
    mean = jnp.sum(weighted * v, axis=-1, keepdims=True) / features
    return scale * weighted - v * (scale * scale * scale) * mean, gain_grad


ROWS = 128


def turned(block, cosine, sine):
    lane = lax.broadcasted_iota(jnp.int32, block.shape, 1)
    other = jnp.where(lane % HD < HD // 2, pltpu.roll(block, 128 - HD // 2, 1), pltpu.roll(block, HD // 2, 1))
    return block * cosine + other * sine


def fill_bias(bias, row_labels, column_labels):
    length = bias.shape[0]
    query = lax.broadcasted_iota(jnp.int32, (length, length), 0)
    key = lax.broadcasted_iota(jnp.int32, (length, length), 1)
    allowed = (row_labels[...] == column_labels[...]) & (query >= key)
    bias[...] = jnp.where(allowed, 0.0, -1e30)


def members(ref, start, rows, group):
    return jnp.concatenate(
        [ref[rows, (group * GROUP + j) * HD + start : (group * GROUP + j + 1) * HD + start] for j in range(GROUP)], axis=0
    )


def softmax(queries, keys, bias):
    scores = lax.dot_general(queries, keys, (((1,), (1,)), ((), ())), preferred_element_type=f32)
    scores = scores + jnp.concatenate([bias] * GROUP, axis=0)
    shifted = jnp.exp(scores - jnp.max(scores, axis=1, keepdims=True))
    return shifted / jnp.sum(shifted, axis=1, keepdims=True)


def attention_kernel(qkv, cosine, sine, row_labels, column_labels, attended, turned_qk, values, bias):
    length = qkv.shape[0]
    wide = HEADS * HD
    narrow = KV * HD
    fill_bias(bias, row_labels, column_labels)
    lane = lax.broadcasted_iota(jnp.int32, (length, 128), 1)
    for at in range(0, wide + narrow, 128):
        scale = jnp.where(lane + at < wide, HD ** -0.5, 1.0)
        block = turned(qkv[:, at : at + 128], cosine[...], sine[...])
        turned_qk[:, at : at + 128] = (block.astype(bf16).astype(f32) * scale).astype(bf16)
    values[...] = qkv[:, wide + narrow : wide + 2 * narrow].astype(bf16)
    for start in range(0, length, ROWS):
        rows = slice(start, start + ROWS)
        upto = slice(0, start + ROWS)
        heads = []
        for group in range(KV):
            queries = members(turned_qk, 0, rows, group)
            keys = turned_qk[upto, wide + group * HD : wide + (group + 1) * HD]
            probs = softmax(queries, keys, bias[rows, upto]).astype(bf16)
            mixed = jnp.dot(probs, values[upto, group * HD : (group + 1) * HD], preferred_element_type=f32)
            heads += [mixed[j * ROWS : (j + 1) * ROWS] for j in range(GROUP)]
        attended[rows, :] = jnp.concatenate(heads, axis=1).astype(bf16)


def attend(qkv, cosine, sine, labels):
    length = qkv.shape[0]
    wide, narrow = HEADS * HD, KV * HD
    return pl.pallas_call(
        attention_kernel,
        out_shape=[
            jax.ShapeDtypeStruct((length, wide), bf16),
            jax.ShapeDtypeStruct((length, wide + narrow), bf16),
            jax.ShapeDtypeStruct((length, narrow), bf16),
        ],
        scratch_shapes=[pltpu.VMEM((length, length), f32)],
        compiler_params=pltpu.CompilerParams(vmem_limit_bytes=32 * 2**20),
        cost_estimate=pl.CostEstimate(flops=4 * length * length * wide, bytes_accessed=length * 10000, transcendentals=length * length * HEADS),
    )(qkv, cosine, sine, labels[:, None], labels[None, :])


def attention_back_kernel(turned_qk, values, grad_att, cosine, sine, row_labels, column_labels, grad_qkv, bias, grad_q, grad_v):
    length = turned_qk.shape[0]
    wide = HEADS * HD
    narrow = KV * HD
    fill_bias(bias, row_labels, column_labels)
    contract = (((0,), (0,)), ((), ()))
    for group in range(KV):
        total_k = [None] * (length // ROWS)
        total_v = [None] * (length // ROWS)
        for start in range(0, length, ROWS):
            rows = slice(start, start + ROWS)
            upto = slice(0, start + ROWS)
            queries = members(turned_qk, 0, rows, group)
            keys = turned_qk[upto, wide + group * HD : wide + (group + 1) * HD]
            mixed = values[upto, group * HD : (group + 1) * HD]
            grads = members(grad_att, 0, rows, group)
            probs = softmax(queries, keys, bias[rows, upto])
            grad_probs = lax.dot_general(grads, mixed, (((1,), (1,)), ((), ())), preferred_element_type=f32)
            part_v = lax.dot_general(probs.astype(bf16), grads, contract, preferred_element_type=f32)
            low = (probs * (grad_probs - jnp.sum(probs * grad_probs, axis=1, keepdims=True))).astype(bf16)
            part_k = lax.dot_general(low, queries, contract, preferred_element_type=f32)
            turned_back = jnp.dot(low, keys, preferred_element_type=f32) * HD ** -0.5
            for j in range(GROUP):
                head = group * GROUP + j
                grad_q[rows, head * HD : (head + 1) * HD] = turned_back[j * ROWS : (j + 1) * ROWS]
            for piece in range(start // ROWS + 1):
                inside = slice(piece * ROWS, (piece + 1) * ROWS)
                total_k[piece] = part_k[inside] if total_k[piece] is None else total_k[piece] + part_k[inside]
                total_v[piece] = part_v[inside] if total_v[piece] is None else total_v[piece] + part_v[inside]
        for piece in range(length // ROWS):
            inside = slice(piece * ROWS, (piece + 1) * ROWS)
            grad_q[inside, wide + group * HD : wide + (group + 1) * HD] = total_k[piece]
            grad_v[inside, group * HD : (group + 1) * HD] = total_v[piece]
    for at in range(0, wide + narrow, 128):
        grad_qkv[:, at : at + 128] = turned(grad_q[:, at : at + 128], cosine[...], -sine[...]).astype(bf16)
    grad_qkv[:, wide + narrow : wide + 2 * narrow] = grad_v[...].astype(bf16)


def attend_back(turned_qk, values, grad_att, cosine, sine, labels):
    length = turned_qk.shape[0]
    wide, narrow = HEADS * HD, KV * HD
    return pl.pallas_call(
        attention_back_kernel,
        out_shape=jax.ShapeDtypeStruct((length, wide + 2 * narrow), bf16),
        scratch_shapes=[pltpu.VMEM((length, length), f32), pltpu.VMEM((length, wide + narrow), f32), pltpu.VMEM((length, narrow), f32)],
        compiler_params=pltpu.CompilerParams(vmem_limit_bytes=32 * 2**20),
        cost_estimate=pl.CostEstimate(flops=10 * length * length * wide, bytes_accessed=length * 10000, transcendentals=length * length * HEADS),
    )(turned_qk, values, grad_att, cosine, sine, labels[:, None], labels[None, :])


def forward(x, source, layer, labels, tables, features):
    turn = iter(source.order[layer])
    x = source.tie(x, next(turn))
    w = source.weights(layer)
    scale_one = norm_scale(x, features)
    normed = (x * scale_one * w.gain_one).astype(bf16)
    qkv = dot(normed, w.qkv)
    qkv = source.tie(qkv, next(turn))
    attended, turned_qk, values = attend(qkv, *tables, labels)
    attended = dot(attended, w.spread).astype(bf16)
    attended = source.tie(attended, next(turn))
    middle = x + dot(attended, w.out)
    middle = source.tie(middle, next(turn))
    w = source.weights(layer)
    scale_two = norm_scale(middle, features)
    second = (middle * scale_two * w.gain_two).astype(bf16)
    gate = dot(second, w.gate)
    up = dot(second, w.up)
    hidden = (jax.nn.silu(gate) * up).astype(bf16)
    hidden = source.tie(hidden, next(turn))
    w = source.weights(layer)
    output = middle + dot(hidden, w.down)
    return output, w, (
        scale_one, normed, turned_qk, values, attended, middle, scale_two, second, gate, up, hidden,
    )


def backward(x, w, labels, tables, features, kept, grad, flow):
    (scale_one, normed, turned_qk, values, attended, middle, scale_two, second, gate, up, hidden) = kept
    low = grad.astype(bf16)
    flow.begin(DOWN, hidden, low)
    grad_hidden = dot_nt(low, w.down)
    sig = jax.nn.sigmoid(gate)
    silu = gate * sig
    gate_low = (grad_hidden * up * (sig * (1.0 + gate * (1.0 - sig)))).astype(bf16)
    up_low = (grad_hidden * silu).astype(bf16)
    gate_low, up_low = flow.tie((gate_low, up_low), (DOWN,), (QKV, OUT))
    flow.begin(GATE_UP, second, jnp.concatenate([gate_low, up_low], axis=1))
    grad_second = dot_nt(gate_low, w.gate) + dot_nt(up_low, w.up)
    grad_norm, gain_two = norm_back(middle, scale_two, w.gain_two, grad_second, features)
    grad_middle = grad + grad_norm
    grad_middle = flow.tie(grad_middle, (GATE_UP,), (QKV, OUT))
    middle_low = grad_middle.astype(bf16)
    flow.begin(OUT, attended, middle_low)
    grad_att = dot_nt(middle_low, w.out).astype(bf16)
    grad_att = dot_nt(grad_att, w.spread).astype(bf16)
    grad_att = flow.tie(grad_att, (DOWN, OUT), ())
    grad_qkv = attend_back(turned_qk, values, grad_att, *tables, labels)
    grad_qkv = flow.tie(grad_qkv, (DOWN, GATE_UP), (DOWN, QKV))
    grad_normed = dot_nt(grad_qkv, w.qkv)
    grad_norm, gain_one = norm_back(x, scale_one, w.gain_one, grad_normed, features)
    flow.begin(QKV, normed, (grad_qkv, gain_one, gain_two))
    grad = flow.tie(grad_middle + grad_norm, (QKV, GATE_UP, OUT), (GATE_UP,))
    flow.next_layer()
    return grad


class Weights:
    def __init__(self, **fields):
        self.__dict__.update(fields)


class Arriving:
    order = (
        ((0, 1, 0, 2, 0, 1, 0, 3, 1, 2, 0), (2, 3), (4, 1), (1, 3), (4, 5, 2, 2)),
        ((4, 3, 3), (5,), (5, 4), (4,), (5, 5)),
    )

    def __init__(self, groups, unpack):
        self.groups = [(steps, next(steps)) for steps in groups]
        self.unpack = unpack

    def tie(self, value, turns):
        for index in turns:
            steps, waited = self.groups[index]
            value, got = lax.optimization_barrier((value, waited))
            try:
                self.groups[index] = (steps, steps.send(got))
            except StopIteration as end:
                self.groups[index] = (None, end.value)
        return value

    def weights(self, layer):
        return self.unpack([got for steps, got in self.groups[3 * layer : 3 * layer + 3] if steps is None])


class Flow:
    def __init__(self, begin):
        self.begun = begin
        self.now, self.before, self.done = {}, {}, []

    def begin(self, name, lhs, rhs):
        steps = self.begun(name, lhs, rhs)
        self.now[name] = (steps, next(steps))

    def tie(self, value, now, before):
        tables = [(self.now, n) for n in now] + [(self.before, n) for n in before]
        tables = [(table, n) for table, n in tables if n in table and table[n][0] is not None]
        value, waited = lax.optimization_barrier((value, [table[n][1] for table, n in tables]))
        for (table, n), got in zip(tables, waited):
            self.advance(table, n, got)
        return value

    def advance(self, table, name, got):
        steps = table[name][0]
        try:
            table[name] = (steps, steps.send(got))
        except StopIteration as end:
            table[name] = (None, end.value)

    def next_layer(self):
        self.done.append(self.before)
        self.before, self.now = self.now, {}

    def finished(self):
        last, earlier = self.before, self.done[1:]
        self.tie((), (), (QKV, OUT))
        others = [table[name] for table in earlier for name in table] + [last[DOWN]]
        waited = self.tie([got for steps, got in others], (), (QKV,))
        for table in earlier:
            for name in table:
                table[name] = (table[name][0], waited.pop(0))
        last[DOWN] = (last[DOWN][0], waited.pop(0))
        self.tie((), (), (QKV, OUT, GATE_UP))
        for table in earlier + [last]:
            while any(steps is not None for steps, _ in table.values()):
                for name in table:
                    if table[name][0] is not None:
                        self.advance(table, name, table[name][1])
        return [{name: value for name, (_, value) in table.items()} for table in earlier + [last]]


class Halves:
    def __init__(self, n, features, hidden):
        self.n, self.features, self.hidden = n, features, hidden
        self.parts = 2 * n
        self.rows = features // self.parts
        self.padded = -(-self.rows // 16) * 16
        self.wide = self.parts * self.padded
        self.down_rows = hidden // self.parts
        self.section = lax.axis_index(SECTION)
        self.first = self.section == 0
        self.place = lax.axis_index(FSDP)
        lane = jnp.arange(self.wide, dtype=jnp.int32)
        inside = lane % self.padded
        natural = jnp.where(inside < self.rows, lane // self.padded * self.rows + inside, -1)
        self.spread = one_hot(features, natural)
        self.y = self.place // 2 % 2
        self.x = self.place % 2
        z, depth = self.place // 4, n // 4
        self.relative = self.block_order(lambda m: m)
        self.arrival = self.block_order(lambda m: (z - m + depth) % depth)

    def permuted_hidden(self, array):
        rows = array.shape[0]
        blocks = array.reshape(rows, self.parts, self.down_rows)
        cut = self.padded
        return jnp.concatenate(
            [
                blocks[:, :, :cut].reshape(rows, -1),
                blocks[:, :, cut : 2 * cut].reshape(rows, -1),
                blocks[:, :, 2 * cut :].reshape(rows, -1),
            ],
            axis=1,
        )

    def natural_hidden(self, array):
        rows = array.shape[0]
        cut = self.padded
        third = self.down_rows - 2 * cut
        one = array[:, : self.wide].reshape(rows, self.parts, cut)
        two = array[:, self.wide : 2 * self.wide].reshape(rows, self.parts, cut)
        three = array[:, 2 * self.wide :].reshape(rows, self.parts, third)
        return jnp.concatenate([one, two, three], axis=2).reshape(rows, self.hidden)

    def swap(self, array):
        return lax.ppermute(array, SECTION, [(0, 1), (1, 0)])

    def packed(self, weights):
        gain_one, query, key, value, out, gain_two, gate, up, down = weights
        self.wide_qkv = query.shape[1] + key.shape[1] + value.shape[1]
        self.cols_qkv = -(-(self.wide_qkv + 2) // 128) * 128
        spare = self.cols_qkv - self.wide_qkv - 2
        rows = query.shape[0]
        half = self.wide // 2

        def halves(parts):
            both = jnp.concatenate(parts, axis=1).reshape(2, self.rows, -1)
            return jnp.pad(both, ((0, 0), (0, self.padded - self.rows), (0, 0)))

        cut = self.padded
        carried = [self.carried(halves([
            query, key, value, gain_one[:, None], gain_two[:, None], jnp.zeros((rows, spare), bf16),
            dot(out, self.spread).astype(bf16),
        ]))]
        (gate, up, down), carried = lax.optimization_barrier(((gate, up, down), carried))
        carried.append(self.carried(halves([self.permuted_hidden(gate), self.permuted_hidden(up)])))
        down = dot(down, self.spread).astype(bf16).reshape(2, self.down_rows, self.wide)
        last = down[:, 2 * cut :]
        last = jnp.concatenate([last[:, :, :half], last[:, :, half:]], axis=1)
        carried.append(self.carried(jnp.concatenate([down[:, :cut], down[:, cut : 2 * cut], last], axis=2)))
        return [zero for zero, one in carried] + [one for zero, one in carried]

    def carried(self, halves):
        keep = jnp.where(self.first, halves[0], halves[1])
        got = self.swap(jnp.where(self.first, halves[1], halves[0]))
        return jnp.where(self.first, keep, got), jnp.where(self.first, got, keep)

    def source(self, weights):
        groups = [self.travelled(part) for part in self.packed(weights)]
        self.whole, self.left, self.right = self.order_matrices()

        def unpack(groups):
            w = Weights(spread=self.spread)
            for unpacked, pieces in zip((self.attention, self.gate_up, self.down), groups):
                unpacked(w, pieces)
            return w

        return Arriving(groups, unpack)

    def assembled(self, pieces, shape, places):
        depth = self.n // 4
        part = self.padded
        count = len(places)

        def kernel(index, *refs):
            sources, out, held, came, gone = refs[: len(pieces)], *refs[len(pieces) :]
            arriving, leaving = [], []
            for number, source in enumerate(sources):
                arriving.append(pltpu.make_async_copy(source, held.at[number], came.at[number]))
                for m in range(depth):
                    block = number * depth + m
                    for place, (rows, columns, base, step, column) in enumerate(places):
                        leaving.append(
                            pltpu.make_async_copy(
                                held.at[
                                    number, pl.ds(m * part + rows[0], rows[1]), pl.ds(columns[0], columns[1])
                                ],
                                out.at[
                                    pl.ds(pl.multiple_of(base + index[block] * step, 16), rows[1]),
                                    pl.ds(column, columns[1]),
                                ],
                                gone.at[block * count + place],
                            )
                        )
            for copy in arriving:
                copy.start()
            for number, copy in enumerate(arriving):
                copy.wait()
                for sent in leaving[number * depth * count : (number + 1) * depth * count]:
                    sent.start()
            for copy in leaving:
                copy.wait()

        anywhere = pl.BlockSpec(memory_space=pl.ANY)
        return pl.pallas_call(
            kernel,
            out_shape=jax.ShapeDtypeStruct(shape, bf16),
            in_specs=[pl.BlockSpec(memory_space=pltpu.SMEM)] + [anywhere] * len(pieces),
            out_specs=anywhere,
            scratch_shapes=[
                pltpu.VMEM((len(pieces),) + pieces[0].shape, bf16),
                pltpu.SemaphoreType.DMA((len(pieces),)),
                pltpu.SemaphoreType.DMA((self.parts * count,)),
            ],
            compiler_params=pltpu.CompilerParams(vmem_limit_bytes=16 * 2**20),
            cost_estimate=pl.CostEstimate(
                flops=0, bytes_accessed=4 * shape[0] * shape[1], transcendentals=0
            ),
        )(self.arrival, *pieces)

    def side_by_side(self, pieces):
        columns = pieces[0].shape[1]
        rows = self.padded
        return self.assembled(pieces, (self.wide, columns), [((0, rows), (0, columns), 0, rows, 0)])

    def attention(self, w, pieces):
        group = self.side_by_side(pieces)
        gains = group[:, self.wide_qkv : self.wide_qkv + 2].astype(f32).T
        w.gain_one, w.gain_two = gains[0], gains[1]
        w.qkv, w.out = group[:, : self.wide_qkv], group[:, self.cols_qkv :]

    def gate_up(self, w, pieces):
        group = self.side_by_side(pieces)
        w.gate, w.up = group[:, : self.hidden], group[:, self.hidden :]

    def down(self, w, pieces):
        wide, cut = self.wide, self.padded
        short, half = cut // 2, wide // 2
        w.down = self.assembled(
            pieces,
            (self.hidden, wide),
            [
                ((0, cut), (0, wide), 0, cut, 0),
                ((0, cut), (wide, wide), wide, cut, 0),
                ((0, short), (2 * wide, half), 2 * wide, short, 0),
                ((short, short), (2 * wide, half), 2 * wide, short, half),
            ],
        )

    def travelled(self, part):
        depth = self.n // 4
        part = yield part
        got = yield [
            lax.ppermute(part, FSDP, [(i, (i + 4 * k) % self.n) for i in range(self.n)])
            for k in range(1, depth)
        ]
        line = jnp.concatenate([part] + list(got), axis=0)
        first_route, second_route = self.routes()
        far = lax.ppermute(line, BOTH, first_route)
        across = [self.swap(line)]
        got = yield lax.ppermute(line, BOTH, second_route)
        across.append(self.swap(got))
        mine = [line, got]
        got = yield [far, lax.ppermute(got, BOTH, first_route)]
        across += [self.swap(one) for one in got]
        mine += got
        across = yield across
        return mine + across

    def block_order(self, chip_z):
        depth = self.n // 4
        block = jnp.arange(self.parts, dtype=jnp.int32)
        quarter = block // depth % 4
        core = self.section ^ (block // self.n)
        low, high = quarter % 2, quarter // 2
        other_x = jnp.where(core == 0, low, high)
        other_y = jnp.where(core == 0, high, low)
        chip = chip_z(block % depth) * 4 + (self.y ^ other_y) * 2 + (self.x ^ other_x)
        return chip * 2 + core

    def order_matrices(self):
        lane = jnp.arange(self.wide, dtype=jnp.int32)
        part = jnp.repeat(self.relative, self.padded)
        inside = lane % self.padded
        half = self.padded // 2
        block = part * half
        return (
            one_hot(self.wide, part * self.padded + inside),
            one_hot(self.wide // 2, jnp.where(inside < half, block + inside, -1)),
            one_hot(self.wide // 2, jnp.where(inside >= half, block + inside - half, -1)),
        )

    def routes(self):
        count = self.n

        def route(flips):
            return [
                (core * count + i, core * count + (i ^ flip))
                for core, flip in enumerate(flips)
                for i in range(count)
            ]

        return route((2, 1)), route((1, 2))

    def reduced(self, terms, direct=False):
        half = self.wide // 2

        def product(lo, hi):
            return jnp.concatenate([dot_tn(a[:, lo:hi], b) for a, b in terms], axis=1)

        first_route, second_route = self.routes()
        got = yield self.swap(product(half, self.wide).astype(bf16))
        mine = (product(0, half) + got.astype(f32)).astype(bf16)
        got = yield lax.ppermute(mine[half // 2 :], BOTH, first_route)
        mine = (mine[: half // 2].astype(f32) + got.astype(f32)).astype(bf16)
        got = yield lax.ppermute(mine[half // 4 :], BOTH, second_route)
        mine = (mine[: half // 4].astype(f32) + got.astype(f32)).astype(bf16)
        depth, part = self.n // 4, self.padded
        if direct:
            blocks = [
                lax.dynamic_slice_in_dim(mine, (self.place // 4 + k) % depth * part, part, 0)
                for k in range(depth)
            ]
            got = yield [
                lax.ppermute(blocks[k], FSDP, [(i, (i + 4 * k) % self.n) for i in range(self.n)])
                for k in range(1, depth)
            ]
            return sum((one.astype(f32) for one in got), blocks[0].astype(f32)).astype(bf16)
        lines = [[q + 4 * z for z in range(depth)] for q in range(4)]
        got = yield lax.psum_scatter(mine, FSDP, scatter_dimension=0, tiled=True, axis_index_groups=lines)
        return got

    def emitter(self):
        whole, half = self.whole, self.wide // 2

        def order(a):
            return dot(a, whole).astype(bf16)

        def begin(name, lhs, rhs):
            if name == DOWN:
                last = lhs[:, 2 * self.wide :]
                both = jnp.concatenate(
                    [dot(last, self.left).astype(bf16), dot(last, self.right).astype(bf16)], axis=0
                )
                sides = jnp.concatenate([rhs[:, :half], rhs[:, half:]], axis=0)
                terms = [
                    (order(lhs[:, : self.wide]), rhs),
                    (order(lhs[:, self.wide : 2 * self.wide]), rhs),
                    (both, sides),
                ]
                return self.reduced(terms)
            if name == GATE_UP:
                return self.reduced([(order(lhs), rhs)])
            if name == OUT:
                return self.reduced([(order(lhs), rhs)], direct=True)
            grad_qkv, gain_one, gain_two = rhs
            length = lhs.shape[0]
            gains = jnp.pad(jnp.stack([gain_one, gain_two]), ((0, 14), (0, 0))).astype(bf16)
            ones = (jnp.arange(16)[:, None] == jnp.arange(self.cols_qkv)[None, :] - self.wide_qkv).astype(bf16)
            rhs = jnp.pad(grad_qkv, ((0, 0), (0, self.cols_qkv - self.wide_qkv)))
            rhs = jnp.concatenate([rhs, ones], axis=0)
            return self.reduced([(order(jnp.concatenate([lhs, gains], axis=0)), rhs)], direct=True)

        return begin

    def shares(self, sums):
        result = []
        for name in (DOWN, GATE_UP, OUT, QKV):
            zero, one = sums[0][name], sums[1][name]
            keep = jnp.where(self.first, zero, one)
            got = self.swap(jnp.where(self.first, one, zero))
            result.append(
                jnp.stack([jnp.where(self.first, keep, got), jnp.where(self.first, got, keep)]).astype(f32)
            )
        down, gate_up, out, qkv = result
        half = self.wide // 2
        cut = self.padded
        last = down[:, :, 2 * self.wide :]
        last = jnp.concatenate([last[:, : cut // 2], last[:, cut // 2 :]], axis=2)
        down = jnp.concatenate([down[:, :, : self.wide], down[:, :, self.wide : 2 * self.wide], last], axis=1)
        down = self.natural_features(down.reshape(2 * self.down_rows, self.wide))
        gate_up = gate_up[:, : self.rows].reshape(2 * self.rows, -1)
        out = self.natural_features(out[:, : self.rows].reshape(2 * self.rows, -1))
        qkv = qkv[:, : self.rows].reshape(2 * self.rows, -1)
        wide, narrow = HEADS * HD, KV * HD
        return (
            qkv[:, self.wide_qkv],
            qkv[:, :wide],
            qkv[:, wide : wide + narrow],
            qkv[:, wide + narrow : wide + 2 * narrow],
            out,
            qkv[:, self.wide_qkv + 1],
            self.natural_hidden(gate_up[:, : self.hidden]),
            self.natural_hidden(gate_up[:, self.hidden :]),
            down,
        )

    def natural_features(self, array):
        return dot_nt(array.astype(bf16), self.spread)


class Plain:
    def __init__(self, n, features, hidden):
        self.first = lax.axis_index(SECTION) == 0
        self.spread = one_hot(features, jnp.arange(features, dtype=jnp.int32))

    def source(self, weights):
        both = [lax.all_gather(part, (SECTION, FSDP), axis=0, tiled=True) for part in weights]
        both = [a.reshape((2, -1) + a.shape[1:]) for a in both]

        def layer_of(layer):
            gain_one, query, key, value, out, gain_two, gate, up, down = [a[layer] for a in both]
            return Weights(
                gain_one=gain_one.astype(f32), gain_two=gain_two.astype(f32), out=out, gate=gate, up=up,
                down=down, qkv=jnp.concatenate([query, key, value], axis=1), spread=self.spread,
            )

        source = Arriving([], None)
        source.tie = lambda value, turns: value
        source.weights = layer_of
        return source

    def emitter(self):
        def reduced(a):
            part = lax.psum_scatter(a, FSDP, scatter_dimension=0, tiled=True)
            return lax.psum(part, SECTION)

        def begin(name, lhs, rhs):
            if name == QKV:
                grad_qkv, gain_one, gain_two = rhs
                yield ()
                return reduced(dot_tn(lhs, grad_qkv)), reduced(gain_one), reduced(gain_two)
            yield ()
            return reduced(dot_tn(lhs, rhs))

        return begin

    def shares(self, sums):
        own = jax.tree.map(lambda a, b: jnp.where(self.first, a, b), sums[0], sums[1])
        qkv, gain_one, gain_two = own[QKV]
        wide, narrow = HEADS * HD, KV * HD
        both = own[GATE_UP]
        hidden = both.shape[1] // 2
        return (
            gain_one,
            qkv[:, :wide],
            qkv[:, wide : wide + narrow],
            qkv[:, wide + narrow :],
            own[OUT],
            gain_two,
            both[:, :hidden],
            both[:, hidden:],
            own[DOWN],
        )


def on_device(inputs, cotangent, segments, positions, *weights):
    n = lax.axis_size(FSDP)
    features = inputs.shape[-1]
    hidden = weights[6].shape[-1]
    fits = n == 16 and features == 960 and hidden == 2560
    plan = (Halves if fits else Plain)(n, features, hidden)
    section = lax.axis_index(SECTION)
    first = section == 0
    source = plan.source([weight[0] for weight in weights])
    spread = plan.spread

    def mine(array):
        return lax.dynamic_index_in_dim(array, section, 0, keepdims=False)

    labels = mine(segments)
    tables = rope_tables(mine(positions))

    start = dot(mine(inputs), spread)
    middle, weights_zero, kept_zero = forward(start, source, 0, labels, tables, features)
    end, weights_one, kept_one = forward(middle, source, 1, labels, tables, features)

    grad = split_dot(mine(cotangent), spread)
    flow = Flow(plan.emitter())
    grad_middle = backward(middle, weights_one, labels, tables, features, kept_one, grad, flow)
    grad_start = backward(start, weights_zero, labels, tables, features, kept_zero, grad_middle, flow)
    sums_one, sums_zero = flow.finished()

    def exchanged(zero, one):
        keep = jnp.where(first, zero, one)
        sent = jnp.where(first, one, zero).astype(bf16)
        got = lax.ppermute(sent, SECTION, [(0, 1), (1, 0)])
        kept = keep.astype(bf16)
        rest = (keep - kept.astype(f32)).astype(bf16)
        kept = dot_nt(kept, spread) + dot_nt(rest, spread)
        got = dot_nt(got, spread)
        return jnp.stack([jnp.where(first, kept, got), jnp.where(first, got, kept)])[None]

    activations = exchanged(middle, end)
    input_grads = exchanged(grad_start, grad_middle)
    shares = plan.shares((sums_zero, sums_one))
    return (activations, input_grads) + tuple(share[None] for share in shares)


def solution(mesh):
    rows = P(SECTION, FSDP)
    matrix = P(SECTION, FSDP, None)
    weights = (rows, matrix, matrix, matrix, matrix, rows, matrix, matrix, matrix)
    tokens = P(None, FSDP, None)
    return jax.shard_map(
        on_device,
        mesh=mesh,
        in_specs=(tokens, tokens, P(None, FSDP), P(None, FSDP)) + weights,
        out_specs=(P(SECTION, None, FSDP, None), P(SECTION, None, FSDP, None)) + weights,
        check_vma=False,
    )
```

time: 835 us -> 672 us (0.80)
  waiting for transfers between devices: 370 us -> 127 us
  starting transfers between devices: 19.1 us -> 125 us
  matrix products: 255 us -> 163 us
  Pallas kernels: 0 us -> 86.4 us
  other arithmetic: 82.3 us -> 56.3 us
    all_gather x2 -> x0, waiting for transfers between devices: 225 us -> none  [gathered(): lax.all_gather(part, ('fsdp', 'section'), axis=0, tiled=True)]
    ppermute x24 -> x105, starting transfers between devices: 17.9 us -> 125 us  [the longest x18 59.8 us: travelled(): lax.ppermute(part, FSDP, [(i, (i + 4 * k) % self.n) for i in range(self.n)])]
    pallas_call x0 -> x10, Pallas kernels: none -> 86.4 us  [the longest x6 44.1 us: assembled(): pl.pallas_call(kernel, out_shape=jax.ShapeDtypeStruct(shape, bf16), in_sp...]
    dot_general x10 -> x0, matrix products: 47.3 us -> none  [the longest x2 16.7 us: backward(): jnp.einsum('qkgd,pkd->kgqp', grad_att, values, preferred_element_type=f32)]
    reduce_scatter x4, waiting for transfers between devices: 35.2 us -> 0.01 us  [reduced(): lax.psum_scatter(mine, FSDP, scatter_dimension=0, tiled=True, axis_index_...]
    convert_element_type x4 -> x7, other arithmetic: 20 us -> 2.56 us  [the longest x2 1.75 us: reduced(): sum((one.astype(f32) for one in got), blocks[0].astype(f32)).astype(bf16)]
    ppermute x24 -> x105, waiting for transfers between devices: 109 us -> 127 us  [the longest x8 40.5 us: reduced(): got = (yield lax.ppermute(mine[half // 2:], BOTH, first_route))]
    dot_general x18, matrix products: 65 us -> 49.6 us  [dot_nt(): lax.dot_general(a, b, (((1,), (1,)), ((), ())), preferred_element_type=f32)]
  transfers between devices with their start and end apart: 32 -> 109, of which waited for: 13 -> 27; matrix products, arithmetic and copies ran while one was open for 20% -> 36% of each run, Pallas kernels for 0% -> 13%
where the time goes in v3:
time: 672 us; the launch traced here: 662 us
  matrix products  163 us (24%)
  waiting for transfers between devices  127 us (19%)
  starting transfers between devices  125 us (19%)
  local copies, waits for them, and re-layouts  87 us (13%)
  Pallas kernels  86.4 us (13%)
  other arithmetic  56.3 us (8%)
  between operations  17.6 us (3%)
    dot_general x31, matrix products, dot(): return jnp.dot(a, b, preferred_element_type=f32)  64.8 us
    ppermute x18, starting transfers between devices, travelled(): lax.ppermute(part, FSDP, [(i, (i + 4 * k) % self.n) for i in range(self.n)])  59.8 us
    dot_general x18, matrix products, dot_nt(): lax.dot_general(a, b, (((1,), (1,)), ((), ())), preferred_element_type=f32)  49.6 us
    dot_general x24, matrix products, dot_tn(): lax.dot_general(a, b, (((0,), (0,)), ((), ())), preferred_element_type=f32)  48.7 us
    unnamed x464, local copies, waits for them, and re-layouts  46.8 us
    pallas_call x6, Pallas kernels, assembled(): pl.pallas_call(kernel, out_shape=jax.ShapeDtypeStruct(shape, bf16), in_sp...  44.1 us
    ppermute x8, waiting for transfers between devices, reduced(): got = (yield lax.ppermute(mine[half // 2:], BOTH, first_route))  40.5 us
    pallas_call x2, Pallas kernels, attend_back(): pl.pallas_call(attention_back_kernel, out_shape=jax.ShapeDtypeStruct((len...  24.7 us
  transfers between devices with their start and end apart: 109, of which 27 were waited for; matrix products, arithmetic and copies ran while one was open for 36% of the time, Pallas kernels for 13%

profile of v3, /device:TPU:0, one launch (start us, length us, event | category | flops | bytes accessed | tf_op | source)
XLA Modules:
  0.0 662.3 jit_solution(12617048300407589500)
XLA Ops:
  44.4 4.2 collective-permute-start.7
  53.1 5.3 collective-permute-done.7
  58.3 12.7 %collective-permute-done.8 = bf16[32,5120]{1,0:T(8,128)(2,1)S(1)} collective-permute-done((bf16[32,5120]{1,0:T(8,128)(2,1)S(1)}, bf16[32,5120]{1,0:T(8,128)(2,1)S(1)}, u32[]{:S(2)}, u32[]{:S(2)}) %collective-permute-start.8) | collective-permute-done | bytes 327712 | tf_op jit(solution)/shard_map/ppermute | solution.py:491
  78.3 7.8 %collective-permute-start.13 = (bf16[32,2560]{1,0:T(8,128)(2,1)}, bf16[32,2560]{1,0:T(8,128)(2,1)S(1)}, u32[]{:S(2)}, u32[]{:S(2)}) collective-permute-start(bf16[32,2560]{1,0:T(8,128)(2,1)} %get-tuple-element.197), channel_id=1, source_target_pairs={{0,4},{1,5},{2,6},{3,7},{4,8},{5,9},{6,10},{7,11},{8,12},{9,13},{1... | collective-permute-start | bytes 491528 | tf_op jit(solution)/shard_map/ppermute | solution.py:491
  88.7 4.8 collective-permute-done.10.refs_2_
  93.5 8.5 %collective-permute-start.15 = (bf16[32,2560]{1,0:T(8,128)(2,1)}, bf16[32,2560]{1,0:T(8,128)(2,1)S(1)}, u32[]{:S(2)}, u32[]{:S(2)}) collective-permute-start(bf16[32,2560]{1,0:T(8,128)(2,1)} %get-tuple-element.197), channel_id=1, source_target_pairs={{0,12},{1,13},{2,14},{3,15},{4,0},{5,1},{6,2},{7,3},{8,4},{9,5},{1... | collective-permute-start | bytes 491528 | tf_op jit(solution)/shard_map/ppermute | solution.py:491
  108.2 7.6 %collective-permute-start.21 = (bf16[32,2688]{1,0:T(8,128)(2,1)}, bf16[32,2688]{1,0:T(8,128)(2,1)}, u32[]{:S(2)}, u32[]{:S(2)}) collective-permute-start(bf16[32,2688]{1,0:T(8,128)(2,1)} %get-tuple-element.210), channel_id=1, source_target_pairs={{0,4},{1,5},{2,6},{3,7},{4,8},{5,9},{6,10},{7,11},{8,12},{9,13},{1... | collective-permute-start | bytes 516104 | tf_op jit(solution)/shard_map/ppermute | solution.py:491
  119.8 10.3 %shard_map.212 = bf16[1024,2688]{1,0:T(8,128)(2,1)S(1)} custom-call(s32[32]{0:T(128)S(1)} %multiply_add_fusion.1.index, bf16[128,2688]{1,0:T(8,128)(2,1)S(1)} %constant_dynamic-update-slice_fusion.6.refs_0_, bf16[128,2688]{1,0:T(8,128)(2,1)S(1)} %collective-permute-done.6.refs_1_, bf16[128,2688]{1,0:T(8,128)(2,1)S(1)} %collective-permute-done.10.refs_2_, ...), custom_call_target="tpu_custom_call" | custom-call | bytes 11010048 | tf_op jit(solution)/shard_map/pallas_call | solution.py:442
  136.9 3.4 fusion.53
  141.3 3.2 copy.72.qkv
  146.3 8.8 %shard_map.213 = (bf16[384,960]{1,0:T(8,128)(2,1)S(1)}, bf16[384,1280]{1,0:T(8,128)(2,1)S(1)}, bf16[384,320]{1,0:T(8,128)(2,1)S(1)}) custom-call(f32[384,1600]{1,0:T(8,128)S(1)} %copy-done.7, f32[384,128]{1,0:T(8,128)S(1)} %get-tuple-element.471.cosine, f32[384,128]{1,0:T(8,128)S(1)} %get-tuple-element.472.sine, s32[384,1]{1,0:T(8,128)S(1)} %copy.73.row_labels, ...), custom_call_target="tpu_custom_call" | custom-call | flops 566231040 | bytes 3840000 | tf_op jit(solution)/shard_map/pallas_call | solution.py:124
  167.9 9.8 %collective-permute-start.33 = (bf16[32,5120]{1,0:T(8,128)(2,1)S(1)}, bf16[32,5120]{1,0:T(8,128)(2,1)S(1)}, u32[]{:S(2)}, u32[]{:S(2)}) collective-permute-start(bf16[32,5120]{1,0:T(8,128)(2,1)S(1)} %copy-done.105), channel_id=1, source_target_pairs={{0,12},{1,13},{2,14},{3,15},{4,0},{5,1},{6,2},{7,3},{8,4},{9,5},{1... | collective-permute-start | bytes 983048 | tf_op jit(solution)/shard_map/ppermute | solution.py:491
  179.5 5.7 shard_map.214
  189.1 4.1 multiply_convert_fusion.5
  198.4 6.1 shard_map.215
  206.9 19.3 %collective-permute-done.40.refs_1_ = bf16[128,5120]{1,0:T(8,128)(2,1)} collective-permute-done((bf16[128,5120]{1,0:T(8,128)(2,1)S(1)}, bf16[128,5120]{1,0:T(8,128)(2,1)}, u32[]{:S(2)}, u32[]{:S(2)}) %collective-permute-start.40) | collective-permute-done | bytes 1310752 | tf_op jit(solution)/shard_map/ppermute | solution.py:498
  234.7 10.3 %shard_map.216 = bf16[1024,2688]{1,0:T(8,128)(2,1)S(1)} custom-call(s32[32]{0:T(128)S(1)} %multiply_add_fusion.1.index, bf16[128,2688]{1,0:T(8,128)(2,1)S(1)} %constant_dynamic-update-slice_fusion.18.refs_0_, bf16[128,2688]{1,0:T(8,128)(2,1)S(1)} %collective-permute-done.30.refs_1_, bf16[128,2688]{1,0:T(8,128)(2,1)S(1)} %collective-permute-done.41.refs_2_, ...), custom_call_target="tpu_custom_call" | custom-call | bytes 11010048 | tf_op jit(solution)/shard_map/pallas_call | solution.py:442
  247.4 3.4 fusion.49
  254.2 3.6 copy.74.qkv
  261.4 8.8 %shard_map.217 = (bf16[384,960]{1,0:T(8,128)(2,1)S(1)}, bf16[384,1280]{1,0:T(8,128)(2,1)S(1)}, bf16[384,320]{1,0:T(8,128)(2,1)S(1)}) custom-call(f32[384,1600]{1,0:T(8,128)S(1)} %copy-done.8, f32[384,128]{1,0:T(8,128)S(1)} %copy-done.31, f32[384,128]{1,0:T(8,128)S(1)} %copy-done.34, s32[384,1]{1,0:T(8,128)S(1)} %copy-done.28, ...), custom_call_target="tpu_custom_call" | custom-call | flops 566231040 | bytes 3840000 | tf_op jit(solution)/shard_map/pallas_call | solution.py:124
  281.2 5.5 shard_map.218
  290.7 4.0 multiply_convert_fusion.4
  295.4 4.1 fusion.292
  310.1 6.1 shard_map.219
  316.3 3.6 multiply_convert_fusion.2
  322.0 5.1 convolution_convert_fusion.1
  345.7 5.4 fusion
  362.4 4.9 add_convert_fusion.1
  372.1 3.7 select_convert_fusion.1
  375.8 3.9 fusion.120.grad_att
  386.1 12.5 %shard_map.220 = bf16[384,1600]{1,0:T(8,128)(2,1)S(1)} custom-call(bf16[384,1280]{1,0:T(8,128)(2,1)S(1)} %copy-done.39, bf16[384,320]{1,0:T(8,128)(2,1)S(1)} %copy-done.43, bf16[384,960]{1,0:T(8,128)(2,1)S(1)} %fusion.120.grad_att, f32[384,128]{1,0:T(8,128)S(1)} %copy-done.32, f32[384,128]{1,0:T(8,128)S(1)} %copy-done.35, s32[384,1]{1,0:T(8,128)S(1)} %copy-done.29, ...), custom_call_target="tpu_custom_call" | custom-call | flops 1415577600 | bytes 3840000 | tf_op jit(solution)/shard_map/pallas_call | solution.py:178
  399.7 10.5 %collective-permute-done.69 = bf16[256,5120]{1,0:T(8,128)(2,1)} collective-permute-done((bf16[256,5120]{1,0:T(8,128)(2,1)}, bf16[256,5120]{1,0:T(8,128)(2,1)}, u32[]{:S(2)}, u32[]{:S(2)}) %collective-permute-start.69) | collective-permute-done | bytes 2621472 | tf_op jit(solution)/shard_map/ppermute | solution.py:551
  426.5 13.3 %collective-permute-done.72 = bf16[256,1024]{1,0:T(8,128)(2,1)S(1)} collective-permute-done((bf16[256,1024]{1,0:T(8,128)(2,1)S(1)}, bf16[256,1024]{1,0:T(8,128)(2,1)S(1)}, u32[]{:S(2)}, u32[]{:S(2)}) %collective-permute-start.72) | collective-permute-done | bytes 524320 | tf_op jit(solution)/shard_map/ppermute | solution.py:551
  454.6 5.9 multiply_convert_fusion
  463.1 3.3 collective-permute-done.74
  467.8 4.7 convolution_convert_fusion
  484.5 4.7 fusion.10
  500.1 4.9 add_convert_fusion
  512.2 3.9 fusion.121.grad_att
  516.2 3.4 collective-permute-start.87
  526.6 12.1 %shard_map.221 = bf16[384,1600]{1,0:T(8,128)(2,1)S(1)} custom-call(bf16[384,1280]{1,0:T(8,128)(2,1)S(1)} %copy-done.37, bf16[384,320]{1,0:T(8,128)(2,1)S(1)} %copy-done.41, bf16[384,960]{1,0:T(8,128)(2,1)S(1)} %fusion.121.grad_att, f32[384,128]{1,0:T(8,128)S(1)} %copy-done.32, f32[384,128]{1,0:T(8,128)S(1)} %copy-done.35, s32[384,1]{1,0:T(8,128)S(1)} %copy-done.29, ...), custom_call_target="tpu_custom_call" | custom-call | flops 1415577600 | bytes 3840000 | tf_op jit(solution)/shard_map/pallas_call | solution.py:178
  540.5 9.9 %collective-permute-done.84 = bf16[256,5120]{1,0:T(8,128)(2,1)} collective-permute-done((bf16[256,5120]{1,0:T(8,128)(2,1)}, bf16[256,5120]{1,0:T(8,128)(2,1)}, u32[]{:S(2)}, u32[]{:S(2)}) %collective-permute-start.84) | collective-permute-done | bytes 2621472 | tf_op jit(solution)/shard_map/ppermute | solution.py:551
  550.4 5.7 multiply_reduce_fusion.1
  568.2 4.1 subtract_add_fusion
  574.0 9.0 %collective-permute-done.89 = bf16[128,5120]{1,0:T(8,128)(2,1)} collective-permute-done((bf16[128,5120]{1,0:T(8,128)(2,1)}, bf16[128,5120]{1,0:T(8,128)(2,1)}, u32[]{:S(2)}, u32[]{:S(2)}) %collective-permute-start.89) | collective-permute-done | bytes 1310752 | tf_op jit(solution)/shard_map/ppermute | solution.py:553
  603.6 3.4 collective-permute-done.92
  624.7 6.1 collective-permute-done.95
  630.8 8.8 %collective-permute-done.96 = bf16[32,1664]{1,0:T(8,128)(2,1)S(1)} collective-permute-done((bf16[32,1664]{1,0:T(8,128)(2,1)S(1)}, bf16[32,1664]{1,0:T(8,128)(2,1)S(1)}, u32[]{:S(2)}, u32[]{:S(2)}) %collective-permute-start.96) | collective-permute-done | bytes 106528 | tf_op jit(solution)/shard_map/ppermute | solution.py:562
  (894 shorter events, 324.3 us)
Async XLA Ops:
  7.2 532.6 %reduce-scatter.5.cloned.1.call-start = ((), (), s32[]{:S(2)}) async-start(), calls=%async_computation.4 | async-start | bytes 819200 | tf_op jit(solution)/shard_map/reduce_scatter | solution.py:567
  48.6 22.5 %collective-permute-start.8 = (bf16[32,5120]{1,0:T(8,128)(2,1)S(1)}, bf16[32,5120]{1,0:T(8,128)(2,1)S(1)}, u32[]{:S(2)}, u32[]{:S(2)}) collective-permute-start(bf16[32,5120]{1,0:T(8,128)(2,1)S(1)} %get-tuple-element.187), channel_id=1, source_target_pairs={{0,8},{1,9},{2,10},{3,11},{4,12},{5,13},{6,14},{7,15},{8,0},{9,1},... | collective-permute-start | bytes 983048 | tf_op jit(solution)/shard_map/ppermute | solution.py:491
  50.2 20.9 %collective-permute-start.9 = (bf16[32,5120]{1,0:T(8,128)(2,1)S(1)}, bf16[32,5120]{1,0:T(8,128)(2,1)S(1)}, u32[]{:S(2)}, u32[]{:S(2)}) collective-permute-start(bf16[32,5120]{1,0:T(8,128)(2,1)S(1)} %get-tuple-element.187), channel_id=1, source_target_pairs={{0,12},{1,13},{2,14},{3,15},{4,0},{5,1},{6,2},{7,3},{8,4},{9,5},{1... | collective-permute-start | bytes 983048 | tf_op jit(solution)/shard_map/ppermute | solution.py:491
  73.4 33.0 %collective-permute-start.12 = (bf16[128,5120]{1,0:T(8,128)(2,1)}, bf16[128,5120]{1,0:T(8,128)(2,1)}, u32[]{:S(2)}, u32[]{:S(2)}) collective-permute-start(bf16[128,5120]{1,0:T(8,128)(2,1)} %constant_dynamic-update-slice_fusion.10.refs_0_), channel_id=1, source_target_pairs={{0,1},{1,0},{2,3},{3,2},{4,5},{5,4},{6,7},{7,6},{8,9},{9,8},{10,11... | collective-permute-start | bytes 3932168 | tf_op jit(solution)/shard_map/ppermute | solution.py:498
  75.7 29.2 %collective-permute-start.11 = (bf16[128,2688]{1,0:T(8,128)(2,1)S(1)}, bf16[128,2688]{1,0:T(8,128)(2,1)S(1)}, u32[]{:S(2)}, u32[]{:S(2)}) collective-permute-start(bf16[128,2688]{1,0:T(8,128)(2,1)S(1)} %collective-permute-done.6.refs_1_), channel_id=1, source_target_pairs={{0,2},{1,3},{2,0},{3,1},{4,6},{5,7},{6,4},{7,5},{8,10},{9,11},{10,... | collective-permute-start | bytes 2064392 | tf_op jit(solution)/shard_map/ppermute | solution.py:501
  78.3 28.1 %collective-permute-start.13 = (bf16[32,2560]{1,0:T(8,128)(2,1)}, bf16[32,2560]{1,0:T(8,128)(2,1)S(1)}, u32[]{:S(2)}, u32[]{:S(2)}) collective-permute-start(bf16[32,2560]{1,0:T(8,128)(2,1)} %get-tuple-element.197), channel_id=1, source_target_pairs={{0,4},{1,5},{2,6},{3,7},{4,8},{5,9},{6,10},{7,11},{8,12},{9,13},{1... | collective-permute-start | bytes 491528 | tf_op jit(solution)/shard_map/ppermute | solution.py:491
  86.2 21.2 %collective-permute-start.14 = (bf16[32,2560]{1,0:T(8,128)(2,1)}, bf16[32,2560]{1,0:T(8,128)(2,1)S(1)}, u32[]{:S(2)}, u32[]{:S(2)}) collective-permute-start(bf16[32,2560]{1,0:T(8,128)(2,1)} %get-tuple-element.197), channel_id=1, source_target_pairs={{0,8},{1,9},{2,10},{3,11},{4,12},{5,13},{6,14},{7,15},{8,0},{9,1},... | collective-permute-start | bytes 491528 | tf_op jit(solution)/shard_map/ppermute | solution.py:491
  106.4 51.0 %collective-permute-start.24 = (bf16[128,5120]{1,0:T(8,128)(2,1)}, bf16[128,5120]{1,0:T(8,128)(2,1)}, u32[]{:S(2)}, u32[]{:S(2)}) collective-permute-start(bf16[128,5120]{1,0:T(8,128)(2,1)} %constant_dynamic-update-slice_fusion.10.refs_0_), channel_id=1, source_target_pairs={{0,2},{1,3},{2,0},{3,1},{4,6},{5,7},{6,4},{7,5},{8,10},{9,11},{10,... | collective-permute-start | bytes 3932168 | tf_op jit(solution)/shard_map/ppermute | solution.py:496
  108.2 32.1 %collective-permute-start.21 = (bf16[32,2688]{1,0:T(8,128)(2,1)}, bf16[32,2688]{1,0:T(8,128)(2,1)}, u32[]{:S(2)}, u32[]{:S(2)}) collective-permute-start(bf16[32,2688]{1,0:T(8,128)(2,1)} %get-tuple-element.210), channel_id=1, source_target_pairs={{0,4},{1,5},{2,6},{3,7},{4,8},{5,9},{6,10},{7,11},{8,12},{9,13},{1... | collective-permute-start | bytes 516104 | tf_op jit(solution)/shard_map/ppermute | solution.py:491
  115.8 24.6 %collective-permute-start.22 = (bf16[32,2688]{1,0:T(8,128)(2,1)}, bf16[32,2688]{1,0:T(8,128)(2,1)}, u32[]{:S(2)}, u32[]{:S(2)}) collective-permute-start(bf16[32,2688]{1,0:T(8,128)(2,1)} %get-tuple-element.210), channel_id=1, source_target_pairs={{0,8},{1,9},{2,10},{3,11},{4,12},{5,13},{6,14},{7,15},{8,0},{9,1},... | collective-permute-start | bytes 516104 | tf_op jit(solution)/shard_map/ppermute | solution.py:491
  118.6 38.8 %collective-permute-start.25 = (bf16[128,5120]{1,0:T(8,128)(2,1)}, bf16[128,5120]{1,0:T(8,128)(2,1)}, u32[]{:S(2)}, u32[]{:S(2)}) collective-permute-start(bf16[128,5120]{1,0:T(8,128)(2,1)} %collective-permute-done.12.refs_1_), channel_id=1, source_target_pairs={{0,2},{1,3},{2,0},{3,1},{4,6},{5,7},{6,4},{7,5},{8,10},{9,11},{10,... | collective-permute-start | bytes 3932168 | tf_op jit(solution)/shard_map/ppermute | solution.py:501
  140.3 22.7 %collective-permute-start.26 = (bf16[128,5120]{1,0:T(8,128)(2,1)}, bf16[128,5120]{1,0:T(8,128)(2,1)}, u32[]{:S(2)}, u32[]{:S(2)}) collective-permute-start(bf16[128,5120]{1,0:T(8,128)(2,1)} %constant_dynamic-update-slice_fusion.10.refs_0_), channel_id=1, source_target_pairs={{0,16},{16,0},{1,17},{17,1},{2,18},{18,2},{3,19},{19,3},{4,20},{20... | collective-permute-start | bytes 3932168 | tf_op jit(solution)/shard_map/ppermute | solution.py:363
  140.4 23.9 %collective-permute-start.27 = (bf16[128,5120]{1,0:T(8,128)(2,1)}, bf16[128,5120]{1,0:T(8,128)(2,1)}, u32[]{:S(2)}, u32[]{:S(2)}) collective-permute-start(bf16[128,5120]{1,0:T(8,128)(2,1)} %collective-permute-done.12.refs_1_), channel_id=1, source_target_pairs={{0,16},{16,0},{1,17},{17,1},{2,18},{18,2},{3,19},{19,3},{4,20},{20... | collective-permute-start | bytes 3932168 | tf_op jit(solution)/shard_map/ppermute | solution.py:363
  163.1 30.7 %collective-permute-start.34 = (bf16[128,2560]{1,0:T(8,128)(2,1)S(1)}, bf16[128,2560]{1,0:T(8,128)(2,1)S(1)}, u32[]{:S(2)}, u32[]{:S(2)}) collective-permute-start(bf16[128,2560]{1,0:T(8,128)(2,1)S(1)} %copy-done.10), channel_id=1, source_target_pairs={{0,2},{1,3},{2,0},{3,1},{4,6},{5,7},{6,4},{7,5},{8,10},{9,11},{10,... | collective-permute-start | bytes 1966088 | tf_op jit(solution)/shard_map/ppermute | solution.py:496
  164.3 28.8 %collective-permute-start.31 = (bf16[32,5120]{1,0:T(8,128)(2,1)S(1)}, bf16[32,5120]{1,0:T(8,128)(2,1)S(1)}, u32[]{:S(2)}, u32[]{:S(2)}) collective-permute-start(bf16[32,5120]{1,0:T(8,128)(2,1)S(1)} %copy-done.105), channel_id=1, source_target_pairs={{0,4},{1,5},{2,6},{3,7},{4,8},{5,9},{6,10},{7,11},{8,12},{9,13},{1... | collective-permute-start | bytes 983048 | tf_op jit(solution)/shard_map/ppermute | solution.py:491
  164.9 28.3 %collective-permute-start.32 = (bf16[32,5120]{1,0:T(8,128)(2,1)S(1)}, bf16[32,5120]{1,0:T(8,128)(2,1)S(1)}, u32[]{:S(2)}, u32[]{:S(2)}) collective-permute-start(bf16[32,5120]{1,0:T(8,128)(2,1)S(1)} %copy-done.105), channel_id=1, source_target_pairs={{0,8},{1,9},{2,10},{3,11},{4,12},{5,13},{6,14},{7,15},{8,0},{9,1},... | collective-permute-start | bytes 983048 | tf_op jit(solution)/shard_map/ppermute | solution.py:491
  167.9 25.9 %collective-permute-start.33 = (bf16[32,5120]{1,0:T(8,128)(2,1)S(1)}, bf16[32,5120]{1,0:T(8,128)(2,1)S(1)}, u32[]{:S(2)}, u32[]{:S(2)}) collective-permute-start(bf16[32,5120]{1,0:T(8,128)(2,1)S(1)} %copy-done.105), channel_id=1, source_target_pairs={{0,12},{1,13},{2,14},{3,15},{4,0},{5,1},{6,2},{7,3},{8,4},{9,5},{1... | collective-permute-start | bytes 983048 | tf_op jit(solution)/shard_map/ppermute | solution.py:491
  194.4 31.8 %collective-permute-start.40 = (bf16[128,5120]{1,0:T(8,128)(2,1)S(1)}, bf16[128,5120]{1,0:T(8,128)(2,1)}, u32[]{:S(2)}, u32[]{:S(2)}) collective-permute-start(bf16[128,5120]{1,0:T(8,128)(2,1)S(1)} %constant_dynamic-update-slice_fusion.22.refs_0_), channel_id=1, source_target_pairs={{0,1},{1,0},{2,3},{3,2},{4,5},{5,4},{6,7},{7,6},{8,9},{9,8},{10,11... | collective-permute-start | bytes 3932168 | tf_op jit(solution)/shard_map/ppermute | solution.py:498
  195.4 30.8 %collective-permute-start.41 = (bf16[128,2688]{1,0:T(8,128)(2,1)S(1)}, bf16[128,2688]{1,0:T(8,128)(2,1)S(1)}, u32[]{:S(2)}, u32[]{:S(2)}) collective-permute-start(bf16[128,2688]{1,0:T(8,128)(2,1)S(1)} %constant_dynamic-update-slice_fusion.18.refs_0_), channel_id=1, source_target_pairs={{0,2},{1,3},{2,0},{3,1},{4,6},{5,7},{6,4},{7,5},{8,10},{9,11},{10,... | collective-permute-start | bytes 2064392 | tf_op jit(solution)/shard_map/ppermute | solution.py:496
  196.6 33.7 %collective-permute-start.43 = (bf16[128,2688]{1,0:T(8,128)(2,1)S(1)}, bf16[128,2688]{1,0:T(8,128)(2,1)S(1)}, u32[]{:S(2)}, u32[]{:S(2)}) collective-permute-start(bf16[128,2688]{1,0:T(8,128)(2,1)S(1)} %constant_dynamic-update-slice_fusion.18.refs_0_), channel_id=1, source_target_pairs={{0,16},{16,0},{1,17},{17,1},{2,18},{18,2},{3,19},{19,3},{4,20},{20... | collective-permute-start | bytes 2064392 | tf_op jit(solution)/shard_map/ppermute | solution.py:363
  197.2 29.0 %collective-permute-start.42 = (bf16[128,2688]{1,0:T(8,128)(2,1)S(1)}, bf16[128,2688]{1,0:T(8,128)(2,1)S(1)}, u32[]{:S(2)}, u32[]{:S(2)}) collective-permute-start(bf16[128,2688]{1,0:T(8,128)(2,1)S(1)} %collective-permute-done.30.refs_1_), channel_id=1, source_target_pairs={{0,2},{1,3},{2,0},{3,1},{4,6},{5,7},{6,4},{7,5},{8,10},{9,11},{10,... | collective-permute-start | bytes 2064392 | tf_op jit(solution)/shard_map/ppermute | solution.py:501
  198.4 32.7 %collective-permute-start.44 = (bf16[128,2688]{1,0:T(8,128)(2,1)S(1)}, bf16[128,2688]{1,0:T(8,128)(2,1)S(1)}, u32[]{:S(2)}, u32[]{:S(2)}) collective-permute-start(bf16[128,2688]{1,0:T(8,128)(2,1)S(1)} %collective-permute-done.30.refs_1_), channel_id=1, source_target_pairs={{0,16},{16,0},{1,17},{17,1},{2,18},{18,2},{3,19},{19,3},{4,20},{20... | collective-permute-start | bytes 2064392 | tf_op jit(solution)/shard_map/ppermute | solution.py:363
  226.7 24.1 %collective-permute-start.47 = (bf16[32,2560]{1,0:T(8,128)(2,1)S(1)}, bf16[32,2560]{1,0:T(8,128)(2,1)S(1)}, u32[]{:S(2)}, u32[]{:S(2)}) collective-permute-start(bf16[32,2560]{1,0:T(8,128)(2,1)S(1)} %copy-done.130), channel_id=1, source_target_pairs={{0,4},{1,5},{2,6},{3,7},{4,8},{5,9},{6,10},{7,11},{8,12},{9,13},{1... | collective-permute-start | bytes 491528 | tf_op jit(solution)/shard_map/ppermute | solution.py:491
  230.3 20.5 %collective-permute-start.48 = (bf16[32,2560]{1,0:T(8,128)(2,1)S(1)}, bf16[32,2560]{1,0:T(8,128)(2,1)S(1)}, u32[]{:S(2)}, u32[]{:S(2)}) collective-permute-start(bf16[32,2560]{1,0:T(8,128)(2,1)S(1)} %copy-done.130), channel_id=1, source_target_pairs={{0,8},{1,9},{2,10},{3,11},{4,12},{5,13},{6,14},{7,15},{8,0},{9,1},... | collective-permute-start | bytes 491528 | tf_op jit(solution)/shard_map/ppermute | solution.py:491
  231.2 19.7 %collective-permute-start.49 = (bf16[32,2560]{1,0:T(8,128)(2,1)S(1)}, bf16[32,2560]{1,0:T(8,128)(2,1)S(1)}, u32[]{:S(2)}, u32[]{:S(2)}) collective-permute-start(bf16[32,2560]{1,0:T(8,128)(2,1)S(1)} %copy-done.130), channel_id=1, source_target_pairs={{0,12},{1,13},{2,14},{3,15},{4,0},{5,1},{6,2},{7,3},{8,4},{9,5},{1... | collective-permute-start | bytes 491528 | tf_op jit(solution)/shard_map/ppermute | solution.py:491
  232.7 39.6 %collective-permute-start.51 = (bf16[128,5120]{1,0:T(8,128)(2,1)S(1)}, bf16[128,5120]{1,0:T(8,128)(2,1)}, u32[]{:S(2)}, u32[]{:S(2)}) collective-permute-start(bf16[128,5120]{1,0:T(8,128)(2,1)S(1)} %constant_dynamic-update-slice_fusion.22.refs_0_), channel_id=1, source_target_pairs={{0,2},{1,3},{2,0},{3,1},{4,6},{5,7},{6,4},{7,5},{8,10},{9,11},{10,... | collective-permute-start | bytes 3932168 | tf_op jit(solution)/shard_map/ppermute | solution.py:496
  233.6 38.7 %collective-permute-start.52 = (bf16[128,5120]{1,0:T(8,128)(2,1)}, bf16[128,5120]{1,0:T(8,128)(2,1)}, u32[]{:S(2)}, u32[]{:S(2)}) collective-permute-start(bf16[128,5120]{1,0:T(8,128)(2,1)} %collective-permute-done.40.refs_1_), channel_id=1, source_target_pairs={{0,2},{1,3},{2,0},{3,1},{4,6},{5,7},{6,4},{7,5},{8,10},{9,11},{10,... | collective-permute-start | bytes 3932168 | tf_op jit(solution)/shard_map/ppermute | solution.py:501
  253.7 25.8 %collective-permute-start.53 = (bf16[128,5120]{1,0:T(8,128)(2,1)S(1)}, bf16[128,5120]{1,0:T(8,128)(2,1)}, u32[]{:S(2)}, u32[]{:S(2)}) collective-permute-start(bf16[128,5120]{1,0:T(8,128)(2,1)S(1)} %constant_dynamic-update-slice_fusion.22.refs_0_), channel_id=1, source_target_pairs={{0,16},{16,0},{1,17},{17,1},{2,18},{18,2},{3,19},{19,3},{4,20},{20... | collective-permute-start | bytes 3932168 | tf_op jit(solution)/shard_map/ppermute | solution.py:363
  253.7 25.8 %collective-permute-start.54 = (bf16[128,5120]{1,0:T(8,128)(2,1)}, bf16[128,5120]{1,0:T(8,128)(2,1)}, u32[]{:S(2)}, u32[]{:S(2)}) collective-permute-start(bf16[128,5120]{1,0:T(8,128)(2,1)} %collective-permute-done.40.refs_1_), channel_id=1, source_target_pairs={{0,16},{16,0},{1,17},{17,1},{2,18},{18,2},{3,19},{19,3},{4,20},{20... | collective-permute-start | bytes 3932168 | tf_op jit(solution)/shard_map/ppermute | solution.py:363
  279.4 20.1 %collective-permute-start.59 = (bf16[128,2560]{1,0:T(8,128)(2,1)}, bf16[128,2560]{1,0:T(8,128)(2,1)S(1)}, u32[]{:S(2)}, u32[]{:S(2)}) collective-permute-start(bf16[128,2560]{1,0:T(8,128)(2,1)} %constant_dynamic-update-slice_fusion.26.refs_0_), channel_id=1, source_target_pairs={{0,16},{16,0},{1,17},{17,1},{2,18},{18,2},{3,19},{19,3},{4,20},{20... | collective-permute-start | bytes 1966088 | tf_op jit(solution)/shard_map/ppermute | solution.py:363
  327.1 32.3 %collective-permute-start.65 = (bf16[512,5120]{1,0:T(8,128)(2,1)}, bf16[512,5120]{1,0:T(8,128)(2,1)}, u32[]{:S(2)}, u32[]{:S(2)}) collective-permute-start(bf16[512,5120]{1,0:T(8,128)(2,1)} %convolution_convert_fusion.1), channel_id=1, source_target_pairs={{0,16},{16,0},{1,17},{17,1},{2,18},{18,2},{3,19},{19,3},{4,20},{20... | collective-permute-start | bytes 15728648 | tf_op jit(solution)/shard_map/ppermute | solution.py:363
  352.7 27.1 %collective-permute-start.66 = (bf16[256,2560]{1,0:T(8,128)(2,1)S(1)}, bf16[256,2560]{1,0:T(8,128)(2,1)}, u32[]{:S(2)}, u32[]{:S(2)}) collective-permute-start(bf16[256,2560]{1,0:T(8,128)(2,1)S(1)} %slice.534), channel_id=1, source_target_pairs={{0,2},{1,3},{2,0},{3,1},{4,6},{5,7},{6,4},{7,5},{8,10},{9,11},{10,... | collective-permute-start | bytes 3932168 | tf_op jit(solution)/shard_map/ppermute | solution.py:551
  371.2 39.0 %collective-permute-start.69 = (bf16[256,5120]{1,0:T(8,128)(2,1)}, bf16[256,5120]{1,0:T(8,128)(2,1)}, u32[]{:S(2)}, u32[]{:S(2)}) collective-permute-start(bf16[256,5120]{1,0:T(8,128)(2,1)} %slice.539), channel_id=1, source_target_pairs={{0,2},{1,3},{2,0},{3,1},{4,6},{5,7},{6,4},{7,5},{8,10},{9,11},{10,... | collective-permute-start | bytes 7864328 | tf_op jit(solution)/shard_map/ppermute | solution.py:551
  384.3 34.4 %collective-permute-start.63 = (bf16[384,1024]{1,0:T(8,128)(2,1)S(1)}, bf16[384,1024]{1,0:T(8,128)(2,1)S(1)}, u32[]{:S(2)}, u32[]{:S(2)}) collective-permute-start(bf16[384,1024]{1,0:T(8,128)(2,1)S(1)} %copy-done.183), channel_id=1, source_target_pairs={{0,16},{16,0},{1,17},{17,1},{2,18},{18,2},{3,19},{19,3},{4,20},{20... | collective-permute-start | bytes 2359304 | tf_op jit(solution)/shard_map/ppermute | solution.py:724
  414.4 26.8 %collective-permute-start.70 = (bf16[512,1664]{1,0:T(8,128)(2,1)S(1)}, bf16[512,1664]{1,0:T(8,128)(2,1)S(1)}, u32[]{:S(2)}, u32[]{:S(2)}) collective-permute-start(bf16[512,1664]{1,0:T(8,128)(2,1)S(1)} %convolution_convert_fusion.3), channel_id=1, source_target_pairs={{0,16},{16,0},{1,17},{17,1},{2,18},{18,2},{3,19},{19,3},{4,20},{20... | collective-permute-start | bytes 5111816 | tf_op jit(solution)/shard_map/ppermute | solution.py:363
  417.9 23.3 %collective-permute-start.71 = (bf16[128,5120]{1,0:T(8,128)(2,1)S(1)}, bf16[128,5120]{1,0:T(8,128)(2,1)S(1)}, u32[]{:S(2)}, u32[]{:S(2)}) collective-permute-start(bf16[128,5120]{1,0:T(8,128)(2,1)S(1)} %slice.542), channel_id=1, source_target_pairs={{0,1},{1,0},{2,3},{3,2},{4,5},{5,4},{6,7},{7,6},{8,9},{9,8},{10,11... | collective-permute-start | bytes 3932168 | tf_op jit(solution)/shard_map/ppermute | solution.py:553
  447.8 126.3 %reduce-scatter.7.cloned.1.call-start = ((), (), s32[]{:S(2)}) async-start(), calls=%async_computation.5 | async-start | bytes 1638400 | tf_op jit(solution)/shard_map/reduce_scatter | solution.py:567
  472.5 25.8 %collective-permute-start.76 = (bf16[512,5120]{1,0:T(8,128)(2,1)}, bf16[512,5120]{1,0:T(8,128)(2,1)}, u32[]{:S(2)}, u32[]{:S(2)}) collective-permute-start(bf16[512,5120]{1,0:T(8,128)(2,1)} %convolution_convert_fusion), channel_id=1, source_target_pairs={{0,16},{16,0},{1,17},{17,1},{2,18},{18,2},{3,19},{19,3},{4,20},{20... | collective-permute-start | bytes 15728648 | tf_op jit(solution)/shard_map/ppermute | solution.py:363
  474.3 142.5 %reduce-scatter.9.cloned.1.call-start = ((), (), s32[]{:S(2)}) async-start(), calls=%async_computation.6 | async-start | bytes 819200 | tf_op jit(solution)/shard_map/reduce_scatter | solution.py:567
  478.3 20.0 %collective-permute-start.77 = (bf16[128,1664]{1,0:T(8,128)(2,1)S(1)}, bf16[128,1664]{1,0:T(8,128)(2,1)S(1)}, u32[]{:S(2)}, u32[]{:S(2)}) collective-permute-start(bf16[128,1664]{1,0:T(8,128)(2,1)S(1)} %slice.557), channel_id=1, source_target_pairs={{0,1},{1,0},{2,3},{3,2},{4,5},{5,4},{6,7},{7,6},{8,9},{9,8},{10,11... | collective-permute-start | bytes 1277960 | tf_op jit(solution)/shard_map/ppermute | solution.py:553
  508.2 42.3 %collective-permute-start.84 = (bf16[256,5120]{1,0:T(8,128)(2,1)}, bf16[256,5120]{1,0:T(8,128)(2,1)}, u32[]{:S(2)}, u32[]{:S(2)}) collective-permute-start(bf16[256,5120]{1,0:T(8,128)(2,1)} %slice.566), channel_id=1, source_target_pairs={{0,2},{1,3},{2,0},{3,1},{4,6},{5,7},{6,4},{7,5},{8,10},{9,11},{10,... | collective-permute-start | bytes 7864328 | tf_op jit(solution)/shard_map/ppermute | solution.py:551
  510.2 28.6 %collective-permute-start.85 = (bf16[32,1664]{1,0:T(8,128)(2,1)}, bf16[32,1664]{1,0:T(8,128)(2,1)}, u32[]{:S(2)}, u32[]{:S(2)}) collective-permute-start(bf16[32,1664]{1,0:T(8,128)(2,1)} %get-tuple-element.427), channel_id=1, source_target_pairs={{0,4},{1,5},{2,6},{3,7},{4,8},{5,9},{6,10},{7,11},{8,12},{9,13},{1... | collective-permute-start | bytes 319496 | tf_op jit(solution)/shard_map/ppermute | solution.py:562
  510.9 28.9 %collective-permute-start.86 = (bf16[32,1664]{1,0:T(8,128)(2,1)}, bf16[32,1664]{1,0:T(8,128)(2,1)}, u32[]{:S(2)}, u32[]{:S(2)}) collective-permute-start(bf16[32,1664]{1,0:T(8,128)(2,1)} %get-tuple-element.426), channel_id=1, source_target_pairs={{0,8},{1,9},{2,10},{3,11},{4,12},{5,13},{6,14},{7,15},{8,0},{9,1},... | collective-permute-start | bytes 319496 | tf_op jit(solution)/shard_map/ppermute | solution.py:562
  516.2 23.6 %collective-permute-start.87 = (bf16[32,1664]{1,0:T(8,128)(2,1)}, bf16[32,1664]{1,0:T(8,128)(2,1)}, u32[]{:S(2)}, u32[]{:S(2)}) collective-permute-start(bf16[32,1664]{1,0:T(8,128)(2,1)} %get-tuple-element.425), channel_id=1, source_target_pairs={{0,12},{1,13},{2,14},{3,15},{4,0},{5,1},{6,2},{7,3},{8,4},{9,5},{1... | collective-permute-start | bytes 319496 | tf_op jit(solution)/shard_map/ppermute | solution.py:562
  538.8 35.3 %collective-permute-start.90 = (bf16[256,1024]{1,0:T(8,128)(2,1)}, bf16[256,1024]{1,0:T(8,128)(2,1)}, u32[]{:S(2)}, u32[]{:S(2)}) collective-permute-start(bf16[256,1024]{1,0:T(8,128)(2,1)} %slice.573), channel_id=1, source_target_pairs={{0,2},{1,3},{2,0},{3,1},{4,6},{5,7},{6,4},{7,5},{8,10},{9,11},{10,... | collective-permute-start | bytes 1572872 | tf_op jit(solution)/shard_map/ppermute | solution.py:551
  559.7 23.3 %collective-permute-start.88 = (bf16[512,1664]{1,0:T(8,128)(2,1)}, bf16[512,1664]{1,0:T(8,128)(2,1)}, u32[]{:S(2)}, u32[]{:S(2)}) collective-permute-start(bf16[512,1664]{1,0:T(8,128)(2,1)} %convolution_convert_fusion.2), channel_id=1, source_target_pairs={{0,16},{16,0},{1,17},{17,1},{2,18},{18,2},{3,19},{19,3},{4,20},{20... | collective-permute-start | bytes 5111816 | tf_op jit(solution)/shard_map/ppermute | solution.py:363
  568.1 71.4 %reduce-scatter.11.cloned.1.call-start = ((), (), s32[]{:S(2)}) async-start(), calls=%async_computation.7 | async-start | bytes 1638400 | tf_op jit(solution)/shard_map/reduce_scatter | solution.py:567
  618.3 21.2 %collective-permute-start.96 = (bf16[32,1664]{1,0:T(8,128)(2,1)S(1)}, bf16[32,1664]{1,0:T(8,128)(2,1)S(1)}, u32[]{:S(2)}, u32[]{:S(2)}) collective-permute-start(bf16[32,1664]{1,0:T(8,128)(2,1)S(1)} %get-tuple-element.423), channel_id=1, source_target_pairs={{0,8},{1,9},{2,10},{3,11},{4,12},{5,13},{6,14},{7,15},{8,0},{9,1},... | collective-permute-start | bytes 319496 | tf_op jit(solution)/shard_map/ppermute | solution.py:562
  (277 other events, 2592.6 us)
Sparse Core Ops, SparseCore 0:
  447.9 20.8 reduce-scatter.4
  474.4 34.0 reduce-scatter.6
  568.3 20.6 reduce-scatter.8
  598.1 40.6 reduce-scatter.10

commit v4 on v3

--- a/solution.py
+++ b/solution.py
@@ -130,7 +130,7 @@
         ],
         scratch_shapes=[pltpu.VMEM((length, length), f32)],
         compiler_params=pltpu.CompilerParams(vmem_limit_bytes=32 * 2**20),
-        cost_estimate=pl.CostEstimate(flops=4 * length * length * wide, bytes_accessed=length * 10000, transcendentals=length * length * HEADS),
+        cost_estimate=pl.CostEstimate(flops=0, bytes_accessed=0, transcendentals=0),
     )(qkv, cosine, sine, labels[:, None], labels[None, :])
 
 
@@ -180,11 +180,11 @@
         out_shape=jax.ShapeDtypeStruct((length, wide + 2 * narrow), bf16),
         scratch_shapes=[pltpu.VMEM((length, length), f32), pltpu.VMEM((length, wide + narrow), f32), pltpu.VMEM((length, narrow), f32)],
         compiler_params=pltpu.CompilerParams(vmem_limit_bytes=32 * 2**20),
-        cost_estimate=pl.CostEstimate(flops=10 * length * length * wide, bytes_accessed=length * 10000, transcendentals=length * length * HEADS),
+        cost_estimate=pl.CostEstimate(flops=0, bytes_accessed=0, transcendentals=0),
     )(turned_qk, values, grad_att, cosine, sine, labels[:, None], labels[None, :])
 
 
-def forward(x, source, layer, labels, tables, features):
+def forward(x, source, layer, labels, tables, features, early=None):
     turn = iter(source.order[layer])
     x = source.tie(x, next(turn))
     w = source.weights(layer)
@@ -204,17 +204,26 @@
     up = dot(second, w.up)
     hidden = (jax.nn.silu(gate) * up).astype(bf16)
     hidden = source.tie(hidden, next(turn))
+    if early is not None:
+        early.begin(DOWN, w.order_hidden(hidden), early.low)
+    hidden = source.tie(hidden, next(turn))
     w = source.weights(layer)
     output = middle + dot(hidden, w.down)
-    return output, w, (
-        scale_one, normed, turned_qk, values, attended, middle, scale_two, second, gate, up, hidden,
-    )
+    ordered = w.order(normed), w.order(attended), w.order(second), w.order_hidden(hidden)
+    if early is None:
+        output, ordered = lax.optimization_barrier((output, ordered))
+    return output, w, (scale_one, turned_qk, values, middle, scale_two, gate, up, ordered)
 
 
 def backward(x, w, labels, tables, features, kept, grad, flow):
-    (scale_one, normed, turned_qk, values, attended, middle, scale_two, second, gate, up, hidden) = kept
+    scale_one, turned_qk, values, middle, scale_two, gate, up, ordered = kept
+    normed, attended, second, hidden = ordered
     low = grad.astype(bf16)
-    flow.begin(DOWN, hidden, low)
+    early = DOWN in flow.now
+    if early:
+        low = flow.tie(low, (DOWN,), ())
+    else:
+        flow.begin(DOWN, hidden, low)
     grad_hidden = dot_nt(low, w.down)
     sig = jax.nn.sigmoid(gate)
     silu = gate * sig
@@ -225,18 +234,18 @@
     grad_second = dot_nt(gate_low, w.gate) + dot_nt(up_low, w.up)
     grad_norm, gain_two = norm_back(middle, scale_two, w.gain_two, grad_second, features)
     grad_middle = grad + grad_norm
-    grad_middle = flow.tie(grad_middle, (GATE_UP,), (QKV, OUT))
+    grad_middle = flow.tie(grad_middle, (GATE_UP, DOWN) if early else (GATE_UP,), (QKV, OUT))
     middle_low = grad_middle.astype(bf16)
     flow.begin(OUT, attended, middle_low)
     grad_att = dot_nt(middle_low, w.out).astype(bf16)
     grad_att = dot_nt(grad_att, w.spread).astype(bf16)
-    grad_att = flow.tie(grad_att, (DOWN, OUT), ())
+    grad_att = flow.tie(grad_att, (OUT,) if early else (DOWN, OUT), ())
     grad_qkv = attend_back(turned_qk, values, grad_att, *tables, labels)
-    grad_qkv = flow.tie(grad_qkv, (DOWN, GATE_UP), (DOWN, QKV))
+    grad_qkv = flow.tie(grad_qkv, (GATE_UP, OUT) if early else (GATE_UP, OUT, DOWN), (DOWN, QKV))
     grad_normed = dot_nt(grad_qkv, w.qkv)
     grad_norm, gain_one = norm_back(x, scale_one, w.gain_one, grad_normed, features)
     flow.begin(QKV, normed, (grad_qkv, gain_one, gain_two))
-    grad = flow.tie(grad_middle + grad_norm, (QKV, GATE_UP, OUT), (GATE_UP,))
+    grad = flow.tie(grad_middle + grad_norm, (QKV, GATE_UP), (GATE_UP,))
     flow.next_layer()
     return grad
 
@@ -248,8 +257,8 @@
 
 class Arriving:
     order = (
-        ((0, 1, 0, 2, 0, 1, 0, 3, 1, 2, 0), (2, 3), (4, 1), (1, 3), (4, 5, 2, 2)),
-        ((4, 3, 3), (5,), (5, 4), (4,), (5, 5)),
+        ((0, 1, 0, 2, 0, 1, 0, 3, 1, 2, 0), (2, 3), (4, 1), (1, 3), (4, 5, 2), (2,)),
+        ((4, 3, 3), (5,), (5, 4), (4,), (5,), (5,)),
     )
 
     def __init__(self, groups, unpack):
@@ -271,12 +280,12 @@
 
 
 class Flow:
-    def __init__(self, begin):
-        self.begun = begin
+    def __init__(self, begin, low):
+        self.begun, self.low = begin, low
         self.now, self.before, self.done = {}, {}, []
 
     def begin(self, name, lhs, rhs):
-        steps = self.begun(name, lhs, rhs)
+        steps = self.begun(name, lhs, rhs, bool(self.before))
         self.now[name] = (steps, next(steps))
 
     def tie(self, value, now, before):
@@ -396,8 +405,18 @@
         groups = [self.travelled(part) for part in self.packed(weights)]
         self.whole, self.left, self.right = self.order_matrices()
 
+        whole, both = self.whole, self.wide
+
+        def order(a):
+            return dot(a, whole).astype(bf16)
+
+        def order_hidden(a):
+            last = a[:, 2 * both :]
+            sides = [dot(last, self.left).astype(bf16), dot(last, self.right).astype(bf16)]
+            return order(a[:, :both]), order(a[:, both : 2 * both]), jnp.concatenate(sides, axis=0)
+
         def unpack(groups):
-            w = Weights(spread=self.spread)
+            w = Weights(spread=self.spread, order=order, order_hidden=order_hidden)
             for unpacked, pieces in zip((self.attention, self.gate_up, self.down), groups):
                 unpacked(w, pieces)
             return w
@@ -450,9 +469,7 @@
                 pltpu.SemaphoreType.DMA((self.parts * count,)),
             ],
             compiler_params=pltpu.CompilerParams(vmem_limit_bytes=16 * 2**20),
-            cost_estimate=pl.CostEstimate(
-                flops=0, bytes_accessed=4 * shape[0] * shape[1], transcendentals=0
-            ),
+            cost_estimate=pl.CostEstimate(flops=0, bytes_accessed=0, transcendentals=0),
         )(self.arrival, *pieces)
 
     def side_by_side(self, pieces):
@@ -568,35 +585,25 @@
         return got
 
     def emitter(self):
-        whole, half = self.whole, self.wide // 2
-
-        def order(a):
-            return dot(a, whole).astype(bf16)
-
-        def begin(name, lhs, rhs):
+        half = self.wide // 2
+
+        def begin(name, lhs, rhs, last):
             if name == DOWN:
-                last = lhs[:, 2 * self.wide :]
-                both = jnp.concatenate(
-                    [dot(last, self.left).astype(bf16), dot(last, self.right).astype(bf16)], axis=0
-                )
+                one, two, both = lhs
                 sides = jnp.concatenate([rhs[:, :half], rhs[:, half:]], axis=0)
-                terms = [
-                    (order(lhs[:, : self.wide]), rhs),
-                    (order(lhs[:, self.wide : 2 * self.wide]), rhs),
-                    (both, sides),
-                ]
-                return self.reduced(terms)
+                return self.reduced([(one, rhs), (two, rhs), (both, sides)])
             if name == GATE_UP:
-                return self.reduced([(order(lhs), rhs)])
+                return self.reduced([(lhs, rhs)], direct=last)
             if name == OUT:
-                return self.reduced([(order(lhs), rhs)], direct=True)
+                return self.reduced([(lhs, rhs)], direct=True)
             grad_qkv, gain_one, gain_two = rhs
             length = lhs.shape[0]
             gains = jnp.pad(jnp.stack([gain_one, gain_two]), ((0, 14), (0, 0))).astype(bf16)
             ones = (jnp.arange(16)[:, None] == jnp.arange(self.cols_qkv)[None, :] - self.wide_qkv).astype(bf16)
             rhs = jnp.pad(grad_qkv, ((0, 0), (0, self.cols_qkv - self.wide_qkv)))
             rhs = jnp.concatenate([rhs, ones], axis=0)
-            return self.reduced([(order(jnp.concatenate([lhs, gains], axis=0)), rhs)], direct=True)
+            gains = dot(gains, self.whole).astype(bf16)
+            return self.reduced([(jnp.concatenate([lhs, gains], axis=0), rhs)], direct=True)
 
         return begin
 
@@ -645,11 +652,15 @@
         both = [lax.all_gather(part, (SECTION, FSDP), axis=0, tiled=True) for part in weights]
         both = [a.reshape((2, -1) + a.shape[1:]) for a in both]
 
+        def same(a):
+            return a
+
         def layer_of(layer):
             gain_one, query, key, value, out, gain_two, gate, up, down = [a[layer] for a in both]
             return Weights(
                 gain_one=gain_one.astype(f32), gain_two=gain_two.astype(f32), out=out, gate=gate, up=up,
                 down=down, qkv=jnp.concatenate([query, key, value], axis=1), spread=self.spread,
+                order=same, order_hidden=same,
             )
 
         source = Arriving([], None)
@@ -662,7 +673,7 @@
             part = lax.psum_scatter(a, FSDP, scatter_dimension=0, tiled=True)
             return lax.psum(part, SECTION)
 
-        def begin(name, lhs, rhs):
+        def begin(name, lhs, rhs, last):
             if name == QKV:
                 grad_qkv, gain_one, gain_two = rhs
                 yield ()
@@ -709,11 +720,11 @@
     tables = rope_tables(mine(positions))
 
     start = dot(mine(inputs), spread)
+    grad = split_dot(mine(cotangent), spread)
     middle, weights_zero, kept_zero = forward(start, source, 0, labels, tables, features)
-    end, weights_one, kept_one = forward(middle, source, 1, labels, tables, features)
-
-    grad = split_dot(mine(cotangent), spread)
-    flow = Flow(plan.emitter())
+    flow = Flow(plan.emitter(), grad.astype(bf16))
+    end, weights_one, kept_one = forward(middle, source, 1, labels, tables, features, flow)
+
     grad_middle = backward(middle, weights_one, labels, tables, features, kept_one, grad, flow)
     grad_start = backward(start, weights_zero, labels, tables, features, kept_zero, grad_middle, flow)
     sums_one, sums_zero = flow.finished()

time: 672 us -> 673 us (level)
    ppermute x12 -> x15, starting transfers between devices: 18.5 us -> 30.2 us  [reduced(): lax.ppermute(blocks[k], FSDP, [(i, (i + 4 * k) % self.n) for i in range(s...]
    ppermute x8, waiting for transfers between devices: 16.6 us -> 24.6 us  [reduced(): got = (yield lax.ppermute(mine[half // 4:], BOTH, second_route))]
    ppermute x6, waiting for transfers between devices: 23.5 us -> 15.7 us  [travelled(): got = (yield lax.ppermute(line, BOTH, second_route))]
    dot_general x31 -> x33, matrix products: 64.8 us -> 60.1 us  [dot(): return jnp.dot(a, b, preferred_element_type=f32)]
    ppermute x12 -> x15, waiting for transfers between devices: 15.7 us -> 11.9 us  [reduced(): lax.ppermute(blocks[k], FSDP, [(i, (i + 4 * k) % self.n) for i in range(s...]
    unnamed x464 -> x338, local copies, waits for them, and re-layouts: 46.8 us -> 43.1 us
  transfers between devices with their start and end apart: 109 -> 111, of which waited for: 27 -> 25; matrix products, arithmetic and copies ran while one was open for 36% -> 33% of each run, Pallas kernels for 13% -> 13%
where the time goes in v4:
time: 673 us; the launch traced here: 663 us
  matrix products  157 us (23%)
  starting transfers between devices  131 us (19%)
  waiting for transfers between devices  127 us (19%)
  Pallas kernels  86 us (13%)
  local copies, waits for them, and re-layouts  83.4 us (12%)
  other arithmetic  61.7 us (9%)
  between operations  17.1 us (3%)
    dot_general x33, matrix products, dot(): return jnp.dot(a, b, preferred_element_type=f32)  60.1 us
    ppermute x18, starting transfers between devices, travelled(): lax.ppermute(part, FSDP, [(i, (i + 4 * k) % self.n) for i in range(self.n)])  55.9 us
    dot_general x18, matrix products, dot_nt(): lax.dot_general(a, b, (((1,), (1,)), ((), ())), preferred_element_type=f32)  49.7 us
    dot_general x24, matrix products, dot_tn(): lax.dot_general(a, b, (((0,), (0,)), ((), ())), preferred_element_type=f32)  47.5 us
    pallas_call x6, Pallas kernels, assembled(): pl.pallas_call(kernel, out_shape=jax.ShapeDtypeStruct(shape, bf16), in_sp...  43.6 us
    unnamed x338, local copies, waits for them, and re-layouts  43.1 us
    ppermute x8, waiting for transfers between devices, reduced(): got = (yield lax.ppermute(mine[half // 2:], BOTH, first_route))  39.1 us
    ppermute x15, starting transfers between devices, reduced(): lax.ppermute(blocks[k], FSDP, [(i, (i + 4 * k) % self.n) for i in range(s...  30.2 us
  transfers between devices with their start and end apart: 111, of which 25 were waited for; matrix products, arithmetic and copies ran while one was open for 33% of the time, Pallas kernels for 13%

profile of v4, /device:TPU:0, one launch (start us, length us, event | category | flops | bytes accessed | tf_op | source)
XLA Modules:
  0.0 663.3 jit_solution(15843597234510701628)
XLA Ops:
  46.3 4.2 collective-permute-start.7
  55.0 5.3 collective-permute-done.7
  60.3 12.8 %collective-permute-done.8 = bf16[32,5120]{1,0:T(8,128)(2,1)S(1)} collective-permute-done((bf16[32,5120]{1,0:T(8,128)(2,1)S(1)}, bf16[32,5120]{1,0:T(8,128)(2,1)S(1)}, u32[]{:S(2)}, u32[]{:S(2)}) %collective-permute-start.8) | collective-permute-done | bytes 327712 | tf_op jit(solution)/shard_map/ppermute | solution.py:508
  79.6 7.6 %collective-permute-start.13 = (bf16[32,2560]{1,0:T(8,128)(2,1)}, bf16[32,2560]{1,0:T(8,128)(2,1)S(1)}, u32[]{:S(2)}, u32[]{:S(2)}) collective-permute-start(bf16[32,2560]{1,0:T(8,128)(2,1)} %get-tuple-element.207), channel_id=1, source_target_pairs={{0,4},{1,5},{2,6},{3,7},{4,8},{5,9},{6,10},{7,11},{8,12},{9,13},{1... | collective-permute-start | bytes 491528 | tf_op jit(solution)/shard_map/ppermute | solution.py:508
  89.7 5.5 collective-permute-done.10.refs_2_
  95.3 8.5 %collective-permute-start.15 = (bf16[32,2560]{1,0:T(8,128)(2,1)}, bf16[32,2560]{1,0:T(8,128)(2,1)S(1)}, u32[]{:S(2)}, u32[]{:S(2)}) collective-permute-start(bf16[32,2560]{1,0:T(8,128)(2,1)} %get-tuple-element.207), channel_id=1, source_target_pairs={{0,12},{1,13},{2,14},{3,15},{4,0},{5,1},{6,2},{7,3},{8,4},{9,5},{1... | collective-permute-start | bytes 491528 | tf_op jit(solution)/shard_map/ppermute | solution.py:508
  110.6 7.6 %collective-permute-start.21 = (bf16[32,2688]{1,0:T(8,128)(2,1)}, bf16[32,2688]{1,0:T(8,128)(2,1)S(1)}, u32[]{:S(2)}, u32[]{:S(2)}) collective-permute-start(bf16[32,2688]{1,0:T(8,128)(2,1)} %get-tuple-element.220), channel_id=1, source_target_pairs={{0,4},{1,5},{2,6},{3,7},{4,8},{5,9},{6,10},{7,11},{8,12},{9,13},{1... | collective-permute-start | bytes 516104 | tf_op jit(solution)/shard_map/ppermute | solution.py:508
  122.5 10.1 %shard_map.212 = bf16[1024,2688]{1,0:T(8,128)(2,1)S(1)} custom-call(s32[32]{0:T(128)S(1)} %multiply_add_fusion.1.index, bf16[128,2688]{1,0:T(8,128)(2,1)S(1)} %constant_dynamic-update-slice_fusion.6.refs_0_, bf16[128,2688]{1,0:T(8,128)(2,1)S(1)} %collective-permute-done.6.refs_1_, bf16[128,2688]{1,0:T(8,128)(2,1)S(1)} %collective-permute-done.10.refs_2_, ...), custom_call_target="tpu_custom_call" | custom-call | tf_op jit(solution)/shard_map/pallas_call | solution.py:461
  136.0 3.4 fusion.55
  144.8 3.2 copy.72.qkv
  149.8 8.9 %shard_map.213 = (bf16[384,960]{1,0:T(8,128)(2,1)S(1)}, bf16[384,1280]{1,0:T(8,128)(2,1)S(1)}, bf16[384,320]{1,0:T(8,128)(2,1)S(1)}) custom-call(f32[384,1600]{1,0:T(8,128)S(1)} %copy-done.5, f32[384,128]{1,0:T(8,128)S(1)} %get-tuple-element.496.cosine, f32[384,128]{1,0:T(8,128)S(1)} %get-tuple-element.497.sine, s32[384,1]{1,0:T(8,128)S(1)} %copy.73.row_labels, ...), custom_call_target="tpu_custom_call" | custom-call | tf_op jit(solution)/shard_map/pallas_call | solution.py:124
  170.8 3.4 collective-permute-start.32
  179.1 5.7 shard_map.214
  188.8 4.0 multiply_convert_fusion.5
  203.9 6.3 shard_map.215
  216.9 10.6 %collective-permute-done.40.refs_1_ = bf16[128,5120]{1,0:T(8,128)(2,1)} collective-permute-done((bf16[128,5120]{1,0:T(8,128)(2,1)S(1)}, bf16[128,5120]{1,0:T(8,128)(2,1)}, u32[]{:S(2)}, u32[]{:S(2)}) %collective-permute-start.40) | collective-permute-done | bytes 1310752 | tf_op jit(solution)/shard_map/ppermute | solution.py:515
  227.9 7.3 %collective-permute-start.47 = (bf16[32,2560]{1,0:T(8,128)(2,1)S(1)}, bf16[32,2560]{1,0:T(8,128)(2,1)S(1)}, u32[]{:S(2)}, u32[]{:S(2)}) collective-permute-start(bf16[32,2560]{1,0:T(8,128)(2,1)S(1)} %copy-done.89), channel_id=1, source_target_pairs={{0,4},{1,5},{2,6},{3,7},{4,8},{5,9},{6,10},{7,11},{8,12},{9,13},{1... | collective-permute-start | bytes 491528 | tf_op jit(solution)/shard_map/ppermute | solution.py:508
  240.4 10.1 %shard_map.216 = bf16[1024,2688]{1,0:T(8,128)(2,1)S(1)} custom-call(s32[32]{0:T(128)S(1)} %multiply_add_fusion.1.index, bf16[128,2688]{1,0:T(8,128)(2,1)} %constant_dynamic-update-slice_fusion.18.refs_0_, bf16[128,2688]{1,0:T(8,128)(2,1)S(1)} %collective-permute-done.30.refs_1_, bf16[128,2688]{1,0:T(8,128)(2,1)S(1)} %collective-permute-done.41.refs_2_, ...), custom_call_target="tpu_custom_call" | custom-call | tf_op jit(solution)/shard_map/pallas_call | solution.py:461
  251.3 3.4 fusion.51
  258.5 3.6 copy.74.qkv
  263.8 8.9 %shard_map.217 = (bf16[384,960]{1,0:T(8,128)(2,1)S(1)}, bf16[384,1280]{1,0:T(8,128)(2,1)S(1)}, bf16[384,320]{1,0:T(8,128)(2,1)S(1)}) custom-call(f32[384,1600]{1,0:T(8,128)S(1)} %copy-done.6, f32[384,128]{1,0:T(8,128)S(1)} %get-tuple-element.496.cosine, f32[384,128]{1,0:T(8,128)S(1)} %get-tuple-element.497.sine, s32[384,1]{1,0:T(8,128)S(1)} %copy.73.row_labels, ...), custom_call_target="tpu_custom_call" | custom-call | tf_op jit(solution)/shard_map/pallas_call | solution.py:124
  286.2 5.5 shard_map.218
  294.0 4.0 multiply_convert_fusion.4
  313.6 5.9 shard_map.219
  319.6 7.5 %fusion = bf16[512,2560]{1,0:T(8,128)(2,1)} fusion(f32[512,512]{1,0:T(8,128)} %fusion.153, f32[512,1024]{1,0:T(8,128)} %fusion.193, f32[512,1024]{1,0:T(8,128)} %fusion.195, bf16[512,2560]{1,0:T(8,128)(2,1)} %collective-permute-done.64), kind=kLoop, calls=%fused_computation.5 | loop fusion | flops 6553600 | bytes 10485760 | tf_op jit(solution)/shard_map/convert_element_type | solution.py:567
  329.4 5.7 multiply_convert_fusion.2
  335.1 11.2 %collective-permute-done.65 = bf16[256,2560]{1,0:T(8,128)(2,1)} collective-permute-done((bf16[256,2560]{1,0:T(8,128)(2,1)S(1)}, bf16[256,2560]{1,0:T(8,128)(2,1)}, u32[]{:S(2)}, u32[]{:S(2)}) %collective-permute-start.65) | collective-permute-done | bytes 1310752 | tf_op jit(solution)/shard_map/ppermute | solution.py:568
  359.4 4.1 collective-permute-done.67
  363.4 5.6 add_convert_fusion.1
  375.0 3.9 fusion.122.grad_att
  384.3 12.4 %shard_map.220 = bf16[384,1600]{1,0:T(8,128)(2,1)S(1)} custom-call(bf16[384,1280]{1,0:T(8,128)(2,1)S(1)} %copy-done.14, bf16[384,320]{1,0:T(8,128)(2,1)S(1)} %copy-done.21, bf16[384,960]{1,0:T(8,128)(2,1)S(1)} %fusion.122.grad_att, f32[384,128]{1,0:T(8,128)S(1)} %get-tuple-element.496.cosine, f32[384,128]{1,0:T(8,128)S(1)} %get-tuple-element.497.sine, ...), custom_call_target="tpu_custom_call" | custom-call | tf_op jit(solution)/shard_map/pallas_call | solution.py:178
  396.6 13.0 %collective-permute-done.70 = bf16[256,1024]{1,0:T(8,128)(2,1)S(1)} collective-permute-done((bf16[256,1024]{1,0:T(8,128)(2,1)S(1)}, bf16[256,1024]{1,0:T(8,128)(2,1)S(1)}, u32[]{:S(2)}, u32[]{:S(2)}) %collective-permute-start.70) | collective-permute-done | bytes 524320 | tf_op jit(solution)/shard_map/ppermute | solution.py:568
  423.5 10.8 %collective-permute-done.72 = bf16[128,5120]{1,0:T(8,128)(2,1)S(1)} collective-permute-done((bf16[128,5120]{1,0:T(8,128)(2,1)S(1)}, bf16[128,5120]{1,0:T(8,128)(2,1)S(1)}, u32[]{:S(2)}, u32[]{:S(2)}) %collective-permute-start.72) | collective-permute-done | bytes 1310752 | tf_op jit(solution)/shard_map/ppermute | solution.py:570
  446.3 5.7 multiply_convert_fusion
  452.0 5.9 collective-permute-done.74
  460.5 4.8 convolution_convert_fusion
  478.1 4.8 fusion.10
  492.6 4.9 add_convert_fusion
  501.3 4.8 fusion.123.grad_att
  526.5 12.2 %shard_map.221 = bf16[384,1600]{1,0:T(8,128)(2,1)S(1)} custom-call(bf16[384,1280]{1,0:T(8,128)(2,1)S(1)} %copy-done.12, bf16[384,320]{1,0:T(8,128)(2,1)S(1)} %copy-done.19, bf16[384,960]{1,0:T(8,128)(2,1)S(1)} %copy-done.15, f32[384,128]{1,0:T(8,128)S(1)} %get-tuple-element.496.cosine, f32[384,128]{1,0:T(8,128)S(1)} %get-tuple-element.497.sine, ...), custom_call_target="tpu_custom_call" | custom-call | tf_op jit(solution)/shard_map/pallas_call | solution.py:178
  538.8 9.1 %collective-permute-done.84 = bf16[256,1024]{1,0:T(8,128)(2,1)} collective-permute-done((bf16[256,1024]{1,0:T(8,128)(2,1)}, bf16[256,1024]{1,0:T(8,128)(2,1)}, u32[]{:S(2)}, u32[]{:S(2)}) %collective-permute-start.84) | collective-permute-done | bytes 524320 | tf_op jit(solution)/shard_map/ppermute | solution.py:568
  547.9 5.6 multiply_reduce_fusion.1
  568.4 4.0 subtract_add_fusion
  573.5 6.6 collective-permute-done.90
  611.7 5.7 collective-permute-done.102
  617.4 7.9 %collective-permute-start.95 = (bf16[32,1664]{1,0:T(8,128)(2,1)S(1)}, bf16[32,1664]{1,0:T(8,128)(2,1)S(1)}, u32[]{:S(2)}, u32[]{:S(2)}) collective-permute-start(bf16[32,1664]{1,0:T(8,128)(2,1)S(1)} %get-tuple-element.449), channel_id=1, source_target_pairs={{0,4},{1,5},{2,6},{3,7},{4,8},{5,9},{6,10},{7,11},{8,12},{9,13},{1... | collective-permute-start | bytes 319496 | tf_op jit(solution)/shard_map/ppermute | solution.py:579
  625.3 3.4 collective-permute-start.96
  632.0 3.9 collective-permute-done.96
  (772 shorter events, 327.3 us)
Async XLA Ops:
  7.2 531.6 %reduce-scatter.4.cloned.1.call-start = ((), (), s32[]{:S(2)}) async-start(), calls=%async_computation.3 | async-start | bytes 819200 | tf_op jit(solution)/shard_map/reduce_scatter | solution.py:584
  50.5 22.5 %collective-permute-start.8 = (bf16[32,5120]{1,0:T(8,128)(2,1)S(1)}, bf16[32,5120]{1,0:T(8,128)(2,1)S(1)}, u32[]{:S(2)}, u32[]{:S(2)}) collective-permute-start(bf16[32,5120]{1,0:T(8,128)(2,1)S(1)} %get-tuple-element.197), channel_id=1, source_target_pairs={{0,8},{1,9},{2,10},{3,11},{4,12},{5,13},{6,14},{7,15},{8,0},{9,1},... | collective-permute-start | bytes 983048 | tf_op jit(solution)/shard_map/ppermute | solution.py:508
  52.1 20.9 %collective-permute-start.9 = (bf16[32,5120]{1,0:T(8,128)(2,1)S(1)}, bf16[32,5120]{1,0:T(8,128)(2,1)S(1)}, u32[]{:S(2)}, u32[]{:S(2)}) collective-permute-start(bf16[32,5120]{1,0:T(8,128)(2,1)S(1)} %get-tuple-element.197), channel_id=1, source_target_pairs={{0,12},{1,13},{2,14},{3,15},{4,0},{5,1},{6,2},{7,3},{8,4},{9,5},{1... | collective-permute-start | bytes 983048 | tf_op jit(solution)/shard_map/ppermute | solution.py:508
  75.3 33.2 %collective-permute-start.12 = (bf16[128,5120]{1,0:T(8,128)(2,1)}, bf16[128,5120]{1,0:T(8,128)(2,1)}, u32[]{:S(2)}, u32[]{:S(2)}) collective-permute-start(bf16[128,5120]{1,0:T(8,128)(2,1)} %constant_dynamic-update-slice_fusion.10.refs_0_), channel_id=1, source_target_pairs={{0,1},{1,0},{2,3},{3,2},{4,5},{5,4},{6,7},{7,6},{8,9},{9,8},{10,11... | collective-permute-start | bytes 3932168 | tf_op jit(solution)/shard_map/ppermute | solution.py:515
  77.4 29.5 %collective-permute-start.11 = (bf16[128,2688]{1,0:T(8,128)(2,1)S(1)}, bf16[128,2688]{1,0:T(8,128)(2,1)}, u32[]{:S(2)}, u32[]{:S(2)}) collective-permute-start(bf16[128,2688]{1,0:T(8,128)(2,1)S(1)} %collective-permute-done.6.refs_1_), channel_id=1, source_target_pairs={{0,2},{1,3},{2,0},{3,1},{4,6},{5,7},{6,4},{7,5},{8,10},{9,11},{10,... | collective-permute-start | bytes 2064392 | tf_op jit(solution)/shard_map/ppermute | solution.py:518
  79.6 29.5 %collective-permute-start.13 = (bf16[32,2560]{1,0:T(8,128)(2,1)}, bf16[32,2560]{1,0:T(8,128)(2,1)S(1)}, u32[]{:S(2)}, u32[]{:S(2)}) collective-permute-start(bf16[32,2560]{1,0:T(8,128)(2,1)} %get-tuple-element.207), channel_id=1, source_target_pairs={{0,4},{1,5},{2,6},{3,7},{4,8},{5,9},{6,10},{7,11},{8,12},{9,13},{1... | collective-permute-start | bytes 491528 | tf_op jit(solution)/shard_map/ppermute | solution.py:508
  87.2 22.8 %collective-permute-start.14 = (bf16[32,2560]{1,0:T(8,128)(2,1)}, bf16[32,2560]{1,0:T(8,128)(2,1)S(1)}, u32[]{:S(2)}, u32[]{:S(2)}) collective-permute-start(bf16[32,2560]{1,0:T(8,128)(2,1)} %get-tuple-element.207), channel_id=1, source_target_pairs={{0,8},{1,9},{2,10},{3,11},{4,12},{5,13},{6,14},{7,15},{8,0},{9,1},... | collective-permute-start | bytes 491528 | tf_op jit(solution)/shard_map/ppermute | solution.py:508
  109.1 53.1 %collective-permute-start.24 = (bf16[128,5120]{1,0:T(8,128)(2,1)}, bf16[128,5120]{1,0:T(8,128)(2,1)}, u32[]{:S(2)}, u32[]{:S(2)}) collective-permute-start(bf16[128,5120]{1,0:T(8,128)(2,1)} %constant_dynamic-update-slice_fusion.10.refs_0_), channel_id=1, source_target_pairs={{0,2},{1,3},{2,0},{3,1},{4,6},{5,7},{6,4},{7,5},{8,10},{9,11},{10,... | collective-permute-start | bytes 3932168 | tf_op jit(solution)/shard_map/ppermute | solution.py:513
  110.6 32.1 %collective-permute-start.21 = (bf16[32,2688]{1,0:T(8,128)(2,1)}, bf16[32,2688]{1,0:T(8,128)(2,1)S(1)}, u32[]{:S(2)}, u32[]{:S(2)}) collective-permute-start(bf16[32,2688]{1,0:T(8,128)(2,1)} %get-tuple-element.220), channel_id=1, source_target_pairs={{0,4},{1,5},{2,6},{3,7},{4,8},{5,9},{6,10},{7,11},{8,12},{9,13},{1... | collective-permute-start | bytes 516104 | tf_op jit(solution)/shard_map/ppermute | solution.py:508
  118.2 25.1 %collective-permute-start.22 = (bf16[32,2688]{1,0:T(8,128)(2,1)}, bf16[32,2688]{1,0:T(8,128)(2,1)}, u32[]{:S(2)}, u32[]{:S(2)}) collective-permute-start(bf16[32,2688]{1,0:T(8,128)(2,1)} %get-tuple-element.220), channel_id=1, source_target_pairs={{0,8},{1,9},{2,10},{3,11},{4,12},{5,13},{6,14},{7,15},{8,0},{9,1},... | collective-permute-start | bytes 516104 | tf_op jit(solution)/shard_map/ppermute | solution.py:508
  119.8 19.6 %collective-permute-start.20 = (bf16[128,2560]{1,0:T(8,128)(2,1)S(1)}, bf16[128,2560]{1,0:T(8,128)(2,1)S(1)}, u32[]{:S(2)}, u32[]{:S(2)}) collective-permute-start(bf16[128,2560]{1,0:T(8,128)(2,1)S(1)} %constant_dynamic-update-slice_fusion.14.refs_0_), channel_id=1, source_target_pairs={{0,1},{1,0},{2,3},{3,2},{4,5},{5,4},{6,7},{7,6},{8,9},{9,8},{10,11... | collective-permute-start | bytes 1966088 | tf_op jit(solution)/shard_map/ppermute | solution.py:515
  121.3 40.9 %collective-permute-start.25 = (bf16[128,5120]{1,0:T(8,128)(2,1)}, bf16[128,5120]{1,0:T(8,128)(2,1)}, u32[]{:S(2)}, u32[]{:S(2)}) collective-permute-start(bf16[128,5120]{1,0:T(8,128)(2,1)} %collective-permute-done.12.refs_1_), channel_id=1, source_target_pairs={{0,2},{1,3},{2,0},{3,1},{4,6},{5,7},{6,4},{7,5},{8,10},{9,11},{10,... | collective-permute-start | bytes 3932168 | tf_op jit(solution)/shard_map/ppermute | solution.py:518
  143.3 25.5 %collective-permute-start.26 = (bf16[128,5120]{1,0:T(8,128)(2,1)}, bf16[128,5120]{1,0:T(8,128)(2,1)}, u32[]{:S(2)}, u32[]{:S(2)}) collective-permute-start(bf16[128,5120]{1,0:T(8,128)(2,1)} %constant_dynamic-update-slice_fusion.10.refs_0_), channel_id=1, source_target_pairs={{0,16},{16,0},{1,17},{17,1},{2,18},{18,2},{3,19},{19,3},{4,20},{20... | collective-permute-start | bytes 3932168 | tf_op jit(solution)/shard_map/ppermute | solution.py:372
  143.4 26.4 %collective-permute-start.27 = (bf16[128,5120]{1,0:T(8,128)(2,1)}, bf16[128,5120]{1,0:T(8,128)(2,1)}, u32[]{:S(2)}, u32[]{:S(2)}) collective-permute-start(bf16[128,5120]{1,0:T(8,128)(2,1)} %collective-permute-done.12.refs_1_), channel_id=1, source_target_pairs={{0,16},{16,0},{1,17},{17,1},{2,18},{18,2},{3,19},{19,3},{4,20},{20... | collective-permute-start | bytes 3932168 | tf_op jit(solution)/shard_map/ppermute | solution.py:372
  168.8 27.2 %collective-permute-start.34 = (bf16[128,2560]{1,0:T(8,128)(2,1)S(1)}, bf16[128,2560]{1,0:T(8,128)(2,1)S(1)}, u32[]{:S(2)}, u32[]{:S(2)}) collective-permute-start(bf16[128,2560]{1,0:T(8,128)(2,1)S(1)} %copy-done.10), channel_id=1, source_target_pairs={{0,2},{1,3},{2,0},{3,1},{4,6},{5,7},{6,4},{7,5},{8,10},{9,11},{10,... | collective-permute-start | bytes 1966088 | tf_op jit(solution)/shard_map/ppermute | solution.py:513
  169.7 23.0 %collective-permute-start.31 = (bf16[32,5120]{1,0:T(8,128)(2,1)S(1)}, bf16[32,5120]{1,0:T(8,128)(2,1)S(1)}, u32[]{:S(2)}, u32[]{:S(2)}) collective-permute-start(bf16[32,5120]{1,0:T(8,128)(2,1)S(1)} %copy-done.73), channel_id=1, source_target_pairs={{0,4},{1,5},{2,6},{3,7},{4,8},{5,9},{6,10},{7,11},{8,12},{9,13},{1... | collective-permute-start | bytes 983048 | tf_op jit(solution)/shard_map/ppermute | solution.py:508
  170.8 24.4 %collective-permute-start.32 = (bf16[32,5120]{1,0:T(8,128)(2,1)S(1)}, bf16[32,5120]{1,0:T(8,128)(2,1)S(1)}, u32[]{:S(2)}, u32[]{:S(2)}) collective-permute-start(bf16[32,5120]{1,0:T(8,128)(2,1)S(1)} %copy-done.73), channel_id=1, source_target_pairs={{0,8},{1,9},{2,10},{3,11},{4,12},{5,13},{6,14},{7,15},{8,0},{9,1},... | collective-permute-start | bytes 983048 | tf_op jit(solution)/shard_map/ppermute | solution.py:508
  174.2 21.0 %collective-permute-start.33 = (bf16[32,5120]{1,0:T(8,128)(2,1)S(1)}, bf16[32,5120]{1,0:T(8,128)(2,1)S(1)}, u32[]{:S(2)}, u32[]{:S(2)}) collective-permute-start(bf16[32,5120]{1,0:T(8,128)(2,1)S(1)} %copy-done.73), channel_id=1, source_target_pairs={{0,12},{1,13},{2,14},{3,15},{4,0},{5,1},{6,2},{7,3},{8,4},{9,5},{1... | collective-permute-start | bytes 983048 | tf_op jit(solution)/shard_map/ppermute | solution.py:508
  195.2 32.2 %collective-permute-start.41 = (bf16[128,2688]{1,0:T(8,128)(2,1)}, bf16[128,2688]{1,0:T(8,128)(2,1)S(1)}, u32[]{:S(2)}, u32[]{:S(2)}) collective-permute-start(bf16[128,2688]{1,0:T(8,128)(2,1)} %constant_dynamic-update-slice_fusion.18.refs_0_), channel_id=1, source_target_pairs={{0,2},{1,3},{2,0},{3,1},{4,6},{5,7},{6,4},{7,5},{8,10},{9,11},{10,... | collective-permute-start | bytes 2064392 | tf_op jit(solution)/shard_map/ppermute | solution.py:513
  198.8 37.2 %collective-permute-start.43 = (bf16[128,2688]{1,0:T(8,128)(2,1)}, bf16[128,2688]{1,0:T(8,128)(2,1)S(1)}, u32[]{:S(2)}, u32[]{:S(2)}) collective-permute-start(bf16[128,2688]{1,0:T(8,128)(2,1)} %constant_dynamic-update-slice_fusion.18.refs_0_), channel_id=1, source_target_pairs={{0,16},{16,0},{1,17},{17,1},{2,18},{18,2},{3,19},{19,3},{4,20},{20... | collective-permute-start | bytes 2064392 | tf_op jit(solution)/shard_map/ppermute | solution.py:372
  199.3 28.1 %collective-permute-start.42 = (bf16[128,2688]{1,0:T(8,128)(2,1)S(1)}, bf16[128,2688]{1,0:T(8,128)(2,1)S(1)}, u32[]{:S(2)}, u32[]{:S(2)}) collective-permute-start(bf16[128,2688]{1,0:T(8,128)(2,1)S(1)} %collective-permute-done.30.refs_1_), channel_id=1, source_target_pairs={{0,2},{1,3},{2,0},{3,1},{4,6},{5,7},{6,4},{7,5},{8,10},{9,11},{10,... | collective-permute-start | bytes 2064392 | tf_op jit(solution)/shard_map/ppermute | solution.py:518
  200.2 36.0 %collective-permute-start.44 = (bf16[128,2688]{1,0:T(8,128)(2,1)S(1)}, bf16[128,2688]{1,0:T(8,128)(2,1)S(1)}, u32[]{:S(2)}, u32[]{:S(2)}) collective-permute-start(bf16[128,2688]{1,0:T(8,128)(2,1)S(1)} %collective-permute-done.30.refs_1_), channel_id=1, source_target_pairs={{0,16},{16,0},{1,17},{17,1},{2,18},{18,2},{3,19},{19,3},{4,20},{20... | collective-permute-start | bytes 2064392 | tf_op jit(solution)/shard_map/ppermute | solution.py:372
  200.2 27.2 %collective-permute-start.40 = (bf16[128,5120]{1,0:T(8,128)(2,1)S(1)}, bf16[128,5120]{1,0:T(8,128)(2,1)}, u32[]{:S(2)}, u32[]{:S(2)}) collective-permute-start(bf16[128,5120]{1,0:T(8,128)(2,1)S(1)} %constant_dynamic-update-slice_fusion.22.refs_0_), channel_id=1, source_target_pairs={{0,1},{1,0},{2,3},{3,2},{4,5},{5,4},{6,7},{7,6},{8,9},{9,8},{10,11... | collective-permute-start | bytes 3932168 | tf_op jit(solution)/shard_map/ppermute | solution.py:515
  227.9 26.8 %collective-permute-start.47 = (bf16[32,2560]{1,0:T(8,128)(2,1)S(1)}, bf16[32,2560]{1,0:T(8,128)(2,1)S(1)}, u32[]{:S(2)}, u32[]{:S(2)}) collective-permute-start(bf16[32,2560]{1,0:T(8,128)(2,1)S(1)} %copy-done.89), channel_id=1, source_target_pairs={{0,4},{1,5},{2,6},{3,7},{4,8},{5,9},{6,10},{7,11},{8,12},{9,13},{1... | collective-permute-start | bytes 491528 | tf_op jit(solution)/shard_map/ppermute | solution.py:508
  238.3 36.4 %collective-permute-start.51 = (bf16[128,5120]{1,0:T(8,128)(2,1)S(1)}, bf16[128,5120]{1,0:T(8,128)(2,1)}, u32[]{:S(2)}, u32[]{:S(2)}) collective-permute-start(bf16[128,5120]{1,0:T(8,128)(2,1)S(1)} %constant_dynamic-update-slice_fusion.22.refs_0_), channel_id=1, source_target_pairs={{0,2},{1,3},{2,0},{3,1},{4,6},{5,7},{6,4},{7,5},{8,10},{9,11},{10,... | collective-permute-start | bytes 3932168 | tf_op jit(solution)/shard_map/ppermute | solution.py:513
  239.2 37.9 %collective-permute-start.52 = (bf16[128,5120]{1,0:T(8,128)(2,1)}, bf16[128,5120]{1,0:T(8,128)(2,1)}, u32[]{:S(2)}, u32[]{:S(2)}) collective-permute-start(bf16[128,5120]{1,0:T(8,128)(2,1)} %collective-permute-done.40.refs_1_), channel_id=1, source_target_pairs={{0,2},{1,3},{2,0},{3,1},{4,6},{5,7},{6,4},{7,5},{8,10},{9,11},{10,... | collective-permute-start | bytes 3932168 | tf_op jit(solution)/shard_map/ppermute | solution.py:518
  258.0 26.6 %collective-permute-start.53 = (bf16[128,5120]{1,0:T(8,128)(2,1)S(1)}, bf16[128,5120]{1,0:T(8,128)(2,1)}, u32[]{:S(2)}, u32[]{:S(2)}) collective-permute-start(bf16[128,5120]{1,0:T(8,128)(2,1)S(1)} %constant_dynamic-update-slice_fusion.22.refs_0_), channel_id=1, source_target_pairs={{0,16},{16,0},{1,17},{17,1},{2,18},{18,2},{3,19},{19,3},{4,20},{20... | collective-permute-start | bytes 3932168 | tf_op jit(solution)/shard_map/ppermute | solution.py:372
  258.0 27.8 %collective-permute-start.54 = (bf16[128,5120]{1,0:T(8,128)(2,1)}, bf16[128,5120]{1,0:T(8,128)(2,1)}, u32[]{:S(2)}, u32[]{:S(2)}) collective-permute-start(bf16[128,5120]{1,0:T(8,128)(2,1)} %collective-permute-done.40.refs_1_), channel_id=1, source_target_pairs={{0,16},{16,0},{1,17},{17,1},{2,18},{18,2},{3,19},{19,3},{4,20},{20... | collective-permute-start | bytes 3932168 | tf_op jit(solution)/shard_map/ppermute | solution.py:372
  372.1 37.5 %collective-permute-start.69 = (bf16[256,5120]{1,0:T(8,128)(2,1)}, bf16[256,5120]{1,0:T(8,128)(2,1)}, u32[]{:S(2)}, u32[]{:S(2)}) collective-permute-start(bf16[256,5120]{1,0:T(8,128)(2,1)} %slice.539), channel_id=1, source_target_pairs={{0,2},{1,3},{2,0},{3,1},{4,6},{5,7},{6,4},{7,5},{8,10},{9,11},{10,... | collective-permute-start | bytes 7864328 | tf_op jit(solution)/shard_map/ppermute | solution.py:568
  381.7 27.9 %collective-permute-start.70 = (bf16[256,1024]{1,0:T(8,128)(2,1)S(1)}, bf16[256,1024]{1,0:T(8,128)(2,1)S(1)}, u32[]{:S(2)}, u32[]{:S(2)}) collective-permute-start(bf16[256,1024]{1,0:T(8,128)(2,1)S(1)} %slice.541), channel_id=1, source_target_pairs={{0,2},{1,3},{2,0},{3,1},{4,6},{5,7},{6,4},{7,5},{8,10},{9,11},{10,... | collective-permute-start | bytes 1572872 | tf_op jit(solution)/shard_map/ppermute | solution.py:568
  413.5 20.8 %collective-permute-start.71 = (bf16[512,1664]{1,0:T(8,128)(2,1)S(1)}, bf16[512,1664]{1,0:T(8,128)(2,1)S(1)}, u32[]{:S(2)}, u32[]{:S(2)}) collective-permute-start(bf16[512,1664]{1,0:T(8,128)(2,1)S(1)} %convolution_convert_fusion.3), channel_id=1, source_target_pairs={{0,16},{16,0},{1,17},{17,1},{2,18},{18,2},{3,19},{19,3},{4,20},{20... | collective-permute-start | bytes 5111816 | tf_op jit(solution)/shard_map/ppermute | solution.py:372
  438.0 19.8 %collective-permute-start.73 = (bf16[512,2560]{1,0:T(8,128)(2,1)S(1)}, bf16[512,2560]{1,0:T(8,128)(2,1)S(1)}, u32[]{:S(2)}, u32[]{:S(2)}) collective-permute-start(bf16[512,2560]{1,0:T(8,128)(2,1)S(1)} %pad_maximum_fusion.1), channel_id=1, source_target_pairs={{0,16},{16,0},{1,17},{17,1},{2,18},{18,2},{3,19},{19,3},{4,20},{20... | collective-permute-start | bytes 7864328 | tf_op jit(solution)/shard_map/ppermute | solution.py:372
  465.3 25.1 %collective-permute-start.76 = (bf16[512,5120]{1,0:T(8,128)(2,1)}, bf16[512,5120]{1,0:T(8,128)(2,1)}, u32[]{:S(2)}, u32[]{:S(2)}) collective-permute-start(bf16[512,5120]{1,0:T(8,128)(2,1)} %convolution_convert_fusion), channel_id=1, source_target_pairs={{0,16},{16,0},{1,17},{17,1},{2,18},{18,2},{3,19},{19,3},{4,20},{20... | collective-permute-start | bytes 15728648 | tf_op jit(solution)/shard_map/ppermute | solution.py:372
  466.5 107.0 %reduce-scatter.6.cloned.1.call-start = ((), (), s32[]{:S(2)}) async-start(), calls=%async_computation.4 | async-start | bytes 1638400 | tf_op jit(solution)/shard_map/reduce_scatter | solution.py:584
  489.4 19.8 %collective-permute-start.81 = (bf16[256,2560]{1,0:T(8,128)(2,1)S(1)}, bf16[256,2560]{1,0:T(8,128)(2,1)}, u32[]{:S(2)}, u32[]{:S(2)}) collective-permute-start(bf16[256,2560]{1,0:T(8,128)(2,1)S(1)} %slice.554), channel_id=1, source_target_pairs={{0,2},{1,3},{2,0},{3,1},{4,6},{5,7},{6,4},{7,5},{8,10},{9,11},{10,... | collective-permute-start | bytes 3932168 | tf_op jit(solution)/shard_map/ppermute | solution.py:568
  500.6 47.3 %collective-permute-start.83 = (bf16[256,5120]{1,0:T(8,128)(2,1)}, bf16[256,5120]{1,0:T(8,128)(2,1)}, u32[]{:S(2)}, u32[]{:S(2)}) collective-permute-start(bf16[256,5120]{1,0:T(8,128)(2,1)} %slice.555), channel_id=1, source_target_pairs={{0,2},{1,3},{2,0},{3,1},{4,6},{5,7},{6,4},{7,5},{8,10},{9,11},{10,... | collective-permute-start | bytes 7864328 | tf_op jit(solution)/shard_map/ppermute | solution.py:568
  512.5 35.4 %collective-permute-start.84 = (bf16[256,1024]{1,0:T(8,128)(2,1)}, bf16[256,1024]{1,0:T(8,128)(2,1)}, u32[]{:S(2)}, u32[]{:S(2)}) collective-permute-start(bf16[256,1024]{1,0:T(8,128)(2,1)} %slice.556), channel_id=1, source_target_pairs={{0,2},{1,3},{2,0},{3,1},{4,6},{5,7},{6,4},{7,5},{8,10},{9,11},{10,... | collective-permute-start | bytes 1572872 | tf_op jit(solution)/shard_map/ppermute | solution.py:568
  517.5 30.4 %collective-permute-start.85 = (bf16[128,2560]{1,0:T(8,128)(2,1)}, bf16[128,2560]{1,0:T(8,128)(2,1)}, u32[]{:S(2)}, u32[]{:S(2)}) collective-permute-start(bf16[128,2560]{1,0:T(8,128)(2,1)} %slice.558), channel_id=1, source_target_pairs={{0,1},{1,0},{2,3},{3,2},{4,5},{5,4},{6,7},{7,6},{8,9},{9,8},{10,11... | collective-permute-start | bytes 1966088 | tf_op jit(solution)/shard_map/ppermute | solution.py:570
  519.9 89.0 %reduce-scatter.8.cloned.1.call-start = ((), (), s32[]{:S(2)}) async-start(), calls=%async_computation.5 | async-start | bytes 819200 | tf_op jit(solution)/shard_map/reduce_scatter | solution.py:584
  519.9 18.8 %collective-permute-start.87 = (bf16[32,1664]{1,0:T(8,128)(2,1)}, bf16[32,1664]{1,0:T(8,128)(2,1)}, u32[]{:S(2)}, u32[]{:S(2)}) collective-permute-start(bf16[32,1664]{1,0:T(8,128)(2,1)} %get-tuple-element.451), channel_id=1, source_target_pairs={{0,8},{1,9},{2,10},{3,11},{4,12},{5,13},{6,14},{7,15},{8,0},{9,1},... | collective-permute-start | bytes 319496 | tf_op jit(solution)/shard_map/ppermute | solution.py:579
  556.7 23.4 %collective-permute-start.89 = (bf16[512,1664]{1,0:T(8,128)(2,1)}, bf16[512,1664]{1,0:T(8,128)(2,1)}, u32[]{:S(2)}, u32[]{:S(2)}) collective-permute-start(bf16[512,1664]{1,0:T(8,128)(2,1)} %convolution_convert_fusion.2), channel_id=1, source_target_pairs={{0,16},{16,0},{1,17},{17,1},{2,18},{18,2},{3,19},{19,3},{4,20},{20... | collective-permute-start | bytes 5111816 | tf_op jit(solution)/shard_map/ppermute | solution.py:372
  567.2 30.7 %collective-permute-start.93 = (bf16[128,1024]{1,0:T(8,128)(2,1)}, bf16[128,1024]{1,0:T(8,128)(2,1)}, u32[]{:S(2)}, u32[]{:S(2)}) collective-permute-start(bf16[128,1024]{1,0:T(8,128)(2,1)} %slice.569), channel_id=1, source_target_pairs={{0,1},{1,0},{2,3},{3,2},{4,5},{5,4},{6,7},{7,6},{8,9},{9,8},{10,11... | collective-permute-start | bytes 786440 | tf_op jit(solution)/shard_map/ppermute | solution.py:570
  590.4 19.8 %collective-permute-start.101 = (bf16[32,5120]{1,0:T(8,128)(2,1)}, bf16[32,5120]{1,0:T(8,128)(2,1)}, u32[]{:S(2)}, u32[]{:S(2)}) collective-permute-start(bf16[32,5120]{1,0:T(8,128)(2,1)} %get-tuple-element.426), channel_id=1, source_target_pairs={{0,4},{1,5},{2,6},{3,7},{4,8},{5,9},{6,10},{7,11},{8,12},{9,13},{1... | collective-permute-start | bytes 983048 | tf_op jit(solution)/shard_map/ppermute | solution.py:579
  591.6 25.8 %collective-permute-start.102 = (bf16[32,5120]{1,0:T(8,128)(2,1)}, bf16[32,5120]{1,0:T(8,128)(2,1)}, u32[]{:S(2)}, u32[]{:S(2)}) collective-permute-start(bf16[32,5120]{1,0:T(8,128)(2,1)} %get-tuple-element.425), channel_id=1, source_target_pairs={{0,8},{1,9},{2,10},{3,11},{4,12},{5,13},{6,14},{7,15},{8,0},{9,1},... | collective-permute-start | bytes 983048 | tf_op jit(solution)/shard_map/ppermute | solution.py:579
  592.5 32.7 %collective-permute-start.103 = (bf16[32,5120]{1,0:T(8,128)(2,1)}, bf16[32,5120]{1,0:T(8,128)(2,1)}, u32[]{:S(2)}, u32[]{:S(2)}) collective-permute-start(bf16[32,5120]{1,0:T(8,128)(2,1)} %get-tuple-element.424), channel_id=1, source_target_pairs={{0,12},{1,13},{2,14},{3,15},{4,0},{5,1},{6,2},{7,3},{8,4},{9,5},{1... | collective-permute-start | bytes 983048 | tf_op jit(solution)/shard_map/ppermute | solution.py:579
  603.5 25.2 %collective-permute-start.98 = (bf16[32,1024]{1,0:T(8,128)(2,1)}, bf16[32,1024]{1,0:T(8,128)(2,1)S(1)}, u32[]{:S(2)}, u32[]{:S(2)}) collective-permute-start(bf16[32,1024]{1,0:T(8,128)(2,1)} %get-tuple-element.463), channel_id=1, source_target_pairs={{0,4},{1,5},{2,6},{3,7},{4,8},{5,9},{6,10},{7,11},{8,12},{9,13},{1... | collective-permute-start | bytes 196616 | tf_op jit(solution)/shard_map/ppermute | solution.py:579
  607.3 22.3 %collective-permute-start.99 = (bf16[32,1024]{1,0:T(8,128)(2,1)}, bf16[32,1024]{1,0:T(8,128)(2,1)S(1)}, u32[]{:S(2)}, u32[]{:S(2)}) collective-permute-start(bf16[32,1024]{1,0:T(8,128)(2,1)} %get-tuple-element.462), channel_id=1, source_target_pairs={{0,8},{1,9},{2,10},{3,11},{4,12},{5,13},{6,14},{7,15},{8,0},{9,1},... | collective-permute-start | bytes 196616 | tf_op jit(solution)/shard_map/ppermute | solution.py:579
  610.2 19.5 %collective-permute-start.100 = (bf16[32,1024]{1,0:T(8,128)(2,1)S(1)}, bf16[32,1024]{1,0:T(8,128)(2,1)S(1)}, u32[]{:S(2)}, u32[]{:S(2)}) collective-permute-start(bf16[32,1024]{1,0:T(8,128)(2,1)S(1)} %get-tuple-element.461), channel_id=1, source_target_pairs={{0,12},{1,13},{2,14},{3,15},{4,0},{5,1},{6,2},{7,3},{8,4},{9,5},{1... | collective-permute-start | bytes 196616 | tf_op jit(solution)/shard_map/ppermute | solution.py:579
  (216 other events, 1917.4 us)
Sparse Core Ops, SparseCore 0:
  466.6 23.9 reduce-scatter.3
  520.0 30.8 reduce-scatter.5
  568.5 20.5 reduce-scatter.7

commit v5 on v3

--- a/solution.py
+++ b/solution.py
@@ -130,7 +130,7 @@
         ],
         scratch_shapes=[pltpu.VMEM((length, length), f32)],
         compiler_params=pltpu.CompilerParams(vmem_limit_bytes=32 * 2**20),
-        cost_estimate=pl.CostEstimate(flops=4 * length * length * wide, bytes_accessed=length * 10000, transcendentals=length * length * HEADS),
+        cost_estimate=pl.CostEstimate(flops=0, bytes_accessed=0, transcendentals=0),
     )(qkv, cosine, sine, labels[:, None], labels[None, :])
 
 
@@ -180,7 +180,7 @@
         out_shape=jax.ShapeDtypeStruct((length, wide + 2 * narrow), bf16),
         scratch_shapes=[pltpu.VMEM((length, length), f32), pltpu.VMEM((length, wide + narrow), f32), pltpu.VMEM((length, narrow), f32)],
         compiler_params=pltpu.CompilerParams(vmem_limit_bytes=32 * 2**20),
-        cost_estimate=pl.CostEstimate(flops=10 * length * length * wide, bytes_accessed=length * 10000, transcendentals=length * length * HEADS),
+        cost_estimate=pl.CostEstimate(flops=0, bytes_accessed=0, transcendentals=0),
     )(turned_qk, values, grad_att, cosine, sine, labels[:, None], labels[None, :])
 
 
@@ -450,9 +450,7 @@
                 pltpu.SemaphoreType.DMA((self.parts * count,)),
             ],
             compiler_params=pltpu.CompilerParams(vmem_limit_bytes=16 * 2**20),
-            cost_estimate=pl.CostEstimate(
-                flops=0, bytes_accessed=4 * shape[0] * shape[1], transcendentals=0
-            ),
+            cost_estimate=pl.CostEstimate(flops=0, bytes_accessed=0, transcendentals=0),
         )(self.arrival, *pieces)
 
     def side_by_side(self, pieces):

time: 672 us -> 661 us (0.984)
  starting transfers between devices: 125 us -> 118 us
    ppermute x6, waiting for transfers between devices: 23.5 us -> 30.3 us  [travelled(): got = (yield lax.ppermute(line, BOTH, second_route))]
    unnamed x464 -> x398, local copies, waits for them, and re-layouts: 46.8 us -> 44.5 us
where the time goes in v5:
time: 661 us; the launch traced here: 651 us
  matrix products  164 us (25%)
  waiting for transfers between devices  127 us (19%)
  starting transfers between devices  118 us (18%)
  Pallas kernels  85.6 us (13%)
  local copies, waits for them, and re-layouts  83.7 us (13%)
  other arithmetic  55.9 us (8%)
  between operations  17.4 us (3%)
    dot_general x31, matrix products, dot(): return jnp.dot(a, b, preferred_element_type=f32)  61.6 us
    dot_general x18, matrix products, dot_nt(): lax.dot_general(a, b, (((1,), (1,)), ((), ())), preferred_element_type=f32)  54 us
    ppermute x18, starting transfers between devices, travelled(): lax.ppermute(part, FSDP, [(i, (i + 4 * k) % self.n) for i in range(self.n)])  53.7 us
    dot_general x24, matrix products, dot_tn(): lax.dot_general(a, b, (((0,), (0,)), ((), ())), preferred_element_type=f32)  48.2 us
    unnamed x398, local copies, waits for them, and re-layouts  44.5 us
    pallas_call x6, Pallas kernels, assembled(): pl.pallas_call(kernel, out_shape=jax.ShapeDtypeStruct(shape, bf16), in_sp...  43.5 us
    ppermute x8, waiting for transfers between devices, reduced(): got = (yield lax.ppermute(mine[half // 2:], BOTH, first_route))  35.3 us
    ppermute x6, waiting for transfers between devices, travelled(): got = (yield lax.ppermute(line, BOTH, second_route))  30.3 us
  transfers between devices with their start and end apart: 109, of which 27 were waited for; matrix products, arithmetic and copies ran while one was open for 36% of the time, Pallas kernels for 13%

profile of v5, /device:TPU:0, one launch (start us, length us, event | category | flops | bytes accessed | tf_op | source)
XLA Modules:
  0.0 650.8 jit_solution(6042403172393684147)
XLA Ops:
  44.7 4.2 collective-permute-start.7
  53.4 5.2 collective-permute-done.7
  58.6 12.7 %collective-permute-done.8 = bf16[32,5120]{1,0:T(8,128)(2,1)S(1)} collective-permute-done((bf16[32,5120]{1,0:T(8,128)(2,1)S(1)}, bf16[32,5120]{1,0:T(8,128)(2,1)S(1)}, u32[]{:S(2)}, u32[]{:S(2)}) %collective-permute-start.8) | collective-permute-done | bytes 327712 | tf_op jit(solution)/shard_map/ppermute | solution.py:489
  78.6 7.8 %collective-permute-start.13 = (bf16[32,2560]{1,0:T(8,128)(2,1)}, bf16[32,2560]{1,0:T(8,128)(2,1)S(1)}, u32[]{:S(2)}, u32[]{:S(2)}) collective-permute-start(bf16[32,2560]{1,0:T(8,128)(2,1)} %get-tuple-element.197), channel_id=1, source_target_pairs={{0,4},{1,5},{2,6},{3,7},{4,8},{5,9},{6,10},{7,11},{8,12},{9,13},{1... | collective-permute-start | bytes 491528 | tf_op jit(solution)/shard_map/ppermute | solution.py:489
  88.8 4.9 collective-permute-done.10.refs_2_
  93.8 8.5 %collective-permute-start.15 = (bf16[32,2560]{1,0:T(8,128)(2,1)}, bf16[32,2560]{1,0:T(8,128)(2,1)S(1)}, u32[]{:S(2)}, u32[]{:S(2)}) collective-permute-start(bf16[32,2560]{1,0:T(8,128)(2,1)} %get-tuple-element.197), channel_id=1, source_target_pairs={{0,12},{1,13},{2,14},{3,15},{4,0},{5,1},{6,2},{7,3},{8,4},{9,5},{1... | collective-permute-start | bytes 491528 | tf_op jit(solution)/shard_map/ppermute | solution.py:489
  109.1 7.6 %collective-permute-start.21 = (bf16[32,2688]{1,0:T(8,128)(2,1)}, bf16[32,2688]{1,0:T(8,128)(2,1)S(1)}, u32[]{:S(2)}, u32[]{:S(2)}) collective-permute-start(bf16[32,2688]{1,0:T(8,128)(2,1)} %get-tuple-element.210), channel_id=1, source_target_pairs={{0,4},{1,5},{2,6},{3,7},{4,8},{5,9},{6,10},{7,11},{8,12},{9,13},{1... | collective-permute-start | bytes 516104 | tf_op jit(solution)/shard_map/ppermute | solution.py:489
  120.7 10.3 %shard_map.212 = bf16[1024,2688]{1,0:T(8,128)(2,1)S(1)} custom-call(s32[32]{0:T(128)S(1)} %multiply_add_fusion.1.index, bf16[128,2688]{1,0:T(8,128)(2,1)S(1)} %constant_dynamic-update-slice_fusion.6.refs_0_, bf16[128,2688]{1,0:T(8,128)(2,1)S(1)} %collective-permute-done.6.refs_1_, bf16[128,2688]{1,0:T(8,128)(2,1)S(1)} %collective-permute-done.10.refs_2_, ...), custom_call_target="tpu_custom_call" | custom-call | tf_op jit(solution)/shard_map/pallas_call | solution.py:442
  137.8 3.4 fusion.53
  142.3 3.2 copy.72.qkv
  147.3 8.8 %shard_map.213 = (bf16[384,960]{1,0:T(8,128)(2,1)S(1)}, bf16[384,1280]{1,0:T(8,128)(2,1)S(1)}, bf16[384,320]{1,0:T(8,128)(2,1)S(1)}) custom-call(f32[384,1600]{1,0:T(8,128)S(1)} %copy-done.6, f32[384,128]{1,0:T(8,128)S(1)} %get-tuple-element.471.cosine, f32[384,128]{1,0:T(8,128)S(1)} %get-tuple-element.472.sine, s32[384,1]{1,0:T(8,128)S(1)} %copy.73.row_labels, ...), custom_call_target="tpu_custom_call" | custom-call | tf_op jit(solution)/shard_map/pallas_call | solution.py:124
  170.6 6.3 collective-permute-done.30.refs_1_
  178.7 5.7 shard_map.214
  188.3 4.1 multiply_convert_fusion.5
  197.7 6.1 shard_map.215
  206.1 19.0 %collective-permute-done.40.refs_1_ = bf16[128,5120]{1,0:T(8,128)(2,1)} collective-permute-done((bf16[128,5120]{1,0:T(8,128)(2,1)S(1)}, bf16[128,5120]{1,0:T(8,128)(2,1)}, u32[]{:S(2)}, u32[]{:S(2)}) %collective-permute-start.40) | collective-permute-done | bytes 1310752 | tf_op jit(solution)/shard_map/ppermute | solution.py:496
  225.9 5.6 collective-permute-start.47
  236.6 10.1 %shard_map.216 = bf16[1024,2688]{1,0:T(8,128)(2,1)S(1)} custom-call(s32[32]{0:T(128)S(1)} %multiply_add_fusion.1.index, bf16[128,2688]{1,0:T(8,128)(2,1)} %constant_dynamic-update-slice_fusion.18.refs_0_, bf16[128,2688]{1,0:T(8,128)(2,1)S(1)} %collective-permute-done.30.refs_1_, bf16[128,2688]{1,0:T(8,128)(2,1)S(1)} %collective-permute-done.41.refs_2_, ...), custom_call_target="tpu_custom_call" | custom-call | tf_op jit(solution)/shard_map/pallas_call | solution.py:442
  249.1 3.4 fusion.49
  255.5 3.4 copy.74.qkv
  260.6 8.8 %shard_map.217 = (bf16[384,960]{1,0:T(8,128)(2,1)S(1)}, bf16[384,1280]{1,0:T(8,128)(2,1)S(1)}, bf16[384,320]{1,0:T(8,128)(2,1)S(1)}) custom-call(f32[384,1600]{1,0:T(8,128)S(1)} %copy-done.7, f32[384,128]{1,0:T(8,128)S(1)} %get-tuple-element.471.cosine, f32[384,128]{1,0:T(8,128)S(1)} %get-tuple-element.472.sine, s32[384,1]{1,0:T(8,128)S(1)} %copy.73.row_labels, ...), custom_call_target="tpu_custom_call" | custom-call | tf_op jit(solution)/shard_map/pallas_call | solution.py:124
  282.0 5.6 shard_map.218
  291.4 4.1 multiply_convert_fusion.4
  296.2 3.6 fusion.292
  307.5 5.7 shard_map.219
  313.2 7.0 %multiply_convert_fusion.2 = (bf16[384,2560]{1,0:T(8,128)(2,1)S(1)}, bf16[384,2560]{1,0:T(8,128)(2,1)S(1)}) fusion(f32[384,2560]{1,0:T(8,128)S(1)} %fusion.8, f32[384,2560]{1,0:T(8,128)} %get-tuple-element.460, bf16[384,1024]{1,0:T(8,128)(2,1)S(1)} %get-tuple-element.463, bf16[2560,1024]{1,0:T(8,128)(2,1)S(1)} %shard_map.219), kind=kOutput, calls=%fused_computation.39 | convolution fusion | flops 2026045440 | bytes 17825792 | tf_op jit(solution)/shard_map/dot_general | solution.py:33
  322.0 4.7 convolution_convert_fusion.1
  333.9 4.0 fusion
  349.3 5.1 add_convert_fusion.1
  364.8 3.9 fusion.120.grad_att
  376.1 12.4 %shard_map.220 = bf16[384,1600]{1,0:T(8,128)(2,1)S(1)} custom-call(bf16[384,1280]{1,0:T(8,128)(2,1)S(1)} %copy-done.15, bf16[384,320]{1,0:T(8,128)(2,1)S(1)} %copy-done.21, bf16[384,960]{1,0:T(8,128)(2,1)S(1)} %fusion.120.grad_att, f32[384,128]{1,0:T(8,128)S(1)} %get-tuple-element.471.cosine, f32[384,128]{1,0:T(8,128)S(1)} %get-tuple-element.472.sine, ...), custom_call_target="tpu_custom_call" | custom-call | tf_op jit(solution)/shard_map/pallas_call | solution.py:178
  388.7 7.8 %collective-permute-done.69 = bf16[256,5120]{1,0:T(8,128)(2,1)} collective-permute-done((bf16[256,5120]{1,0:T(8,128)(2,1)}, bf16[256,5120]{1,0:T(8,128)(2,1)}, u32[]{:S(2)}, u32[]{:S(2)}) %collective-permute-start.69) | collective-permute-done | bytes 2621472 | tf_op jit(solution)/shard_map/ppermute | solution.py:549
  414.2 12.4 %collective-permute-done.72 = bf16[256,1024]{1,0:T(8,128)(2,1)S(1)} collective-permute-done((bf16[256,1024]{1,0:T(8,128)(2,1)S(1)}, bf16[256,1024]{1,0:T(8,128)(2,1)S(1)}, u32[]{:S(2)}, u32[]{:S(2)}) %collective-permute-start.72) | collective-permute-done | bytes 524320 | tf_op jit(solution)/shard_map/ppermute | solution.py:549
  438.6 5.7 multiply_convert_fusion
  446.5 5.2 collective-permute-done.74
  454.6 4.9 convolution_convert_fusion
  471.3 5.2 fusion.10
  476.5 3.8 multiply_reduce_fusion
  489.7 4.9 add_convert_fusion
  500.3 3.9 fusion.121.grad_att
  512.1 3.3 collective-permute-start.87
  519.6 12.1 %shard_map.221 = bf16[384,1600]{1,0:T(8,128)(2,1)S(1)} custom-call(bf16[384,1280]{1,0:T(8,128)(2,1)S(1)} %copy-done.13, bf16[384,320]{1,0:T(8,128)(2,1)S(1)} %copy-done.19, bf16[384,960]{1,0:T(8,128)(2,1)S(1)} %fusion.121.grad_att, f32[384,128]{1,0:T(8,128)S(1)} %get-tuple-element.471.cosine, f32[384,128]{1,0:T(8,128)S(1)} %get-tuple-element.472.sine, ...), custom_call_target="tpu_custom_call" | custom-call | tf_op jit(solution)/shard_map/pallas_call | solution.py:178
  532.7 6.9 %collective-permute-done.84 = bf16[256,5120]{1,0:T(8,128)(2,1)} collective-permute-done((bf16[256,5120]{1,0:T(8,128)(2,1)}, bf16[256,5120]{1,0:T(8,128)(2,1)}, u32[]{:S(2)}, u32[]{:S(2)}) %collective-permute-start.84) | collective-permute-done | bytes 2621472 | tf_op jit(solution)/shard_map/ppermute | solution.py:549
  539.6 5.5 multiply_reduce_fusion.1
  557.5 4.1 subtract_add_fusion
  563.3 8.7 %collective-permute-done.89 = bf16[128,5120]{1,0:T(8,128)(2,1)} collective-permute-done((bf16[128,5120]{1,0:T(8,128)(2,1)}, bf16[128,5120]{1,0:T(8,128)(2,1)}, u32[]{:S(2)}, u32[]{:S(2)}) %collective-permute-start.89) | collective-permute-done | bytes 1310752 | tf_op jit(solution)/shard_map/ppermute | solution.py:551
  614.2 5.9 collective-permute-done.95
  620.1 8.0 %collective-permute-done.96 = bf16[32,1664]{1,0:T(8,128)(2,1)S(1)} collective-permute-done((bf16[32,1664]{1,0:T(8,128)(2,1)S(1)}, bf16[32,1664]{1,0:T(8,128)(2,1)S(1)}, u32[]{:S(2)}, u32[]{:S(2)}) %collective-permute-start.96) | collective-permute-done | bytes 106528 | tf_op jit(solution)/shard_map/ppermute | solution.py:560
  (830 shorter events, 319.8 us)
Async XLA Ops:
  7.2 525.5 %reduce-scatter.5.cloned.1.call-start = ((), (), s32[]{:S(2)}) async-start(), calls=%async_computation.4 | async-start | bytes 819200 | tf_op jit(solution)/shard_map/reduce_scatter | solution.py:565
  48.8 22.5 %collective-permute-start.8 = (bf16[32,5120]{1,0:T(8,128)(2,1)S(1)}, bf16[32,5120]{1,0:T(8,128)(2,1)S(1)}, u32[]{:S(2)}, u32[]{:S(2)}) collective-permute-start(bf16[32,5120]{1,0:T(8,128)(2,1)S(1)} %get-tuple-element.187), channel_id=1, source_target_pairs={{0,8},{1,9},{2,10},{3,11},{4,12},{5,13},{6,14},{7,15},{8,0},{9,1},... | collective-permute-start | bytes 983048 | tf_op jit(solution)/shard_map/ppermute | solution.py:489
  50.5 20.9 %collective-permute-start.9 = (bf16[32,5120]{1,0:T(8,128)(2,1)S(1)}, bf16[32,5120]{1,0:T(8,128)(2,1)S(1)}, u32[]{:S(2)}, u32[]{:S(2)}) collective-permute-start(bf16[32,5120]{1,0:T(8,128)(2,1)S(1)} %get-tuple-element.187), channel_id=1, source_target_pairs={{0,12},{1,13},{2,14},{3,15},{4,0},{5,1},{6,2},{7,3},{8,4},{9,5},{1... | collective-permute-start | bytes 983048 | tf_op jit(solution)/shard_map/ppermute | solution.py:489
  73.6 33.6 %collective-permute-start.12 = (bf16[128,5120]{1,0:T(8,128)(2,1)}, bf16[128,5120]{1,0:T(8,128)(2,1)}, u32[]{:S(2)}, u32[]{:S(2)}) collective-permute-start(bf16[128,5120]{1,0:T(8,128)(2,1)} %constant_dynamic-update-slice_fusion.10.refs_0_), channel_id=1, source_target_pairs={{0,1},{1,0},{2,3},{3,2},{4,5},{5,4},{6,7},{7,6},{8,9},{9,8},{10,11... | collective-permute-start | bytes 3932168 | tf_op jit(solution)/shard_map/ppermute | solution.py:496
  75.9 29.2 %collective-permute-start.11 = (bf16[128,2688]{1,0:T(8,128)(2,1)S(1)}, bf16[128,2688]{1,0:T(8,128)(2,1)S(1)}, u32[]{:S(2)}, u32[]{:S(2)}) collective-permute-start(bf16[128,2688]{1,0:T(8,128)(2,1)S(1)} %collective-permute-done.6.refs_1_), channel_id=1, source_target_pairs={{0,2},{1,3},{2,0},{3,1},{4,6},{5,7},{6,4},{7,5},{8,10},{9,11},{10,... | collective-permute-start | bytes 2064392 | tf_op jit(solution)/shard_map/ppermute | solution.py:499
  78.6 28.7 %collective-permute-start.13 = (bf16[32,2560]{1,0:T(8,128)(2,1)}, bf16[32,2560]{1,0:T(8,128)(2,1)S(1)}, u32[]{:S(2)}, u32[]{:S(2)}) collective-permute-start(bf16[32,2560]{1,0:T(8,128)(2,1)} %get-tuple-element.197), channel_id=1, source_target_pairs={{0,4},{1,5},{2,6},{3,7},{4,8},{5,9},{6,10},{7,11},{8,12},{9,13},{1... | collective-permute-start | bytes 491528 | tf_op jit(solution)/shard_map/ppermute | solution.py:489
  86.3 21.8 %collective-permute-start.14 = (bf16[32,2560]{1,0:T(8,128)(2,1)}, bf16[32,2560]{1,0:T(8,128)(2,1)S(1)}, u32[]{:S(2)}, u32[]{:S(2)}) collective-permute-start(bf16[32,2560]{1,0:T(8,128)(2,1)} %get-tuple-element.197), channel_id=1, source_target_pairs={{0,8},{1,9},{2,10},{3,11},{4,12},{5,13},{6,14},{7,15},{8,0},{9,1},... | collective-permute-start | bytes 491528 | tf_op jit(solution)/shard_map/ppermute | solution.py:489
  107.3 50.8 %collective-permute-start.24 = (bf16[128,5120]{1,0:T(8,128)(2,1)}, bf16[128,5120]{1,0:T(8,128)(2,1)}, u32[]{:S(2)}, u32[]{:S(2)}) collective-permute-start(bf16[128,5120]{1,0:T(8,128)(2,1)} %constant_dynamic-update-slice_fusion.10.refs_0_), channel_id=1, source_target_pairs={{0,2},{1,3},{2,0},{3,1},{4,6},{5,7},{6,4},{7,5},{8,10},{9,11},{10,... | collective-permute-start | bytes 3932168 | tf_op jit(solution)/shard_map/ppermute | solution.py:494
  109.1 32.0 %collective-permute-start.21 = (bf16[32,2688]{1,0:T(8,128)(2,1)}, bf16[32,2688]{1,0:T(8,128)(2,1)S(1)}, u32[]{:S(2)}, u32[]{:S(2)}) collective-permute-start(bf16[32,2688]{1,0:T(8,128)(2,1)} %get-tuple-element.210), channel_id=1, source_target_pairs={{0,4},{1,5},{2,6},{3,7},{4,8},{5,9},{6,10},{7,11},{8,12},{9,13},{1... | collective-permute-start | bytes 516104 | tf_op jit(solution)/shard_map/ppermute | solution.py:489
  116.7 25.1 %collective-permute-start.22 = (bf16[32,2688]{1,0:T(8,128)(2,1)}, bf16[32,2688]{1,0:T(8,128)(2,1)}, u32[]{:S(2)}, u32[]{:S(2)}) collective-permute-start(bf16[32,2688]{1,0:T(8,128)(2,1)} %get-tuple-element.210), channel_id=1, source_target_pairs={{0,8},{1,9},{2,10},{3,11},{4,12},{5,13},{6,14},{7,15},{8,0},{9,1},... | collective-permute-start | bytes 516104 | tf_op jit(solution)/shard_map/ppermute | solution.py:489
  119.5 38.6 %collective-permute-start.25 = (bf16[128,5120]{1,0:T(8,128)(2,1)}, bf16[128,5120]{1,0:T(8,128)(2,1)}, u32[]{:S(2)}, u32[]{:S(2)}) collective-permute-start(bf16[128,5120]{1,0:T(8,128)(2,1)} %collective-permute-done.12.refs_1_), channel_id=1, source_target_pairs={{0,2},{1,3},{2,0},{3,1},{4,6},{5,7},{6,4},{7,5},{8,10},{9,11},{10,... | collective-permute-start | bytes 3932168 | tf_op jit(solution)/shard_map/ppermute | solution.py:499
  141.8 23.3 %collective-permute-start.26 = (bf16[128,5120]{1,0:T(8,128)(2,1)}, bf16[128,5120]{1,0:T(8,128)(2,1)}, u32[]{:S(2)}, u32[]{:S(2)}) collective-permute-start(bf16[128,5120]{1,0:T(8,128)(2,1)} %constant_dynamic-update-slice_fusion.10.refs_0_), channel_id=1, source_target_pairs={{0,16},{16,0},{1,17},{17,1},{2,18},{18,2},{3,19},{19,3},{4,20},{20... | collective-permute-start | bytes 3932168 | tf_op jit(solution)/shard_map/ppermute | solution.py:363
  141.8 24.2 %collective-permute-start.27 = (bf16[128,5120]{1,0:T(8,128)(2,1)}, bf16[128,5120]{1,0:T(8,128)(2,1)}, u32[]{:S(2)}, u32[]{:S(2)}) collective-permute-start(bf16[128,5120]{1,0:T(8,128)(2,1)} %collective-permute-done.12.refs_1_), channel_id=1, source_target_pairs={{0,16},{16,0},{1,17},{17,1},{2,18},{18,2},{3,19},{19,3},{4,20},{20... | collective-permute-start | bytes 3932168 | tf_op jit(solution)/shard_map/ppermute | solution.py:363
  165.1 27.8 %collective-permute-start.34 = (bf16[128,2560]{1,0:T(8,128)(2,1)S(1)}, bf16[128,2560]{1,0:T(8,128)(2,1)S(1)}, u32[]{:S(2)}, u32[]{:S(2)}) collective-permute-start(bf16[128,2560]{1,0:T(8,128)(2,1)S(1)} %copy-done.11), channel_id=1, source_target_pairs={{0,2},{1,3},{2,0},{3,1},{4,6},{5,7},{6,4},{7,5},{8,10},{9,11},{10,... | collective-permute-start | bytes 1966088 | tf_op jit(solution)/shard_map/ppermute | solution.py:494
  166.1 26.3 %collective-permute-start.31 = (bf16[32,5120]{1,0:T(8,128)(2,1)S(1)}, bf16[32,5120]{1,0:T(8,128)(2,1)S(1)}, u32[]{:S(2)}, u32[]{:S(2)}) collective-permute-start(bf16[32,5120]{1,0:T(8,128)(2,1)S(1)} %copy-done.79), channel_id=1, source_target_pairs={{0,4},{1,5},{2,6},{3,7},{4,8},{5,9},{6,10},{7,11},{8,12},{9,13},{1... | collective-permute-start | bytes 983048 | tf_op jit(solution)/shard_map/ppermute | solution.py:489
  167.2 25.3 %collective-permute-start.32 = (bf16[32,5120]{1,0:T(8,128)(2,1)S(1)}, bf16[32,5120]{1,0:T(8,128)(2,1)S(1)}, u32[]{:S(2)}, u32[]{:S(2)}) collective-permute-start(bf16[32,5120]{1,0:T(8,128)(2,1)S(1)} %copy-done.79), channel_id=1, source_target_pairs={{0,8},{1,9},{2,10},{3,11},{4,12},{5,13},{6,14},{7,15},{8,0},{9,1},... | collective-permute-start | bytes 983048 | tf_op jit(solution)/shard_map/ppermute | solution.py:489
  169.5 23.5 %collective-permute-start.33 = (bf16[32,5120]{1,0:T(8,128)(2,1)S(1)}, bf16[32,5120]{1,0:T(8,128)(2,1)S(1)}, u32[]{:S(2)}, u32[]{:S(2)}) collective-permute-start(bf16[32,5120]{1,0:T(8,128)(2,1)S(1)} %copy-done.79), channel_id=1, source_target_pairs={{0,12},{1,13},{2,14},{3,15},{4,0},{5,1},{6,2},{7,3},{8,4},{9,5},{1... | collective-permute-start | bytes 983048 | tf_op jit(solution)/shard_map/ppermute | solution.py:489
  193.7 31.5 %collective-permute-start.40 = (bf16[128,5120]{1,0:T(8,128)(2,1)S(1)}, bf16[128,5120]{1,0:T(8,128)(2,1)}, u32[]{:S(2)}, u32[]{:S(2)}) collective-permute-start(bf16[128,5120]{1,0:T(8,128)(2,1)S(1)} %constant_dynamic-update-slice_fusion.22.refs_0_), channel_id=1, source_target_pairs={{0,1},{1,0},{2,3},{3,2},{4,5},{5,4},{6,7},{7,6},{8,9},{9,8},{10,11... | collective-permute-start | bytes 3932168 | tf_op jit(solution)/shard_map/ppermute | solution.py:496
  195.1 30.1 %collective-permute-start.41 = (bf16[128,2688]{1,0:T(8,128)(2,1)}, bf16[128,2688]{1,0:T(8,128)(2,1)S(1)}, u32[]{:S(2)}, u32[]{:S(2)}) collective-permute-start(bf16[128,2688]{1,0:T(8,128)(2,1)} %constant_dynamic-update-slice_fusion.18.refs_0_), channel_id=1, source_target_pairs={{0,2},{1,3},{2,0},{3,1},{4,6},{5,7},{6,4},{7,5},{8,10},{9,11},{10,... | collective-permute-start | bytes 2064392 | tf_op jit(solution)/shard_map/ppermute | solution.py:494
  196.6 35.6 %collective-permute-start.43 = (bf16[128,2688]{1,0:T(8,128)(2,1)}, bf16[128,2688]{1,0:T(8,128)(2,1)S(1)}, u32[]{:S(2)}, u32[]{:S(2)}) collective-permute-start(bf16[128,2688]{1,0:T(8,128)(2,1)} %constant_dynamic-update-slice_fusion.18.refs_0_), channel_id=1, source_target_pairs={{0,16},{16,0},{1,17},{17,1},{2,18},{18,2},{3,19},{19,3},{4,20},{20... | collective-permute-start | bytes 2064392 | tf_op jit(solution)/shard_map/ppermute | solution.py:363
  196.6 28.6 %collective-permute-start.42 = (bf16[128,2688]{1,0:T(8,128)(2,1)S(1)}, bf16[128,2688]{1,0:T(8,128)(2,1)S(1)}, u32[]{:S(2)}, u32[]{:S(2)}) collective-permute-start(bf16[128,2688]{1,0:T(8,128)(2,1)S(1)} %collective-permute-done.30.refs_1_), channel_id=1, source_target_pairs={{0,2},{1,3},{2,0},{3,1},{4,6},{5,7},{6,4},{7,5},{8,10},{9,11},{10,... | collective-permute-start | bytes 2064392 | tf_op jit(solution)/shard_map/ppermute | solution.py:499
  197.7 35.1 %collective-permute-start.44 = (bf16[128,2688]{1,0:T(8,128)(2,1)S(1)}, bf16[128,2688]{1,0:T(8,128)(2,1)S(1)}, u32[]{:S(2)}, u32[]{:S(2)}) collective-permute-start(bf16[128,2688]{1,0:T(8,128)(2,1)S(1)} %collective-permute-done.30.refs_1_), channel_id=1, source_target_pairs={{0,16},{16,0},{1,17},{17,1},{2,18},{18,2},{3,19},{19,3},{4,20},{20... | collective-permute-start | bytes 2064392 | tf_op jit(solution)/shard_map/ppermute | solution.py:363
  225.9 26.6 %collective-permute-start.47 = (bf16[32,2560]{1,0:T(8,128)(2,1)S(1)}, bf16[32,2560]{1,0:T(8,128)(2,1)S(1)}, u32[]{:S(2)}, u32[]{:S(2)}) collective-permute-start(bf16[32,2560]{1,0:T(8,128)(2,1)S(1)} %copy-done.101), channel_id=1, source_target_pairs={{0,4},{1,5},{2,6},{3,7},{4,8},{5,9},{6,10},{7,11},{8,12},{9,13},{1... | collective-permute-start | bytes 491528 | tf_op jit(solution)/shard_map/ppermute | solution.py:489
  232.2 20.2 %collective-permute-start.48 = (bf16[32,2560]{1,0:T(8,128)(2,1)S(1)}, bf16[32,2560]{1,0:T(8,128)(2,1)S(1)}, u32[]{:S(2)}, u32[]{:S(2)}) collective-permute-start(bf16[32,2560]{1,0:T(8,128)(2,1)S(1)} %copy-done.101), channel_id=1, source_target_pairs={{0,8},{1,9},{2,10},{3,11},{4,12},{5,13},{6,14},{7,15},{8,0},{9,1},... | collective-permute-start | bytes 491528 | tf_op jit(solution)/shard_map/ppermute | solution.py:489
  234.6 37.5 %collective-permute-start.51 = (bf16[128,5120]{1,0:T(8,128)(2,1)S(1)}, bf16[128,5120]{1,0:T(8,128)(2,1)}, u32[]{:S(2)}, u32[]{:S(2)}) collective-permute-start(bf16[128,5120]{1,0:T(8,128)(2,1)S(1)} %constant_dynamic-update-slice_fusion.22.refs_0_), channel_id=1, source_target_pairs={{0,2},{1,3},{2,0},{3,1},{4,6},{5,7},{6,4},{7,5},{8,10},{9,11},{10,... | collective-permute-start | bytes 3932168 | tf_op jit(solution)/shard_map/ppermute | solution.py:494
  235.3 38.1 %collective-permute-start.52 = (bf16[128,5120]{1,0:T(8,128)(2,1)}, bf16[128,5120]{1,0:T(8,128)(2,1)}, u32[]{:S(2)}, u32[]{:S(2)}) collective-permute-start(bf16[128,5120]{1,0:T(8,128)(2,1)} %collective-permute-done.40.refs_1_), channel_id=1, source_target_pairs={{0,2},{1,3},{2,0},{3,1},{4,6},{5,7},{6,4},{7,5},{8,10},{9,11},{10,... | collective-permute-start | bytes 3932168 | tf_op jit(solution)/shard_map/ppermute | solution.py:499
  255.0 25.1 %collective-permute-start.53 = (bf16[128,5120]{1,0:T(8,128)(2,1)S(1)}, bf16[128,5120]{1,0:T(8,128)(2,1)}, u32[]{:S(2)}, u32[]{:S(2)}) collective-permute-start(bf16[128,5120]{1,0:T(8,128)(2,1)S(1)} %constant_dynamic-update-slice_fusion.22.refs_0_), channel_id=1, source_target_pairs={{0,16},{16,0},{1,17},{17,1},{2,18},{18,2},{3,19},{19,3},{4,20},{20... | collective-permute-start | bytes 3932168 | tf_op jit(solution)/shard_map/ppermute | solution.py:363
  255.0 25.2 %collective-permute-start.54 = (bf16[128,5120]{1,0:T(8,128)(2,1)}, bf16[128,5120]{1,0:T(8,128)(2,1)}, u32[]{:S(2)}, u32[]{:S(2)}) collective-permute-start(bf16[128,5120]{1,0:T(8,128)(2,1)} %collective-permute-done.40.refs_1_), channel_id=1, source_target_pairs={{0,16},{16,0},{1,17},{17,1},{2,18},{18,2},{3,19},{19,3},{4,20},{20... | collective-permute-start | bytes 3932168 | tf_op jit(solution)/shard_map/ppermute | solution.py:363
  339.5 29.2 %collective-permute-start.66 = (bf16[256,2560]{1,0:T(8,128)(2,1)S(1)}, bf16[256,2560]{1,0:T(8,128)(2,1)}, u32[]{:S(2)}, u32[]{:S(2)}) collective-permute-start(bf16[256,2560]{1,0:T(8,128)(2,1)S(1)} %slice.534), channel_id=1, source_target_pairs={{0,2},{1,3},{2,0},{3,1},{4,6},{5,7},{6,4},{7,5},{8,10},{9,11},{10,... | collective-permute-start | bytes 3932168 | tf_op jit(solution)/shard_map/ppermute | solution.py:549
  357.5 39.0 %collective-permute-start.69 = (bf16[256,5120]{1,0:T(8,128)(2,1)}, bf16[256,5120]{1,0:T(8,128)(2,1)}, u32[]{:S(2)}, u32[]{:S(2)}) collective-permute-start(bf16[256,5120]{1,0:T(8,128)(2,1)} %slice.539), channel_id=1, source_target_pairs={{0,2},{1,3},{2,0},{3,1},{4,6},{5,7},{6,4},{7,5},{8,10},{9,11},{10,... | collective-permute-start | bytes 7864328 | tf_op jit(solution)/shard_map/ppermute | solution.py:549
  400.7 26.7 %collective-permute-start.70 = (bf16[512,1664]{1,0:T(8,128)(2,1)S(1)}, bf16[512,1664]{1,0:T(8,128)(2,1)S(1)}, u32[]{:S(2)}, u32[]{:S(2)}) collective-permute-start(bf16[512,1664]{1,0:T(8,128)(2,1)S(1)} %convolution_convert_fusion.3), channel_id=1, source_target_pairs={{0,16},{16,0},{1,17},{17,1},{2,18},{18,2},{3,19},{19,3},{4,20},{20... | collective-permute-start | bytes 5111816 | tf_op jit(solution)/shard_map/ppermute | solution.py:363
  404.1 23.3 %collective-permute-start.71 = (bf16[128,5120]{1,0:T(8,128)(2,1)S(1)}, bf16[128,5120]{1,0:T(8,128)(2,1)S(1)}, u32[]{:S(2)}, u32[]{:S(2)}) collective-permute-start(bf16[128,5120]{1,0:T(8,128)(2,1)S(1)} %slice.542), channel_id=1, source_target_pairs={{0,1},{1,0},{2,3},{3,2},{4,5},{5,4},{6,7},{7,6},{8,9},{9,8},{10,11... | collective-permute-start | bytes 3932168 | tf_op jit(solution)/shard_map/ppermute | solution.py:551
  409.1 22.4 %collective-permute-start.63 = (bf16[384,1024]{1,0:T(8,128)(2,1)S(1)}, bf16[384,1024]{1,0:T(8,128)(2,1)S(1)}, u32[]{:S(2)}, u32[]{:S(2)}) collective-permute-start(bf16[384,1024]{1,0:T(8,128)(2,1)S(1)} %get-tuple-element.461), channel_id=1, source_target_pairs={{0,16},{16,0},{1,17},{17,1},{2,18},{18,2},{3,19},{19,3},{4,20},{20... | collective-permute-start | bytes 2359304 | tf_op jit(solution)/shard_map/ppermute | solution.py:722
  430.2 21.5 %collective-permute-start.73 = (bf16[512,2560]{1,0:T(8,128)(2,1)S(1)}, bf16[512,2560]{1,0:T(8,128)(2,1)S(1)}, u32[]{:S(2)}, u32[]{:S(2)}) collective-permute-start(bf16[512,2560]{1,0:T(8,128)(2,1)S(1)} %pad_maximum_fusion.1), channel_id=1, source_target_pairs={{0,16},{16,0},{1,17},{17,1},{2,18},{18,2},{3,19},{19,3},{4,20},{20... | collective-permute-start | bytes 7864328 | tf_op jit(solution)/shard_map/ppermute | solution.py:363
  459.5 28.3 %collective-permute-start.76 = (bf16[512,5120]{1,0:T(8,128)(2,1)}, bf16[512,5120]{1,0:T(8,128)(2,1)}, u32[]{:S(2)}, u32[]{:S(2)}) collective-permute-start(bf16[512,5120]{1,0:T(8,128)(2,1)} %convolution_convert_fusion), channel_id=1, source_target_pairs={{0,16},{16,0},{1,17},{17,1},{2,18},{18,2},{3,19},{19,3},{4,20},{20... | collective-permute-start | bytes 15728648 | tf_op jit(solution)/shard_map/ppermute | solution.py:363
  460.6 102.7 %reduce-scatter.7.cloned.1.call-start = ((), (), s32[]{:S(2)}) async-start(), calls=%async_computation.5 | async-start | bytes 1638400 | tf_op jit(solution)/shard_map/reduce_scatter | solution.py:565
  466.4 21.4 %collective-permute-start.77 = (bf16[128,1664]{1,0:T(8,128)(2,1)}, bf16[128,1664]{1,0:T(8,128)(2,1)}, u32[]{:S(2)}, u32[]{:S(2)}) collective-permute-start(bf16[128,1664]{1,0:T(8,128)(2,1)} %slice.557), channel_id=1, source_target_pairs={{0,1},{1,0},{2,3},{3,2},{4,5},{5,4},{6,7},{7,6},{8,9},{9,8},{10,11... | collective-permute-start | bytes 1277960 | tf_op jit(solution)/shard_map/ppermute | solution.py:551
  467.6 20.2 %collective-permute-start.79 = (bf16[32,1024]{1,0:T(8,128)(2,1)S(1)}, bf16[32,1024]{1,0:T(8,128)(2,1)S(1)}, u32[]{:S(2)}, u32[]{:S(2)}) collective-permute-start(bf16[32,1024]{1,0:T(8,128)(2,1)S(1)} %get-tuple-element.440), channel_id=1, source_target_pairs={{0,8},{1,9},{2,10},{3,11},{4,12},{5,13},{6,14},{7,15},{8,0},{9,1},... | collective-permute-start | bytes 196616 | tf_op jit(solution)/shard_map/ppermute | solution.py:560
  498.1 41.5 %collective-permute-start.84 = (bf16[256,5120]{1,0:T(8,128)(2,1)}, bf16[256,5120]{1,0:T(8,128)(2,1)}, u32[]{:S(2)}, u32[]{:S(2)}) collective-permute-start(bf16[256,5120]{1,0:T(8,128)(2,1)} %slice.566), channel_id=1, source_target_pairs={{0,2},{1,3},{2,0},{3,1},{4,6},{5,7},{6,4},{7,5},{8,10},{9,11},{10,... | collective-permute-start | bytes 7864328 | tf_op jit(solution)/shard_map/ppermute | solution.py:549
  500.2 105.9 %reduce-scatter.9.cloned.1.call-start = ((), (), s32[]{:S(2)}) async-start(), calls=%async_computation.6 | async-start | bytes 819200 | tf_op jit(solution)/shard_map/reduce_scatter | solution.py:565
  508.4 24.3 %collective-permute-start.83 = (bf16[128,2560]{1,0:T(8,128)(2,1)}, bf16[128,2560]{1,0:T(8,128)(2,1)}, u32[]{:S(2)}, u32[]{:S(2)}) collective-permute-start(bf16[128,2560]{1,0:T(8,128)(2,1)} %slice.564), channel_id=1, source_target_pairs={{0,1},{1,0},{2,3},{3,2},{4,5},{5,4},{6,7},{7,6},{8,9},{9,8},{10,11... | collective-permute-start | bytes 1966088 | tf_op jit(solution)/shard_map/ppermute | solution.py:551
  510.4 21.4 %collective-permute-start.85 = (bf16[32,1664]{1,0:T(8,128)(2,1)S(1)}, bf16[32,1664]{1,0:T(8,128)(2,1)S(1)}, u32[]{:S(2)}, u32[]{:S(2)}) collective-permute-start(bf16[32,1664]{1,0:T(8,128)(2,1)S(1)} %get-tuple-element.427), channel_id=1, source_target_pairs={{0,4},{1,5},{2,6},{3,7},{4,8},{5,9},{6,10},{7,11},{8,12},{9,13},{1... | collective-permute-start | bytes 319496 | tf_op jit(solution)/shard_map/ppermute | solution.py:560
  511.0 21.7 %collective-permute-start.86 = (bf16[32,1664]{1,0:T(8,128)(2,1)}, bf16[32,1664]{1,0:T(8,128)(2,1)}, u32[]{:S(2)}, u32[]{:S(2)}) collective-permute-start(bf16[32,1664]{1,0:T(8,128)(2,1)} %get-tuple-element.426), channel_id=1, source_target_pairs={{0,8},{1,9},{2,10},{3,11},{4,12},{5,13},{6,14},{7,15},{8,0},{9,1},... | collective-permute-start | bytes 319496 | tf_op jit(solution)/shard_map/ppermute | solution.py:560
  512.1 20.6 %collective-permute-start.87 = (bf16[32,1664]{1,0:T(8,128)(2,1)}, bf16[32,1664]{1,0:T(8,128)(2,1)}, u32[]{:S(2)}, u32[]{:S(2)}) collective-permute-start(bf16[32,1664]{1,0:T(8,128)(2,1)} %get-tuple-element.425), channel_id=1, source_target_pairs={{0,12},{1,13},{2,14},{3,15},{4,0},{5,1},{6,2},{7,3},{8,4},{9,5},{1... | collective-permute-start | bytes 319496 | tf_op jit(solution)/shard_map/ppermute | solution.py:560
  531.7 31.6 %collective-permute-start.90 = (bf16[256,1024]{1,0:T(8,128)(2,1)}, bf16[256,1024]{1,0:T(8,128)(2,1)}, u32[]{:S(2)}, u32[]{:S(2)}) collective-permute-start(bf16[256,1024]{1,0:T(8,128)(2,1)} %slice.573), channel_id=1, source_target_pairs={{0,2},{1,3},{2,0},{3,1},{4,6},{5,7},{6,4},{7,5},{8,10},{9,11},{10,... | collective-permute-start | bytes 1572872 | tf_op jit(solution)/shard_map/ppermute | solution.py:549
  548.6 23.4 %collective-permute-start.88 = (bf16[512,1664]{1,0:T(8,128)(2,1)}, bf16[512,1664]{1,0:T(8,128)(2,1)}, u32[]{:S(2)}, u32[]{:S(2)}) collective-permute-start(bf16[512,1664]{1,0:T(8,128)(2,1)} %convolution_convert_fusion.2), channel_id=1, source_target_pairs={{0,16},{16,0},{1,17},{17,1},{2,18},{18,2},{3,19},{19,3},{4,20},{20... | collective-permute-start | bytes 5111816 | tf_op jit(solution)/shard_map/ppermute | solution.py:363
  557.4 70.7 %reduce-scatter.11.cloned.1.call-start = ((), (), s32[]{:S(2)}) async-start(), calls=%async_computation.7 | async-start | bytes 1638400 | tf_op jit(solution)/shard_map/reduce_scatter | solution.py:565
  607.6 20.5 %collective-permute-start.96 = (bf16[32,1664]{1,0:T(8,128)(2,1)S(1)}, bf16[32,1664]{1,0:T(8,128)(2,1)S(1)}, u32[]{:S(2)}, u32[]{:S(2)}) collective-permute-start(bf16[32,1664]{1,0:T(8,128)(2,1)S(1)} %get-tuple-element.423), channel_id=1, source_target_pairs={{0,8},{1,9},{2,10},{3,11},{4,12},{5,13},{6,14},{7,15},{8,0},{9,1},... | collective-permute-start | bytes 319496 | tf_op jit(solution)/shard_map/ppermute | solution.py:560
  (244 other events, 2117.0 us)
Sparse Core Ops, SparseCore 0:
  460.7 24.1 reduce-scatter.4
  500.3 36.2 reduce-scatter.6
  557.5 20.4 reduce-scatter.8
  587.1 39.4 reduce-scatter.10
